TPU v7x, 32 devices: a whole 2x2x4 slice. The times are simulated.
32 devices in a mesh: segment: 4 (over y, core), slab: 8 (over z, x).
Axes of the slice: x: 2, y: 2, z: 4, core: 2. Of those that a mesh axis runs over, the one named last changes fastest.
Arguments:
- video_in: bfloat16 [8, 16, 64, 384], P(None, 'slab'), may hold values from -6 to 6
- cache_in: bfloat16 [4, 2, 16, 64, 384], P('segment', None, 'slab'), may hold values from -0.25 to 2
- conv_weight: bfloat16 [4, 3, 3, 3, 384, 384], P('segment'), may hold values from -0.0625 to 0.0625
- conv_bias: float32 [4, 384], P('segment'), may hold values from -1.5 to 1.5
- norm_gain: float32 [4, 384], P('segment'), may hold values from 0.5 to 2
Outputs:
- video_out: bfloat16 [8, 16, 64, 384], P('segment', 'slab')
- cache_out: bfloat16 [4, 2, 16, 64, 384], P('segment', None, 'slab')
All inputs are finite; a program needn't handle non-finite values.
Results may differ from a plain program's by a relative error of at most 0.0067.
Values may be sent and summed in bfloat16 or wider, within the bound.
No kernel may reach another device: no remote copies, remote signals or barrier semaphores. Data moves between devices by JAX's collectives and lax.ppermute only.
A program may use at most 64 MiB of HBM per device.

v0:
```python
import functools
import jax
import jax.numpy as jnp
from jax import lax
from jax.experimental import pallas as pl
from jax.experimental.pallas import tpu as pltpu
from jax.sharding import PartitionSpec as P

LAG = 2
CHUNK = 128
VMEM_BYTES = 24 * 2**20
F32 = jnp.float32
BF16 = jnp.bfloat16
ANY = pl.BlockSpec(memory_space=pl.ANY)
VMEM = pl.BlockSpec(memory_space=pltpu.VMEM)
SMEM = pl.BlockSpec(memory_space=pltpu.SMEM)


def turn_kernel(w_ref, bias_ref, gain_ref, out_ref, bias_out, gain_out, ws, sems):
    channels = w_ref.shape[-1]
    copies = [pltpu.make_async_copy(w_ref.at[k // 3, k % 3], ws.at[k], sems.at[k]) for k in range(9)]
    for copy in copies:
        copy.start()
    for row, out in ((bias_ref, bias_out), (gain_ref, gain_out)):
        out[...] = jnp.transpose(jnp.broadcast_to(row[...], (8, channels)), (1, 0))[:, :1]
    for k, copy in enumerate(copies):
        copy.wait()
        for c in range(3):
            out_ref[k % 3, :, pl.ds((k // 3 * 3 + c) * channels, channels)] = jnp.transpose(ws[k, c], (1, 0))


def turned_weights(weight, bias, gain):
    channels = weight.shape[-1]
    return pl.pallas_call(
        turn_kernel,
        out_shape=(
            jax.ShapeDtypeStruct((3, channels, 9 * channels), BF16),
            jax.ShapeDtypeStruct((channels, 1), F32),
            jax.ShapeDtypeStruct((channels, 1), F32),
        ),
        in_specs=[ANY, VMEM, VMEM],
        out_specs=(VMEM, VMEM, VMEM),
        scratch_shapes=[pltpu.VMEM((9, 3, channels, channels), BF16), pltpu.SemaphoreType.DMA((9,))],
        compiler_params=pltpu.CompilerParams(vmem_limit_bytes=VMEM_BYTES),
        cost_estimate=pl.CostEstimate(flops=0, bytes_accessed=4 * weight.size, transcendentals=0),
    )(weight, bias, gain)


def layer_kernel(cases, rows_in, own, cols, block, height, n_in, place_ref, w_ref, bias_ref, gain_ref, *refs):
    ins = refs[:n_in]
    out_ref, acts_ref, next_ref = refs[n_in:n_in + 3]
    xs, buf, total, sems = refs[n_in + 6:]
    channels = xs.shape[0]
    row = block * cols
    rows_out = rows_in - 2
    lanes_in, lanes_out = rows_in * row, rows_out * row
    segment, slab = place_ref[0], place_ref[1]
    next_ref[0], next_ref[1] = segment, slab

    def slot(a, c):
        return (3 * a + c) * channels

    def source(part):
        at, index = part[0], part[1]
        return ins[at] if index is None else ins[at].at[index]

    active = functools.reduce(jnp.logical_or, [segment == g for g, _, _ in cases])
    for g, x_parts, before in cases:
        @pl.when(segment == g)
        def _():
            copies = []
            for parts, target in ((x_parts, xs), (before, buf.at[pl.ds(slot(0, 1), channels)])):
                at = 0
                for part in parts:
                    src = source(part)
                    width = part[3] * row
                    copies.append(pltpu.make_async_copy(
                        src.at[:, pl.ds(part[2] * row, width)], target.at[:, pl.ds(at, width)],
                        sems.at[len(copies)]))
                    at += width
            for c in copies:
                c.start()
            for c in copies:
                c.wait()

    @pl.when(active)
    def _():
        def squares(i, acc):
            v = xs[pl.ds(pl.multiple_of(i * CHUNK, CHUNK), CHUNK), :].astype(F32)
            v = v * v
            for k in range(0, CHUNK, 8):
                acc = acc + v[k:k + 8]
            return acc

        acc = lax.fori_loop(0, channels // CHUNK, squares, jnp.zeros((8, lanes_in), F32))
        scale = lax.rsqrt(jnp.sum(acc, axis=0, keepdims=True) * (1.0 / channels) + 1e-06)
        lane = lax.broadcasted_iota(jnp.int32, (CHUNK, row), 1)
        col = lax.rem(lane, cols)
        first, last = col == 0, col == cols - 1
        head = lane < row - cols
        zero = jnp.zeros((), BF16)

        def spread(i, _):
            at = pl.multiple_of(i * CHUNK, CHUNK)
            gain = gain_ref[pl.ds(at, CHUNK), :]
            here = [pl.ds(r * row, row) for r in range(rows_in)]
            values = [xs[pl.ds(at, CHUNK), h].astype(F32) for h in here]
            olds = [buf[pl.ds(slot(0, 1) + at, CHUNK), h] for h in here]
            results = []
            for r in range(rows_in):
                g = values[r] * scale[:, r * row:(r + 1) * row] * gain
                new = (0.5 * g * (1.0 + jnp.tanh(0.5 * g))).astype(BF16)
                mixed = pltpu.roll(jnp.where(head, new, olds[r]), cols, 1)
                for a, v in enumerate((olds[r], mixed, new)):
                    results.append((a, 0, r, jnp.where(first, zero, pltpu.roll(v, 1, 1))))
                    results.append((a, 2, r, jnp.where(last, zero, pltpu.roll(v, row - 1, 1))))
                    if a:
                        results.append((a, 1, r, v))
            for a, c, r, v in results:
                buf[pl.ds(slot(a, c) + at, CHUNK), here[r]] = v
            return 0

        lax.fori_loop(0, channels // CHUNK, spread, 0)
        acts_done = pltpu.make_async_copy(buf.at[pl.ds(slot(2, 1), channels)], acts_ref, sems.at[0])
        acts_done.start()
        step = 2 * row

        def taps(n, _):
            at = pl.multiple_of(n * step, step)
            part = None
            for b in range(3):
                tap = jnp.dot(w_ref[b], buf[:, pl.ds(at + b * row, step)], preferred_element_type=F32)
                part = tap if part is None else part + tap
            total[:, pl.ds(at, step)] = part
            return 0

        lax.fori_loop(0, lanes_out // step, taps, 0)
        top = slab * own - (rows_out - own) // 2

        def finish(i, _):
            at = pl.multiple_of(i * CHUNK, CHUNK)
            bias = bias_ref[pl.ds(at, CHUNK), :]
            sums = []
            for r in range(rows_out):
                value = xs[pl.ds(at, CHUNK), pl.ds((r + 1) * row, row)].astype(F32)
                value = value + (total[pl.ds(at, CHUNK), pl.ds(r * row, row)] + bias)
                inside = jnp.logical_and(top + r >= 0, top + r < height)
                sums.append(jnp.where(inside, value, 0.0).astype(BF16))
            for r in range(rows_out):
                xs[pl.ds(at, CHUNK), pl.ds(r * row, row)] = sums[r]
            return 0

        lax.fori_loop(0, channels // CHUNK, finish, 0)
        out_done = pltpu.make_async_copy(xs.at[:, pl.ds(0, lanes_out)], out_ref, sems.at[1])
        out_done.start()
        acts_done.wait()
        out_done.wait()


def layer_call(cases, rows_in, own, cols, block, height, fixed, ins):
    place, weight, bias, gain = fixed
    channels = weight.shape[1]
    row = block * cols
    return pl.pallas_call(
        functools.partial(layer_kernel, cases, rows_in, own, cols, block, height, len(ins)),
        out_shape=(
            jax.ShapeDtypeStruct((channels, (rows_in - 2) * row), BF16),
            jax.ShapeDtypeStruct((channels, rows_in * row), BF16),
            jax.ShapeDtypeStruct(place.shape, place.dtype),
            jax.ShapeDtypeStruct(weight.shape, weight.dtype),
            jax.ShapeDtypeStruct(bias.shape, bias.dtype),
            jax.ShapeDtypeStruct(gain.shape, gain.dtype),
        ),
        in_specs=[SMEM, VMEM, VMEM, VMEM] + [ANY] * len(ins),
        out_specs=(ANY, ANY, SMEM, VMEM, VMEM, VMEM),
        input_output_aliases={1: 3, 2: 4, 3: 5},
        scratch_shapes=[
            pltpu.VMEM((channels, rows_in * row), BF16),
            pltpu.VMEM((9 * channels, rows_in * row), BF16),
            pltpu.VMEM((channels, (rows_in - 2) * row), F32),
            pltpu.SemaphoreType.DMA((8,)),
        ],
        compiler_params=pltpu.CompilerParams(vmem_limit_bytes=VMEM_BYTES),
        cost_estimate=pl.CostEstimate(
            flops=2 * (rows_in - 2) * row * 27 * channels * channels, bytes_accessed=0, transcendentals=0),
    )(place, weight, bias, gain, *ins)


def local(segments, slabs, video_in, cache_in, conv_weight, conv_bias, norm_gain):
    frames, own, cols, channels = video_in.shape
    height = own * slabs
    segment = lax.axis_index("segment")
    slab = lax.axis_index("slab")
    axes = ("segment", "slab")
    block = frames // segments
    row = block * cols
    blocks = frames // block
    place = jnp.stack([segment, slab]).astype(jnp.int32)
    evens = range(0, segments, 2)
    odds = range(1, segments, 2)

    def moved(value, pairs, step):
        return lax.ppermute(value, axes, [
            (a * slabs + s, b * slabs + s + step) for a, b in pairs for s in range(slabs) if 0 <= s + step < slabs])

    def around(value, pairs, rows):
        above = moved(value[..., (own - rows) * row:], pairs, 1)
        below = moved(value[..., :rows * row], pairs, -1)
        return above, below

    def lanes(value):
        value = value.reshape(-1, block, own, cols, channels)
        return value.transpose(0, 4, 2, 1, 3).reshape(-1, channels, own * row)

    first = lanes(jnp.concatenate([cache_in[0], video_in[:block]], axis=0))
    first_above, first_below = around(first, [(g, g) for g in evens], 2)
    later, first_above, first_below = lax.optimization_barrier((lanes(video_in[block:]), first_above, first_below))
    fixed = (place,) + tuple(turned_weights(conv_weight[0], conv_bias, norm_gain))
    odd_above, odd_below = around(first[0], [(g, g) for g in odds], 1)
    later_above, later_below = around(later, [(0, 0)], 2)

    call = functools.partial(layer_call, own=own, cols=cols, block=block, height=height)
    across = [(g, g + 1) for g in evens]
    hop = [(g, g + 1) for g in odds if g + 1 < segments]
    planes = segments // 2
    arrived, done = [], []
    even_acts = odd_acts = None
    even_cache, odd_cache = [None] * planes, [None] * planes
    ticks = blocks + LAG * (planes - 1)
    for tick in range(ticks):
        busy = [p for p in range(planes) if 0 <= tick - LAG * p < blocks]
        ins = [first, first_above, first_below]
        old = [(1, 0, 0, 2), (0, 0, 0, own), (2, 0, 0, 2)]
        if tick:
            ins.append(even_acts)
            kept = [(3, None, 0, own + 4)]
        cases = []
        for p in busy:
            b = tick - LAG * p
            if p == 0 and b == 0:
                parts = [(1, 1, 0, 2), (0, 1, 0, own), (2, 1, 0, 2)]
            else:
                n = len(ins)
                if p == 0:
                    ins += [later, later_above, later_below]
                    parts = [(n + 1, b - 1, 0, 2), (n, b - 1, 0, own), (n + 2, b - 1, 0, 2)]
                else:
                    ins += list(arrived[b])
                    parts = [(n + 1, None, 0, 2), (n, None, 0, own), (n + 2, None, 0, 2)]
            cases.append((2 * p, parts, old if b == 0 else kept))
        if tick == 0:
            ins += [odd_above, odd_below]
        if tick == ticks - 1:
            ins.append(done[-2])
        out, even_acts, *fixed = call(cases, own + 4, fixed=fixed, ins=ins)
        if 0 < tick <= blocks:
            out, *arrived[tick - 1] = lax.optimization_barrier((out, *arrived[tick - 1]))
        crossed = moved(out, across, 0)

        ins = [crossed, first, odd_above, odd_below]
        old = [(2, None, 0, 1), (1, 0, 0, own), (3, None, 0, 1)]
        if tick:
            ins.append(odd_acts)
        if tick == 0:
            ins += [later_above, later_below]
        if tick >= ticks - 2:
            ins.append(done[0] if tick < ticks - 1 else done[-1])
        cases = [(2 * p + 1, [(0, None, 0, own + 2)], old if tick == LAG * p else [(4, None, 0, own + 2)]) for p in busy]
        out, odd_acts, *fixed = call(cases, own + 2, fixed=fixed, ins=ins)
        if tick < blocks:
            arrived.append((moved(out, hop, 0), moved(out[:, (own - 2) * row:], hop, 1), moved(out[:, :2 * row], hop, -1)))
        b = tick - LAG * (planes - 1)
        if 0 <= b < blocks:
            done.append(out if b == segments - 1 else moved(out, [(segments - 1, b)], 0))
        for p in busy:
            if tick - LAG * p == blocks - 1:
                even_cache[p] = even_acts[:, 2 * row:(2 + own) * row]
                odd_cache[p] = odd_acts[:, row:(1 + own) * row]

    def natural(value):
        return value.reshape(channels, own, block, cols).transpose(2, 1, 3, 0)

    result = done[-1]
    for b in range(blocks - 1):
        result = jnp.where(segment == b, done[b], result)
    cache = odd_cache[-1]
    for p in range(planes):
        cache = jnp.where(segment == 2 * p, even_cache[p], cache)
        cache = jnp.where(segment == 2 * p + 1, odd_cache[p], cache)
    return natural(result), natural(cache)[None]


def solution(mesh):
    segments, slabs = mesh.shape["segment"], mesh.shape["slab"]
    return jax.shard_map(
        functools.partial(local, segments, slabs),
        mesh=mesh,
        in_specs=(
            P(None, "slab", None, None),
            P("segment", None, "slab", None, None),
            P("segment", None, None, None, None, None),
            P("segment", None),
            P("segment", None),
        ),
        out_specs=(P("segment", "slab", None, None), P("segment", None, "slab", None, None)),
        check_vma=False,
    )
```

profile of v0, /device:TPU:13, one launch (start us, length us, event | category | flops | bytes accessed | tf_op | source)
XLA Modules:
  0.0 149.1 jit_solution(12377991570041955919)
XLA Ops:
  4.4 3.1 %collective-permute-start.2 = (bf16[384,128]{1,0:T(8,128)(2,1)S(1)}, bf16[384,128]{1,0:T(8,128)(2,1)S(1)}, u32[]{:S(2)}, u32[]{:S(2)}) collective-permute-start(bf16[384,128]{1,0:T(8,128)(2,1)S(1)} %copy.100), channel_id=1, source_target_pairs={{8,9},{9,10},{10,11},{11,12},{12,13},{13,14},{14,15},{24,25},{25,2... | collective-permute-start | bytes 294920 | tf_op jit(solution)/shard_map/ppermute | solution.py:203
  7.7 3.1 %collective-permute-start.3 = (bf16[384,128]{1,0:T(8,128)(2,1)S(1)}, bf16[384,128]{1,0:T(8,128)(2,1)S(1)}, u32[]{:S(2)}, u32[]{:S(2)}) collective-permute-start(bf16[384,128]{1,0:T(8,128)(2,1)S(1)} %copy.101), channel_id=1, source_target_pairs={{9,8},{10,9},{11,10},{12,11},{13,12},{14,13},{15,14},{25,24},{26,2... | collective-permute-start | bytes 294920 | tf_op jit(solution)/shard_map/ppermute | solution.py:203
  12.0 3.3 %copy-done.4 = bf16[1,3,3,3,384,384]{5,4,3,2,1,0:T(8,128)(2,1)S(1)} copy-done((bf16[1,3,3,3,384,384]{5,4,3,2,1,0:T(8,128)(2,1)S(1)}, bf16[1,3,3,3,384,384]{5,4,3,2,1,0:T(8,128)(2,1)}, u32[]{:S(2)}) %copy-start.4) | copy-done | bytes 7962648
  16.6 4.5 %shard_map.68 = (bf16[3,384,3456]{2,1,0:T(8,128)(2,1)S(1)}, f32[384,1]{1,0:T(8,128)S(1)}, f32[384,1]{1,0:T(8,128)S(1)}) custom-call(bf16[3,3,3,384,384]{4,3,2,1,0:T(8,128)(2,1)S(1)} %bitcast.21, f32[1,384]{1,0:T(1,128)S(1)} %copy-done.6, f32[1,384]{1,0:T(1,128)S(1)} %copy-done.7), custom_call_target="tpu_custom_call" | custom-call | bytes 15925248 | tf_op jit(solution)/shard_map/pallas_call | solution.py:34
  21.1 3.1 %copy-done = bf16[3,384,3456]{2,1,0:T(8,128)(2,1)} copy-done((bf16[3,384,3456]{2,1,0:T(8,128)(2,1)}, bf16[3,384,3456]{2,1,0:T(8,128)(2,1)S(1)}, u32[]{:S(2)}) %copy-start) | copy-done | bytes 7962648
  26.0 3.3 %copy-done.1 = bf16[3,384,3456]{2,1,0:T(8,128)(2,1)S(1)} copy-done((bf16[3,384,3456]{2,1,0:T(8,128)(2,1)S(1)}, bf16[3,384,3456]{2,1,0:T(8,128)(2,1)}, u32[]{:S(2)}) %copy-start.1) | copy-done | bytes 7962648
  30.4 1.3 collective-permute-start.4
  31.7 2.4 %collective-permute-done.4.refs_0_ = bf16[384,512]{1,0:T(8,128)(2,1)S(1)} collective-permute-done((bf16[384,512]{1,0:T(8,128)(2,1)S(1)}, bf16[384,512]{1,0:T(8,128)(2,1)S(1)}, u32[]{:S(2)}, u32[]{:S(2)}) %collective-permute-start.4) | collective-permute-done | bytes 393248 | tf_op jit(solution)/shard_map/ppermute | solution.py:203
  38.7 1.3 collective-permute-start.10
  40.0 24.5 %collective-permute-done.10.refs_0_ = bf16[384,512]{1,0:T(8,128)(2,1)S(1)} collective-permute-done((bf16[384,512]{1,0:T(8,128)(2,1)S(1)}, bf16[384,512]{1,0:T(8,128)(2,1)S(1)}, u32[]{:S(2)}, u32[]{:S(2)}) %collective-permute-start.10) | collective-permute-done | bytes 393248 | tf_op jit(solution)/shard_map/ppermute | solution.py:203
  64.5 1.4 shard_map.72
  69.2 1.3 collective-permute-start.14
  70.5 11.7 %collective-permute-done.14.refs_0_ = bf16[384,512]{1,0:T(8,128)(2,1)S(1)} collective-permute-done((bf16[384,512]{1,0:T(8,128)(2,1)S(1)}, bf16[384,512]{1,0:T(8,128)(2,1)S(1)}, u32[]{:S(2)}, u32[]{:S(2)}) %collective-permute-start.14) | collective-permute-done | bytes 393248 | tf_op jit(solution)/shard_map/ppermute | solution.py:203
  82.2 5.7 %shard_map.74 = (bf16[384,256]{1,0:T(8,128)(2,1)S(1)}, bf16[384,512]{1,0:T(8,128)(2,1)S(1)}, s32[2]{0:T(128)S(1)}, bf16[3,384,3456]{2,1,0:T(8,128)(2,1)S(1)}, f3...) custom-call(s32[2]{0:T(128)S(1)} %get-tuple-element.124.place_ref, ...), custom_call_target="tpu_custom_call", output_to_operand_aliasing={{3}: (1, {}), {4}: (2, {}), {5}: (3, {})} | custom-call | flops 2038431744 | tf_op jit(solution)/shard_map/pallas_call | solution.py:164
  92.5 7.2 %collective-permute-done.18.refs_0_ = bf16[384,512]{1,0:T(8,128)(2,1)S(1)} collective-permute-done((bf16[384,512]{1,0:T(8,128)(2,1)S(1)}, bf16[384,512]{1,0:T(8,128)(2,1)S(1)}, u32[]{:S(2)}, u32[]{:S(2)}) %collective-permute-start.18) | collective-permute-done | bytes 393248 | tf_op jit(solution)/shard_map/ppermute | solution.py:203
  99.8 6.0 %shard_map.76 = (bf16[384,256]{1,0:T(8,128)(2,1)S(1)}, bf16[384,512]{1,0:T(8,128)(2,1)S(1)}, s32[2]{0:T(128)S(1)}, bf16[3,384,3456]{2,1,0:T(8,128)(2,1)S(1)}, f3...) custom-call(s32[2]{0:T(128)S(1)} %get-tuple-element.140.place_ref, ...), custom_call_target="tpu_custom_call", output_to_operand_aliasing={{3}: (1, {}), {4}: (2, {}), {5}: (3, {})} | custom-call | flops 2038431744 | tf_op jit(solution)/shard_map/pallas_call | solution.py:164
  109.1 1.4 collective-permute-start.22
  110.6 7.6 %collective-permute-start.23 = (bf16[384,256]{1,0:T(8,128)(2,1)S(1)}, bf16[384,256]{1,0:T(8,128)(2,1)S(1)}, u32[]{:S(2)}, u32[]{:S(2)}) collective-permute-start(bf16[384,256]{1,0:T(8,128)(2,1)S(1)} %get-tuple-element.145), channel_id=1, source_target_pairs={{24,0},{25,1},{26,2},{27,3},{28,4},{29,5},{30,6},{31,7}} | collective-permute-start | bytes 589832 | tf_op jit(solution)/shard_map/ppermute | solution.py:203
  118.2 1.3 collective-permute-start.25
  120.8 5.8 %shard_map.78 = (bf16[384,256]{1,0:T(8,128)(2,1)S(1)}, bf16[384,512]{1,0:T(8,128)(2,1)S(1)}, s32[2]{0:T(128)S(1)}, bf16[3,384,3456]{2,1,0:T(8,128)(2,1)S(1)}, f3...) custom-call(s32[2]{0:T(128)S(1)} %get-tuple-element.156.place_ref, ...), custom_call_target="tpu_custom_call", output_to_operand_aliasing={{3}: (1, {}), {4}: (2, {}), {5}: (3, {})} | custom-call | flops 2038431744 | tf_op jit(solution)/shard_map/pallas_call | solution.py:164
  127.8 3.1 %copy-done.2 = bf16[3,384,3456]{2,1,0:T(8,128)(2,1)} copy-done((bf16[3,384,3456]{2,1,0:T(8,128)(2,1)}, bf16[3,384,3456]{2,1,0:T(8,128)(2,1)S(1)}, u32[]{:S(2)}) %copy-start.2) | copy-done | bytes 7962648
  133.2 3.1 %collective-permute-start.24 = (bf16[384,256]{1,0:T(8,128)(2,1)S(1)}, bf16[384,256]{1,0:T(8,128)(2,1)S(1)}, u32[]{:S(2)}, u32[]{:S(2)}) collective-permute-start(bf16[384,256]{1,0:T(8,128)(2,1)S(1)} %get-tuple-element.164), channel_id=1, source_target_pairs={{24,16},{25,17},{26,18},{27,19},{28,20},{29,21},{30,22},{31,23}} | collective-permute-start | bytes 589832 | tf_op jit(solution)/shard_map/ppermute | solution.py:203
  137.3 3.3 %copy-done.3 = bf16[3,384,3456]{2,1,0:T(8,128)(2,1)S(1)} copy-done((bf16[3,384,3456]{2,1,0:T(8,128)(2,1)S(1)}, bf16[3,384,3456]{2,1,0:T(8,128)(2,1)}, u32[]{:S(2)}) %copy-start.3) | copy-done | bytes 7962648
  140.5 5.7 %shard_map.80 = (bf16[384,256]{1,0:T(8,128)(2,1)S(1)}, bf16[384,512]{1,0:T(8,128)(2,1)S(1)}, s32[2]{0:T(128)}, bf16[3,384,3456]{2,1,0:T(8,128)(2,1)S(1)}, f32[384,1]{1,0:T(8,128)S(1)}, /*index=5*/f32[384,1]{1,0:T(8,128)S(1)}) custom-call(s32[2]{0:T(128)S(1)} %get-tuple-element.173.place_ref, ...), custom_call_target="tpu_custom_call", output_to_operand_aliasing={{3}: (1, {}), {4}: (2, {}), {5}: (3, {})} | custom-call | flops 2038431744 | tf_op jit(solution)/shard_map/pallas_call | solution.py:164
  (81 shorter events, 33.4 us)
Async XLA Ops:
  2.8 21.5 %collective-permute-start = (bf16[2,384,256]{2,1,0:T(8,128)(2,1)S(1)}, bf16[2,384,256]{2,1,0:T(8,128)(2,1)S(1)}, u32[]{:S(2)}, u32[]{:S(2)}) collective-permute-start(bf16[2,384,256]{2,1,0:T(8,128)(2,1)S(1)} %copy.79.refs_0_.refs_1_), channel_id=1, source_target_pairs={{0,1},{1,2},{2,3},{3,4},{4,5},{5,6},{6,7},{16,17},{17,18},{18,19},... | collective-permute-start | bytes 1179656 | tf_op jit(solution)/shard_map/ppermute | solution.py:203
  3.5 20.8 %collective-permute-start.1 = (bf16[2,384,256]{2,1,0:T(8,128)(2,1)S(1)}, bf16[2,384,256]{2,1,0:T(8,128)(2,1)S(1)}, u32[]{:S(2)}, u32[]{:S(2)}) collective-permute-start(bf16[2,384,256]{2,1,0:T(8,128)(2,1)S(1)} %copy.79.refs_0_.refs_1_), channel_id=1, source_target_pairs={{1,0},{2,1},{3,2},{4,3},{5,4},{6,5},{7,6},{17,16},{18,17},{19,18},... | collective-permute-start | bytes 1179656 | tf_op jit(solution)/shard_map/ppermute | solution.py:203
  4.4 21.5 %collective-permute-start.2 = (bf16[384,128]{1,0:T(8,128)(2,1)S(1)}, bf16[384,128]{1,0:T(8,128)(2,1)S(1)}, u32[]{:S(2)}, u32[]{:S(2)}) collective-permute-start(bf16[384,128]{1,0:T(8,128)(2,1)S(1)} %copy.100), channel_id=1, source_target_pairs={{8,9},{9,10},{10,11},{11,12},{12,13},{13,14},{14,15},{24,25},{25,2... | collective-permute-start | bytes 294920 | tf_op jit(solution)/shard_map/ppermute | solution.py:203
  7.7 18.3 %collective-permute-start.3 = (bf16[384,128]{1,0:T(8,128)(2,1)S(1)}, bf16[384,128]{1,0:T(8,128)(2,1)S(1)}, u32[]{:S(2)}, u32[]{:S(2)}) collective-permute-start(bf16[384,128]{1,0:T(8,128)(2,1)S(1)} %copy.101), channel_id=1, source_target_pairs={{9,8},{10,9},{11,10},{12,11},{13,12},{14,13},{15,14},{25,24},{26,2... | collective-permute-start | bytes 294920 | tf_op jit(solution)/shard_map/ppermute | solution.py:203
  24.5 9.6 %collective-permute-start.5 = (bf16[3,384,256]{2,1,0:T(8,128)(2,1)S(1)}, bf16[3,384,256]{2,1,0:T(8,128)(2,1)S(1)}, u32[]{:S(2)}, u32[]{:S(2)}) collective-permute-start(bf16[3,384,256]{2,1,0:T(8,128)(2,1)S(1)} %copy.80.refs_4_), channel_id=1, source_target_pairs={{0,1},{1,2},{2,3},{3,4},{4,5},{5,6},{6,7}} | collective-permute-start | bytes 1769480 | tf_op jit(solution)/shard_map/ppermute | solution.py:203
  25.2 8.9 %collective-permute-start.6 = (bf16[3,384,256]{2,1,0:T(8,128)(2,1)S(1)}, bf16[3,384,256]{2,1,0:T(8,128)(2,1)S(1)}, u32[]{:S(2)}, u32[]{:S(2)}) collective-permute-start(bf16[3,384,256]{2,1,0:T(8,128)(2,1)S(1)} %copy.80.refs_4_), channel_id=1, source_target_pairs={{1,0},{2,1},{3,2},{4,3},{5,4},{6,5},{7,6}} | collective-permute-start | bytes 1769480 | tf_op jit(solution)/shard_map/ppermute | solution.py:203
  30.4 3.7 %collective-permute-start.4 = (bf16[384,512]{1,0:T(8,128)(2,1)S(1)}, bf16[384,512]{1,0:T(8,128)(2,1)S(1)}, u32[]{:S(2)}, u32[]{:S(2)}) collective-permute-start(bf16[384,512]{1,0:T(8,128)(2,1)S(1)} %get-tuple-element.101), channel_id=1, source_target_pairs={{0,8},{1,9},{2,10},{3,11},{4,12},{5,13},{6,14},{7,15},{16,24},{17,... | collective-permute-start | bytes 1179656 | tf_op jit(solution)/shard_map/ppermute | solution.py:203
  35.4 3.3 %collective-permute-start.7 = (bf16[384,256]{1,0:T(8,128)(2,1)S(1)}, bf16[384,256]{1,0:T(8,128)(2,1)S(1)}, u32[]{:S(2)}, u32[]{:S(2)}) collective-permute-start(bf16[384,256]{1,0:T(8,128)(2,1)S(1)} %get-tuple-element.113), channel_id=1, source_target_pairs={{8,16},{9,17},{10,18},{11,19},{12,20},{13,21},{14,22},{15,23}} | collective-permute-start | bytes 589832 | tf_op jit(solution)/shard_map/ppermute | solution.py:203
  36.0 2.6 %collective-permute-start.8 = (bf16[384,256]{1,0:T(8,128)(2,1)S(1)}, bf16[384,256]{1,0:T(8,128)(2,1)S(1)}, u32[]{:S(2)}, u32[]{:S(2)}) collective-permute-start(bf16[384,256]{1,0:T(8,128)(2,1)S(1)} %get-tuple-element.113), channel_id=1, source_target_pairs={{8,17},{9,18},{10,19},{11,20},{12,21},{13,22},{14,23}} | collective-permute-start | bytes 589832 | tf_op jit(solution)/shard_map/ppermute | solution.py:203
  38.7 25.8 %collective-permute-start.10 = (bf16[384,512]{1,0:T(8,128)(2,1)S(1)}, bf16[384,512]{1,0:T(8,128)(2,1)S(1)}, u32[]{:S(2)}, u32[]{:S(2)}) collective-permute-start(bf16[384,512]{1,0:T(8,128)(2,1)S(1)} %get-tuple-element.114), channel_id=1, source_target_pairs={{0,8},{1,9},{2,10},{3,11},{4,12},{5,13},{6,14},{7,15},{16,24},{17,... | collective-permute-start | bytes 1179656 | tf_op jit(solution)/shard_map/ppermute | solution.py:203
  65.9 3.3 %collective-permute-start.11 = (bf16[384,256]{1,0:T(8,128)(2,1)S(1)}, bf16[384,256]{1,0:T(8,128)(2,1)S(1)}, u32[]{:S(2)}, u32[]{:S(2)}) collective-permute-start(bf16[384,256]{1,0:T(8,128)(2,1)S(1)} %get-tuple-element.129), channel_id=1, source_target_pairs={{8,16},{9,17},{10,18},{11,19},{12,20},{13,21},{14,22},{15,23}} | collective-permute-start | bytes 589832 | tf_op jit(solution)/shard_map/ppermute | solution.py:203
  66.6 2.6 %collective-permute-start.12 = (bf16[384,256]{1,0:T(8,128)(2,1)S(1)}, bf16[384,256]{1,0:T(8,128)(2,1)S(1)}, u32[]{:S(2)}, u32[]{:S(2)}) collective-permute-start(bf16[384,256]{1,0:T(8,128)(2,1)S(1)} %get-tuple-element.129), channel_id=1, source_target_pairs={{8,17},{9,18},{10,19},{11,20},{12,21},{13,22},{14,23}} | collective-permute-start | bytes 589832 | tf_op jit(solution)/shard_map/ppermute | solution.py:203
  69.2 13.0 %collective-permute-start.14 = (bf16[384,512]{1,0:T(8,128)(2,1)S(1)}, bf16[384,512]{1,0:T(8,128)(2,1)S(1)}, u32[]{:S(2)}, u32[]{:S(2)}) collective-permute-start(bf16[384,512]{1,0:T(8,128)(2,1)S(1)} %get-tuple-element.130), channel_id=1, source_target_pairs={{0,8},{1,9},{2,10},{3,11},{4,12},{5,13},{6,14},{7,15},{16,24},{17,... | collective-permute-start | bytes 1179656 | tf_op jit(solution)/shard_map/ppermute | solution.py:203
  87.9 3.3 %collective-permute-start.15 = (bf16[384,256]{1,0:T(8,128)(2,1)S(1)}, bf16[384,256]{1,0:T(8,128)(2,1)S(1)}, u32[]{:S(2)}, u32[]{:S(2)}) collective-permute-start(bf16[384,256]{1,0:T(8,128)(2,1)S(1)} %get-tuple-element.145), channel_id=1, source_target_pairs={{8,16},{9,17},{10,18},{11,19},{12,20},{13,21},{14,22},{15,23}} | collective-permute-start | bytes 589832 | tf_op jit(solution)/shard_map/ppermute | solution.py:203
  88.6 2.6 %collective-permute-start.16 = (bf16[384,256]{1,0:T(8,128)(2,1)S(1)}, bf16[384,256]{1,0:T(8,128)(2,1)S(1)}, u32[]{:S(2)}, u32[]{:S(2)}) collective-permute-start(bf16[384,256]{1,0:T(8,128)(2,1)S(1)} %get-tuple-element.145), channel_id=1, source_target_pairs={{8,17},{9,18},{10,19},{11,20},{12,21},{13,22},{14,23}} | collective-permute-start | bytes 589832 | tf_op jit(solution)/shard_map/ppermute | solution.py:203
  91.2 8.5 %collective-permute-start.18 = (bf16[384,512]{1,0:T(8,128)(2,1)S(1)}, bf16[384,512]{1,0:T(8,128)(2,1)S(1)}, u32[]{:S(2)}, u32[]{:S(2)}) collective-permute-start(bf16[384,512]{1,0:T(8,128)(2,1)S(1)} %get-tuple-element.146), channel_id=1, source_target_pairs={{0,8},{1,9},{2,10},{3,11},{4,12},{5,13},{6,14},{7,15},{16,24},{17,... | collective-permute-start | bytes 1179656 | tf_op jit(solution)/shard_map/ppermute | solution.py:203
  105.8 3.3 %collective-permute-start.19 = (bf16[384,256]{1,0:T(8,128)(2,1)S(1)}, bf16[384,256]{1,0:T(8,128)(2,1)S(1)}, u32[]{:S(2)}, u32[]{:S(2)}) collective-permute-start(bf16[384,256]{1,0:T(8,128)(2,1)S(1)} %get-tuple-element.161), channel_id=1, source_target_pairs={{8,16},{9,17},{10,18},{11,19},{12,20},{13,21},{14,22},{15,23}} | collective-permute-start | bytes 589832 | tf_op jit(solution)/shard_map/ppermute | solution.py:203
  106.5 2.6 %collective-permute-start.20 = (bf16[384,256]{1,0:T(8,128)(2,1)S(1)}, bf16[384,256]{1,0:T(8,128)(2,1)S(1)}, u32[]{:S(2)}, u32[]{:S(2)}) collective-permute-start(bf16[384,256]{1,0:T(8,128)(2,1)S(1)} %get-tuple-element.161), channel_id=1, source_target_pairs={{8,17},{9,18},{10,19},{11,20},{12,21},{13,22},{14,23}} | collective-permute-start | bytes 589832 | tf_op jit(solution)/shard_map/ppermute | solution.py:203
  107.2 2.0 %collective-permute-start.21 = (bf16[384,256]{1,0:T(8,128)(2,1)S(1)}, bf16[384,256]{1,0:T(8,128)(2,1)S(1)}, u32[]{:S(2)}, u32[]{:S(2)}) collective-permute-start(bf16[384,256]{1,0:T(8,128)(2,1)S(1)} %get-tuple-element.161), channel_id=1, source_target_pairs={{9,16},{10,17},{11,18},{12,19},{13,20},{14,21},{15,22}} | collective-permute-start | bytes 589832 | tf_op jit(solution)/shard_map/ppermute | solution.py:203
  109.1 11.6 %collective-permute-start.22 = (bf16[384,512]{1,0:T(8,128)(2,1)S(1)}, bf16[384,512]{1,0:T(8,128)(2,1)S(1)}, u32[]{:S(2)}, u32[]{:S(2)}) collective-permute-start(bf16[384,512]{1,0:T(8,128)(2,1)S(1)} %get-tuple-element.162), channel_id=1, source_target_pairs={{0,8},{1,9},{2,10},{3,11},{4,12},{5,13},{6,14},{7,15},{16,24},{17,... | collective-permute-start | bytes 1179656 | tf_op jit(solution)/shard_map/ppermute | solution.py:203
  110.6 10.2 %collective-permute-start.23 = (bf16[384,256]{1,0:T(8,128)(2,1)S(1)}, bf16[384,256]{1,0:T(8,128)(2,1)S(1)}, u32[]{:S(2)}, u32[]{:S(2)}) collective-permute-start(bf16[384,256]{1,0:T(8,128)(2,1)S(1)} %get-tuple-element.145), channel_id=1, source_target_pairs={{24,0},{25,1},{26,2},{27,3},{28,4},{29,5},{30,6},{31,7}} | collective-permute-start | bytes 589832 | tf_op jit(solution)/shard_map/ppermute | solution.py:203
  118.2 8.4 %collective-permute-start.25 = (bf16[384,256]{1,0:T(8,128)(2,1)S(1)}, bf16[384,256]{1,0:T(8,128)(2,1)S(1)}, u32[]{:S(2)}, u32[]{:S(2)}) collective-permute-start(bf16[384,256]{1,0:T(8,128)(2,1)S(1)} %get-tuple-element.161), channel_id=1, source_target_pairs={{24,8},{25,9},{26,10},{27,11},{28,12},{29,13},{30,14},{31,15}} | collective-permute-start | bytes 589832 | tf_op jit(solution)/shard_map/ppermute | solution.py:203
  131.9 5.4 %collective-permute-start.26 = (bf16[384,512]{1,0:T(8,128)(2,1)}, bf16[384,512]{1,0:T(8,128)(2,1)S(1)}, u32[]{:S(2)}, u32[]{:S(2)}) collective-permute-start(bf16[384,512]{1,0:T(8,128)(2,1)} %get-tuple-element.177), channel_id=1, source_target_pairs={{0,8},{1,9},{2,10},{3,11},{4,12},{5,13},{6,14},{7,15},{16,24},{17,... | collective-permute-start | bytes 1179656 | tf_op jit(solution)/shard_map/ppermute | solution.py:203
  133.2 4.1 %collective-permute-start.24 = (bf16[384,256]{1,0:T(8,128)(2,1)S(1)}, bf16[384,256]{1,0:T(8,128)(2,1)S(1)}, u32[]{:S(2)}, u32[]{:S(2)}) collective-permute-start(bf16[384,256]{1,0:T(8,128)(2,1)S(1)} %get-tuple-element.164), channel_id=1, source_target_pairs={{24,16},{25,17},{26,18},{27,19},{28,20},{29,21},{30,22},{31,23}} | collective-permute-start | bytes 589832 | tf_op jit(solution)/shard_map/ppermute | solution.py:203
  (13 other events, 125.2 us)
where the time goes:
time: 150 us; the launch traced here: 149 us
  waiting for transfers between devices  48.2 us (32%)
  Pallas kernels  37.7 us (25%)
  starting transfers between devices  36.9 us (25%)
  local copies, waits for them, and re-layouts  22.9 us (15%)
  other arithmetic  2.09 us (1%)
    ppermute x27, waiting for transfers between devices, moved(): lax.ppermute(value, axes, [(a * slabs + s, b * slabs + s + step) for a, b...  48.2 us
    ppermute x27, starting transfers between devices, moved(): lax.ppermute(value, axes, [(a * slabs + s, b * slabs + s + step) for a, b...  36.9 us
    pallas_call x12, Pallas kernels, layer_call(): pl.pallas_call(functools.partial(layer_kernel, cases, rows_in, own, cols,...  33.2 us
    unnamed x24, local copies, waits for them, and re-layouts  19.9 us
    pallas_call x1, Pallas kernels, turned_weights(): pl.pallas_call(turn_kernel, out_shape=(jax.ShapeDtypeStruct((3, channels,...  4.48 us
  transfers between devices with their start and end apart: 27, of which 6 were waited for; matrix products, arithmetic and copies ran while one was open for 1% of the time, Pallas kernels for 11%

commit v1 on v0

--- a/solution.py
+++ b/solution.py
@@ -16,20 +16,25 @@
 SMEM = pl.BlockSpec(memory_space=pltpu.SMEM)
 
 
-def turn_kernel(w_ref, bias_ref, gain_ref, out_ref, bias_out, gain_out, ws, sems):
+def turn_kernel(w_ref, bias_ref, gain_ref, _, out_ref, bias_out, gain_out, ws, rows, sems):
     channels = w_ref.shape[-1]
     copies = [pltpu.make_async_copy(w_ref.at[k // 3, k % 3], ws.at[k], sems.at[k]) for k in range(9)]
-    for copy in copies:
+    vectors = [pltpu.make_async_copy(ref, rows.at[pl.ds(k, 1)], sems.at[9 + k])
+               for k, ref in enumerate((bias_ref, gain_ref))]
+    for copy in vectors + copies:
         copy.start()
-    for row, out in ((bias_ref, bias_out), (gain_ref, gain_out)):
-        out[...] = jnp.transpose(jnp.broadcast_to(row[...], (8, channels)), (1, 0))[:, :1]
     for k, copy in enumerate(copies):
         copy.wait()
         for c in range(3):
             out_ref[k % 3, :, pl.ds((k // 3 * 3 + c) * channels, channels)] = jnp.transpose(ws[k, c], (1, 0))
-
-
-def turned_weights(weight, bias, gain):
+    for copy in vectors:
+        copy.wait()
+    turned = jnp.transpose(rows[...], (1, 0))
+    bias_out[...] = turned[:, 0:1]
+    gain_out[...] = turned[:, 1:2]
+
+
+def turned_weights(weight, bias, gain, ahead):
     channels = weight.shape[-1]
     return pl.pallas_call(
         turn_kernel,
@@ -38,12 +43,16 @@
             jax.ShapeDtypeStruct((channels, 1), F32),
             jax.ShapeDtypeStruct((channels, 1), F32),
         ),
-        in_specs=[ANY, VMEM, VMEM],
+        in_specs=[pl.BlockSpec(memory_space=pltpu.HBM)] * 3 + [ANY],
         out_specs=(VMEM, VMEM, VMEM),
-        scratch_shapes=[pltpu.VMEM((9, 3, channels, channels), BF16), pltpu.SemaphoreType.DMA((9,))],
+        scratch_shapes=[
+            pltpu.VMEM((9, 3, channels, channels), BF16),
+            pltpu.VMEM((8, channels), F32),
+            pltpu.SemaphoreType.DMA((11,)),
+        ],
         compiler_params=pltpu.CompilerParams(vmem_limit_bytes=VMEM_BYTES),
         cost_estimate=pl.CostEstimate(flops=0, bytes_accessed=4 * weight.size, transcendentals=0),
-    )(weight, bias, gain)
+    )(*(pltpu.with_memory_space_constraint(v, pltpu.HBM) for v in (weight, bias, gain)), ahead)
 
 
 def layer_kernel(cases, rows_in, own, cols, block, height, n_in, place_ref, w_ref, bias_ref, gain_ref, *refs):
@@ -124,34 +133,20 @@
         acts_done = pltpu.make_async_copy(buf.at[pl.ds(slot(2, 1), channels)], acts_ref, sems.at[0])
         acts_done.start()
         step = 2 * row
+        top = slab * own - (rows_out - own) // 2
 
         def taps(n, _):
             at = pl.multiple_of(n * step, step)
-            part = None
+            part = xs[:, pl.ds(at + row, step)].astype(F32) + bias_ref[...]
             for b in range(3):
-                tap = jnp.dot(w_ref[b], buf[:, pl.ds(at + b * row, step)], preferred_element_type=F32)
-                part = tap if part is None else part + tap
-            total[:, pl.ds(at, step)] = part
+                part = part + jnp.dot(w_ref[b], buf[:, pl.ds(at + b * row, step)], preferred_element_type=F32)
+            line = top + 2 * n + lax.broadcasted_iota(jnp.int32, (1, step), 1) // row
+            total[:, pl.ds(at, step)] = jnp.where(
+                jnp.logical_and(line >= 0, line < height), part, 0.0).astype(BF16)
             return 0
 
         lax.fori_loop(0, lanes_out // step, taps, 0)
-        top = slab * own - (rows_out - own) // 2
-
-        def finish(i, _):
-            at = pl.multiple_of(i * CHUNK, CHUNK)
-            bias = bias_ref[pl.ds(at, CHUNK), :]
-            sums = []
-            for r in range(rows_out):
-                value = xs[pl.ds(at, CHUNK), pl.ds((r + 1) * row, row)].astype(F32)
-                value = value + (total[pl.ds(at, CHUNK), pl.ds(r * row, row)] + bias)
-                inside = jnp.logical_and(top + r >= 0, top + r < height)
-                sums.append(jnp.where(inside, value, 0.0).astype(BF16))
-            for r in range(rows_out):
-                xs[pl.ds(at, CHUNK), pl.ds(r * row, row)] = sums[r]
-            return 0
-
-        lax.fori_loop(0, channels // CHUNK, finish, 0)
-        out_done = pltpu.make_async_copy(xs.at[:, pl.ds(0, lanes_out)], out_ref, sems.at[1])
+        out_done = pltpu.make_async_copy(total, out_ref, sems.at[1])
         out_done.start()
         acts_done.wait()
         out_done.wait()
@@ -177,7 +172,7 @@
         scratch_shapes=[
             pltpu.VMEM((channels, rows_in * row), BF16),
             pltpu.VMEM((9 * channels, rows_in * row), BF16),
-            pltpu.VMEM((channels, (rows_in - 2) * row), F32),
+            pltpu.VMEM((channels, (rows_in - 2) * row), BF16),
             pltpu.SemaphoreType.DMA((8,)),
         ],
         compiler_params=pltpu.CompilerParams(vmem_limit_bytes=VMEM_BYTES),
@@ -214,13 +209,15 @@
 
     first = lanes(jnp.concatenate([cache_in[0], video_in[:block]], axis=0))
     first_above, first_below = around(first, [(g, g) for g in evens], 2)
-    later, first_above, first_below = lax.optimization_barrier((lanes(video_in[block:]), first_above, first_below))
-    fixed = (place,) + tuple(turned_weights(conv_weight[0], conv_bias, norm_gain))
     odd_above, odd_below = around(first[0], [(g, g) for g in odds], 1)
+    later, place, weight = lax.optimization_barrier((lanes(video_in[block:]), place, conv_weight[0]))
+    weight, bias, gain = turned_weights(weight, conv_bias, norm_gain, later)
+    later, weight = lax.optimization_barrier((later, weight))
     later_above, later_below = around(later, [(0, 0)], 2)
+    fixed = (place, weight, bias, gain)
 
     call = functools.partial(layer_call, own=own, cols=cols, block=block, height=height)
-    across = [(g, g + 1) for g in evens]
+    across = [(g, g ^ 1) for g in range(segments)]
     hop = [(g, g + 1) for g in odds if g + 1 < segments]
     planes = segments // 2
     arrived, done = [], []
@@ -280,7 +277,7 @@
     def natural(value):
         return value.reshape(channels, own, block, cols).transpose(2, 1, 3, 0)
 
-    result = done[-1]
+    result, segment = lax.optimization_barrier((done[-1], segment))
     for b in range(blocks - 1):
         result = jnp.where(segment == b, done[b], result)
     cache = odd_cache[-1]

time: 150 us -> 130 us (0.87)
  waiting for transfers between devices: 48.2 us -> 7.84 us
  starting transfers between devices: 36.9 us -> 69.9 us
  local copies, waits for them, and re-layouts: 22.9 us -> 11.3 us
    ppermute x27, waiting for transfers between devices: 48.2 us -> 7.84 us  [moved(): lax.ppermute(value, axes, [(a * slabs + s, b * slabs + s + step) for a, b...]
    ppermute x27, starting transfers between devices: 36.9 us -> 69.9 us  [moved(): lax.ppermute(value, axes, [(a * slabs + s, b * slabs + s + step) for a, b...]
    unnamed x24 -> x10, local copies, waits for them, and re-layouts: 19.9 us -> 8.01 us
  transfers between devices with their start and end apart: 27 -> 27, of which waited for: 6 -> 6; matrix products, arithmetic and copies ran while one was open for 1% -> 2% of each run, Pallas kernels for 11% -> 12%
where the time goes in v1:
time: 130 us; the launch traced here: 129 us
  starting transfers between devices  69.9 us (54%)
  Pallas kernels  37.2 us (29%)
  local copies, waits for them, and re-layouts  11.3 us (9%)
  waiting for transfers between devices  7.84 us (6%)
  other arithmetic  2.06 us (2%)
    ppermute x27, starting transfers between devices, moved(): lax.ppermute(value, axes, [(a * slabs + s, b * slabs + s + step) for a, b...  69.9 us
    pallas_call x12, Pallas kernels, layer_call(): pl.pallas_call(functools.partial(layer_kernel, cases, rows_in, own, cols,...  33.1 us
    unnamed x10, local copies, waits for them, and re-layouts  8.01 us
    ppermute x27, waiting for transfers between devices, moved(): lax.ppermute(value, axes, [(a * slabs + s, b * slabs + s + step) for a, b...  7.84 us
    pallas_call x1, Pallas kernels, turned_weights(): pl.pallas_call(turn_kernel, out_shape=(jax.ShapeDtypeStruct((3, channels,...  4.14 us
  transfers between devices with their start and end apart: 27, of which 6 were waited for; matrix products, arithmetic and copies ran while one was open for 2% of the time, Pallas kernels for 12%

profile of v1, /device:TPU:13, one launch (start us, length us, event | category | flops | bytes accessed | tf_op | source)
XLA Modules:
  0.0 129.5 jit_solution(10755948793990602403)
XLA Ops:
  4.4 3.1 %collective-permute-start.2 = (bf16[384,128]{1,0:T(8,128)(2,1)S(1)}, bf16[384,128]{1,0:T(8,128)(2,1)S(1)}, u32[]{:S(2)}, u32[]{:S(2)}) collective-permute-start(bf16[384,128]{1,0:T(8,128)(2,1)S(1)} %copy.102), channel_id=1, source_target_pairs={{8,9},{9,10},{10,11},{11,12},{12,13},{13,14},{14,15},{24,25},{25,2... | collective-permute-start | bytes 294920 | tf_op jit(solution)/shard_map/ppermute | solution.py:198
  7.7 3.1 %collective-permute-start.3 = (bf16[384,128]{1,0:T(8,128)(2,1)S(1)}, bf16[384,128]{1,0:T(8,128)(2,1)S(1)}, u32[]{:S(2)}, u32[]{:S(2)}) collective-permute-start(bf16[384,128]{1,0:T(8,128)(2,1)S(1)} %copy.103), channel_id=1, source_target_pairs={{9,8},{10,9},{11,10},{12,11},{13,12},{14,13},{15,14},{25,24},{26,2... | collective-permute-start | bytes 294920 | tf_op jit(solution)/shard_map/ppermute | solution.py:198
  12.3 4.1 %shard_map.68 = (bf16[3,384,3456]{2,1,0:T(8,128)(2,1)S(1)}, f32[384,1]{1,0:T(8,128)S(1)}, f32[384,1]{1,0:T(8,128)S(1)}) custom-call(bf16[3,3,3,384,384]{4,3,2,1,0:T(8,128)(2,1)} %bitcast.21, f32[1,384]{1,0:T(1,128)} %bias_ref.1, f32[1,384]{1,0:T(1,128)} %gain_ref.1, bf16[3,384,256]{2,1,0:T(8,128)(2,1)S(1)} %copy.74._), custom_call_target="tpu_custom_call" | custom-call | bytes 15925248 | tf_op jit(solution)/shard_map/pallas_call | solution.py:39
  16.4 3.1 %copy-done = bf16[3,384,3456]{2,1,0:T(8,128)(2,1)} copy-done((bf16[3,384,3456]{2,1,0:T(8,128)(2,1)}, bf16[3,384,3456]{2,1,0:T(8,128)(2,1)S(1)}, u32[]{:S(2)}) %copy-start) | copy-done | bytes 7962648
  21.3 3.3 %copy-done.1 = bf16[3,384,3456]{2,1,0:T(8,128)(2,1)S(1)} copy-done((bf16[3,384,3456]{2,1,0:T(8,128)(2,1)S(1)}, bf16[3,384,3456]{2,1,0:T(8,128)(2,1)}, u32[]{:S(2)}) %copy-start.1) | copy-done | bytes 7962648
  26.1 1.4 %collective-permute-done.4.refs_0_ = bf16[384,512]{1,0:T(8,128)(2,1)S(1)} collective-permute-done((bf16[384,512]{1,0:T(8,128)(2,1)S(1)}, bf16[384,512]{1,0:T(8,128)(2,1)S(1)}, u32[]{:S(2)}, u32[]{:S(2)}) %collective-permute-start.4) | collective-permute-done | bytes 393248 | tf_op jit(solution)/shard_map/ppermute | solution.py:198
  32.1 24.9 %collective-permute-start.10 = (bf16[384,512]{1,0:T(8,128)(2,1)S(1)}, bf16[384,512]{1,0:T(8,128)(2,1)S(1)}, u32[]{:S(2)}, u32[]{:S(2)}) collective-permute-start(bf16[384,512]{1,0:T(8,128)(2,1)S(1)} %get-tuple-element.120), channel_id=1, source_target_pairs={{0,8},{1,9},{2,10},{3,11},{4,12},{5,13},{6,14},{7,15},{8,0},{9,1},... | collective-permute-start | bytes 1179656 | tf_op jit(solution)/shard_map/ppermute | solution.py:198
  57.0 1.3 %collective-permute-done.10.refs_0_ = bf16[384,512]{1,0:T(8,128)(2,1)S(1)} collective-permute-done((bf16[384,512]{1,0:T(8,128)(2,1)S(1)}, bf16[384,512]{1,0:T(8,128)(2,1)S(1)}, u32[]{:S(2)}, u32[]{:S(2)}) %collective-permute-start.10) | collective-permute-done | bytes 393248 | tf_op jit(solution)/shard_map/ppermute | solution.py:198
  58.3 1.4 %shard_map.72 = (bf16[384,256]{1,0:T(8,128)(2,1)S(1)}, bf16[384,512]{1,0:T(8,128)(2,1)S(1)}, s32[2]{0:T(128)S(1)}, bf16[3,384,3456]{2,1,0:T(8,128)(2,1)S(1)}, f3...) custom-call(s32[2]{0:T(128)S(1)} %get-tuple-element.114.place_ref, ...), custom_call_target="tpu_custom_call", output_to_operand_aliasing={{3}: (1, {}), {4}: (2, {}), {5}: (3, {})} | custom-call | flops 2038431744 | tf_op jit(solution)/shard_map/pallas_call | solution.py:159
  61.8 1.2 shard_map.73
  63.0 9.5 %collective-permute-start.14 = (bf16[384,512]{1,0:T(8,128)(2,1)S(1)}, bf16[384,512]{1,0:T(8,128)(2,1)S(1)}, u32[]{:S(2)}, u32[]{:S(2)}) collective-permute-start(bf16[384,512]{1,0:T(8,128)(2,1)S(1)} %get-tuple-element.136), channel_id=1, source_target_pairs={{0,8},{1,9},{2,10},{3,11},{4,12},{5,13},{6,14},{7,15},{8,0},{9,1},... | collective-permute-start | bytes 1179656 | tf_op jit(solution)/shard_map/ppermute | solution.py:198
  72.6 1.3 %collective-permute-done.14.refs_0_ = bf16[384,512]{1,0:T(8,128)(2,1)S(1)} collective-permute-done((bf16[384,512]{1,0:T(8,128)(2,1)S(1)}, bf16[384,512]{1,0:T(8,128)(2,1)S(1)}, u32[]{:S(2)}, u32[]{:S(2)}) %collective-permute-start.14) | collective-permute-done | bytes 393248 | tf_op jit(solution)/shard_map/ppermute | solution.py:198
  73.9 5.6 %shard_map.74 = (bf16[384,256]{1,0:T(8,128)(2,1)S(1)}, bf16[384,512]{1,0:T(8,128)(2,1)S(1)}, s32[2]{0:T(128)S(1)}, bf16[3,384,3456]{2,1,0:T(8,128)(2,1)S(1)}, f3...) custom-call(s32[2]{0:T(128)S(1)} %get-tuple-element.130.place_ref, ...), custom_call_target="tpu_custom_call", output_to_operand_aliasing={{3}: (1, {}), {4}: (2, {}), {5}: (3, {})} | custom-call | flops 2038431744 | tf_op jit(solution)/shard_map/pallas_call | solution.py:159
  81.6 1.2 shard_map.75
  82.9 6.9 %collective-permute-start.18 = (bf16[384,512]{1,0:T(8,128)(2,1)S(1)}, bf16[384,512]{1,0:T(8,128)(2,1)S(1)}, u32[]{:S(2)}, u32[]{:S(2)}) collective-permute-start(bf16[384,512]{1,0:T(8,128)(2,1)S(1)} %get-tuple-element.152), channel_id=1, source_target_pairs={{0,8},{1,9},{2,10},{3,11},{4,12},{5,13},{6,14},{7,15},{8,0},{9,1},... | collective-permute-start | bytes 1179656 | tf_op jit(solution)/shard_map/ppermute | solution.py:198
  89.8 1.3 %collective-permute-done.18.refs_0_ = bf16[384,512]{1,0:T(8,128)(2,1)S(1)} collective-permute-done((bf16[384,512]{1,0:T(8,128)(2,1)S(1)}, bf16[384,512]{1,0:T(8,128)(2,1)S(1)}, u32[]{:S(2)}, u32[]{:S(2)}) %collective-permute-start.18) | collective-permute-done | bytes 393248 | tf_op jit(solution)/shard_map/ppermute | solution.py:198
  91.2 6.0 %shard_map.76 = (bf16[384,256]{1,0:T(8,128)(2,1)S(1)}, bf16[384,512]{1,0:T(8,128)(2,1)S(1)}, s32[2]{0:T(128)S(1)}, bf16[3,384,3456]{2,1,0:T(8,128)(2,1)S(1)}, f3...) custom-call(s32[2]{0:T(128)S(1)} %get-tuple-element.146.place_ref, ...), custom_call_target="tpu_custom_call", output_to_operand_aliasing={{3}: (1, {}), {4}: (2, {}), {5}: (3, {})} | custom-call | flops 2038431744 | tf_op jit(solution)/shard_map/pallas_call | solution.py:159
  100.5 6.0 %collective-permute-start.22 = (bf16[384,512]{1,0:T(8,128)(2,1)S(1)}, bf16[384,512]{1,0:T(8,128)(2,1)S(1)}, u32[]{:S(2)}, u32[]{:S(2)}) collective-permute-start(bf16[384,512]{1,0:T(8,128)(2,1)S(1)} %get-tuple-element.168), channel_id=1, source_target_pairs={{0,8},{1,9},{2,10},{3,11},{4,12},{5,13},{6,14},{7,15},{8,0},{9,1},... | collective-permute-start | bytes 1179656 | tf_op jit(solution)/shard_map/ppermute | solution.py:198
  106.5 1.3 collective-permute-start.23
  107.8 1.3 %collective-permute-start.24 = (bf16[384,256]{1,0:T(8,128)(2,1)S(1)}, bf16[384,256]{1,0:T(8,128)(2,1)S(1)}, u32[]{:S(2)}, u32[]{:S(2)}) collective-permute-start(bf16[384,256]{1,0:T(8,128)(2,1)S(1)} %get-tuple-element.167), channel_id=1, source_target_pairs={{24,8},{25,9},{26,10},{27,11},{28,12},{29,13},{30,14},{31,15}} | collective-permute-start | bytes 589832 | tf_op jit(solution)/shard_map/ppermute | solution.py:198
  109.1 1.3 collective-permute-done.23.refs_5_
  110.4 5.8 %shard_map.78 = (bf16[384,256]{1,0:T(8,128)(2,1)S(1)}, bf16[384,512]{1,0:T(8,128)(2,1)S(1)}, s32[2]{0:T(128)S(1)}, bf16[3,384,3456]{2,1,0:T(8,128)(2,1)S(1)}, f3...) custom-call(s32[2]{0:T(128)S(1)} %get-tuple-element.162.place_ref, ...), custom_call_target="tpu_custom_call", output_to_operand_aliasing={{3}: (1, {}), {4}: (2, {}), {5}: (3, {})} | custom-call | flops 2038431744 | tf_op jit(solution)/shard_map/pallas_call | solution.py:159
  118.0 1.9 %collective-permute-start.26 = (bf16[384,256]{1,0:T(8,128)(2,1)S(1)}, bf16[384,256]{1,0:T(8,128)(2,1)S(1)}, u32[]{:S(2)}, u32[]{:S(2)}) collective-permute-start(bf16[384,256]{1,0:T(8,128)(2,1)S(1)} %get-tuple-element.184), channel_id=1, source_target_pairs={{24,16},{25,17},{26,18},{27,19},{28,20},{29,21},{30,22},{31,23}} | collective-permute-start | bytes 589832 | tf_op jit(solution)/shard_map/ppermute | solution.py:198
  121.0 5.7 %shard_map.80 = (bf16[384,256]{1,0:T(8,128)(2,1)S(1)}, bf16[384,512]{1,0:T(8,128)(2,1)S(1)}, s32[2]{0:T(128)}, bf16[3,384,3456]{2,1,0:T(8,128)(2,1)S(1)}, f32[384,1]{1,0:T(8,128)S(1)}, /*index=5*/f32[384,1]{1,0:T(8,128)S(1)}) custom-call(s32[2]{0:T(128)S(1)} %get-tuple-element.178.place_ref, ...), custom_call_target="tpu_custom_call", output_to_operand_aliasing={{3}: (1, {}), {4}: (2, {}), {5}: (3, {})} | custom-call | flops 2038431744 | tf_op jit(solution)/shard_map/pallas_call | solution.py:159
  (68 shorter events, 26.0 us)
Async XLA Ops:
  2.8 18.4 %collective-permute-start.1 = (bf16[2,384,256]{2,1,0:T(8,128)(2,1)S(1)}, bf16[2,384,256]{2,1,0:T(8,128)(2,1)S(1)}, u32[]{:S(2)}, u32[]{:S(2)}) collective-permute-start(bf16[2,384,256]{2,1,0:T(8,128)(2,1)S(1)} %copy.81.refs_0_.refs_1_), channel_id=1, source_target_pairs={{1,0},{2,1},{3,2},{4,3},{5,4},{6,5},{7,6},{17,16},{18,17},{19,18},... | collective-permute-start | bytes 1179656 | tf_op jit(solution)/shard_map/ppermute | solution.py:198
  3.5 17.8 %collective-permute-start = (bf16[2,384,256]{2,1,0:T(8,128)(2,1)S(1)}, bf16[2,384,256]{2,1,0:T(8,128)(2,1)S(1)}, u32[]{:S(2)}, u32[]{:S(2)}) collective-permute-start(bf16[2,384,256]{2,1,0:T(8,128)(2,1)S(1)} %copy.81.refs_0_.refs_1_), channel_id=1, source_target_pairs={{0,1},{1,2},{2,3},{3,4},{4,5},{5,6},{6,7},{16,17},{17,18},{18,19},... | collective-permute-start | bytes 1179656 | tf_op jit(solution)/shard_map/ppermute | solution.py:198
  4.4 16.1 %collective-permute-start.2 = (bf16[384,128]{1,0:T(8,128)(2,1)S(1)}, bf16[384,128]{1,0:T(8,128)(2,1)S(1)}, u32[]{:S(2)}, u32[]{:S(2)}) collective-permute-start(bf16[384,128]{1,0:T(8,128)(2,1)S(1)} %copy.102), channel_id=1, source_target_pairs={{8,9},{9,10},{10,11},{11,12},{12,13},{13,14},{14,15},{24,25},{25,2... | collective-permute-start | bytes 294920 | tf_op jit(solution)/shard_map/ppermute | solution.py:198
  7.7 13.6 %collective-permute-start.3 = (bf16[384,128]{1,0:T(8,128)(2,1)S(1)}, bf16[384,128]{1,0:T(8,128)(2,1)S(1)}, u32[]{:S(2)}, u32[]{:S(2)}) collective-permute-start(bf16[384,128]{1,0:T(8,128)(2,1)S(1)} %copy.103), channel_id=1, source_target_pairs={{9,8},{10,9},{11,10},{12,11},{13,12},{14,13},{15,14},{25,24},{26,2... | collective-permute-start | bytes 294920 | tf_op jit(solution)/shard_map/ppermute | solution.py:198
  19.8 6.3 %collective-permute-start.6 = (bf16[3,384,256]{2,1,0:T(8,128)(2,1)S(1)}, bf16[3,384,256]{2,1,0:T(8,128)(2,1)S(1)}, u32[]{:S(2)}, u32[]{:S(2)}) collective-permute-start(bf16[3,384,256]{2,1,0:T(8,128)(2,1)S(1)} %copy.82.refs_4_), channel_id=1, source_target_pairs={{1,0},{2,1},{3,2},{4,3},{5,4},{6,5},{7,6}} | collective-permute-start | bytes 1769480 | tf_op jit(solution)/shard_map/ppermute | solution.py:198
  20.5 5.6 %collective-permute-start.5 = (bf16[3,384,256]{2,1,0:T(8,128)(2,1)S(1)}, bf16[3,384,256]{2,1,0:T(8,128)(2,1)S(1)}, u32[]{:S(2)}, u32[]{:S(2)}) collective-permute-start(bf16[3,384,256]{2,1,0:T(8,128)(2,1)S(1)} %copy.82.refs_4_), channel_id=1, source_target_pairs={{0,1},{1,2},{2,3},{3,4},{4,5},{5,6},{6,7}} | collective-permute-start | bytes 1769480 | tf_op jit(solution)/shard_map/ppermute | solution.py:198
  28.7 3.3 %collective-permute-start.9 = (bf16[384,256]{1,0:T(8,128)(2,1)S(1)}, bf16[384,256]{1,0:T(8,128)(2,1)S(1)}, u32[]{:S(2)}, u32[]{:S(2)}) collective-permute-start(bf16[384,256]{1,0:T(8,128)(2,1)S(1)} %get-tuple-element.119), channel_id=1, source_target_pairs={{9,16},{10,17},{11,18},{12,19},{13,20},{14,21},{15,22}} | collective-permute-start | bytes 589832 | tf_op jit(solution)/shard_map/ppermute | solution.py:198
  29.4 2.6 %collective-permute-start.8 = (bf16[384,256]{1,0:T(8,128)(2,1)S(1)}, bf16[384,256]{1,0:T(8,128)(2,1)S(1)}, u32[]{:S(2)}, u32[]{:S(2)}) collective-permute-start(bf16[384,256]{1,0:T(8,128)(2,1)S(1)} %get-tuple-element.119), channel_id=1, source_target_pairs={{8,17},{9,18},{10,19},{11,20},{12,21},{13,22},{14,23}} | collective-permute-start | bytes 589832 | tf_op jit(solution)/shard_map/ppermute | solution.py:198
  32.1 26.3 %collective-permute-start.10 = (bf16[384,512]{1,0:T(8,128)(2,1)S(1)}, bf16[384,512]{1,0:T(8,128)(2,1)S(1)}, u32[]{:S(2)}, u32[]{:S(2)}) collective-permute-start(bf16[384,512]{1,0:T(8,128)(2,1)S(1)} %get-tuple-element.120), channel_id=1, source_target_pairs={{0,8},{1,9},{2,10},{3,11},{4,12},{5,13},{6,14},{7,15},{8,0},{9,1},... | collective-permute-start | bytes 1179656 | tf_op jit(solution)/shard_map/ppermute | solution.py:198
  59.7 3.3 %collective-permute-start.13 = (bf16[384,256]{1,0:T(8,128)(2,1)S(1)}, bf16[384,256]{1,0:T(8,128)(2,1)S(1)}, u32[]{:S(2)}, u32[]{:S(2)}) collective-permute-start(bf16[384,256]{1,0:T(8,128)(2,1)S(1)} %get-tuple-element.135), channel_id=1, source_target_pairs={{9,16},{10,17},{11,18},{12,19},{13,20},{14,21},{15,22}} | collective-permute-start | bytes 589832 | tf_op jit(solution)/shard_map/ppermute | solution.py:198
  60.4 2.6 %collective-permute-start.12 = (bf16[384,256]{1,0:T(8,128)(2,1)S(1)}, bf16[384,256]{1,0:T(8,128)(2,1)S(1)}, u32[]{:S(2)}, u32[]{:S(2)}) collective-permute-start(bf16[384,256]{1,0:T(8,128)(2,1)S(1)} %get-tuple-element.135), channel_id=1, source_target_pairs={{8,17},{9,18},{10,19},{11,20},{12,21},{13,22},{14,23}} | collective-permute-start | bytes 589832 | tf_op jit(solution)/shard_map/ppermute | solution.py:198
  61.1 1.9 %collective-permute-start.11 = (bf16[384,256]{1,0:T(8,128)(2,1)S(1)}, bf16[384,256]{1,0:T(8,128)(2,1)S(1)}, u32[]{:S(2)}, u32[]{:S(2)}) collective-permute-start(bf16[384,256]{1,0:T(8,128)(2,1)S(1)} %get-tuple-element.135), channel_id=1, source_target_pairs={{8,16},{9,17},{10,18},{11,19},{12,20},{13,21},{14,22},{15,23}} | collective-permute-start | bytes 589832 | tf_op jit(solution)/shard_map/ppermute | solution.py:198
  63.0 10.9 %collective-permute-start.14 = (bf16[384,512]{1,0:T(8,128)(2,1)S(1)}, bf16[384,512]{1,0:T(8,128)(2,1)S(1)}, u32[]{:S(2)}, u32[]{:S(2)}) collective-permute-start(bf16[384,512]{1,0:T(8,128)(2,1)S(1)} %get-tuple-element.136), channel_id=1, source_target_pairs={{0,8},{1,9},{2,10},{3,11},{4,12},{5,13},{6,14},{7,15},{8,0},{9,1},... | collective-permute-start | bytes 1179656 | tf_op jit(solution)/shard_map/ppermute | solution.py:198
  79.6 3.3 %collective-permute-start.17 = (bf16[384,256]{1,0:T(8,128)(2,1)S(1)}, bf16[384,256]{1,0:T(8,128)(2,1)S(1)}, u32[]{:S(2)}, u32[]{:S(2)}) collective-permute-start(bf16[384,256]{1,0:T(8,128)(2,1)S(1)} %get-tuple-element.151), channel_id=1, source_target_pairs={{9,16},{10,17},{11,18},{12,19},{13,20},{14,21},{15,22}} | collective-permute-start | bytes 589832 | tf_op jit(solution)/shard_map/ppermute | solution.py:198
  80.2 2.6 %collective-permute-start.16 = (bf16[384,256]{1,0:T(8,128)(2,1)S(1)}, bf16[384,256]{1,0:T(8,128)(2,1)S(1)}, u32[]{:S(2)}, u32[]{:S(2)}) collective-permute-start(bf16[384,256]{1,0:T(8,128)(2,1)S(1)} %get-tuple-element.151), channel_id=1, source_target_pairs={{8,17},{9,18},{10,19},{11,20},{12,21},{13,22},{14,23}} | collective-permute-start | bytes 589832 | tf_op jit(solution)/shard_map/ppermute | solution.py:198
  80.9 1.9 %collective-permute-start.15 = (bf16[384,256]{1,0:T(8,128)(2,1)S(1)}, bf16[384,256]{1,0:T(8,128)(2,1)S(1)}, u32[]{:S(2)}, u32[]{:S(2)}) collective-permute-start(bf16[384,256]{1,0:T(8,128)(2,1)S(1)} %get-tuple-element.151), channel_id=1, source_target_pairs={{8,16},{9,17},{10,18},{11,19},{12,20},{13,21},{14,22},{15,23}} | collective-permute-start | bytes 589832 | tf_op jit(solution)/shard_map/ppermute | solution.py:198
  82.9 8.3 %collective-permute-start.18 = (bf16[384,512]{1,0:T(8,128)(2,1)S(1)}, bf16[384,512]{1,0:T(8,128)(2,1)S(1)}, u32[]{:S(2)}, u32[]{:S(2)}) collective-permute-start(bf16[384,512]{1,0:T(8,128)(2,1)S(1)} %get-tuple-element.152), channel_id=1, source_target_pairs={{0,8},{1,9},{2,10},{3,11},{4,12},{5,13},{6,14},{7,15},{8,0},{9,1},... | collective-permute-start | bytes 1179656 | tf_op jit(solution)/shard_map/ppermute | solution.py:198
  97.2 3.3 %collective-permute-start.21 = (bf16[384,256]{1,0:T(8,128)(2,1)S(1)}, bf16[384,256]{1,0:T(8,128)(2,1)S(1)}, u32[]{:S(2)}, u32[]{:S(2)}) collective-permute-start(bf16[384,256]{1,0:T(8,128)(2,1)S(1)} %get-tuple-element.167), channel_id=1, source_target_pairs={{9,16},{10,17},{11,18},{12,19},{13,20},{14,21},{15,22}} | collective-permute-start | bytes 589832 | tf_op jit(solution)/shard_map/ppermute | solution.py:198
  97.9 2.6 %collective-permute-start.20 = (bf16[384,256]{1,0:T(8,128)(2,1)S(1)}, bf16[384,256]{1,0:T(8,128)(2,1)S(1)}, u32[]{:S(2)}, u32[]{:S(2)}) collective-permute-start(bf16[384,256]{1,0:T(8,128)(2,1)S(1)} %get-tuple-element.167), channel_id=1, source_target_pairs={{8,17},{9,18},{10,19},{11,20},{12,21},{13,22},{14,23}} | collective-permute-start | bytes 589832 | tf_op jit(solution)/shard_map/ppermute | solution.py:198
  100.5 9.9 %collective-permute-start.22 = (bf16[384,512]{1,0:T(8,128)(2,1)S(1)}, bf16[384,512]{1,0:T(8,128)(2,1)S(1)}, u32[]{:S(2)}, u32[]{:S(2)}) collective-permute-start(bf16[384,512]{1,0:T(8,128)(2,1)S(1)} %get-tuple-element.168), channel_id=1, source_target_pairs={{0,8},{1,9},{2,10},{3,11},{4,12},{5,13},{6,14},{7,15},{8,0},{9,1},... | collective-permute-start | bytes 1179656 | tf_op jit(solution)/shard_map/ppermute | solution.py:198
  106.5 3.9 %collective-permute-start.23 = (bf16[384,256]{1,0:T(8,128)(2,1)S(1)}, bf16[384,256]{1,0:T(8,128)(2,1)S(1)}, u32[]{:S(2)}, u32[]{:S(2)}) collective-permute-start(bf16[384,256]{1,0:T(8,128)(2,1)S(1)} %get-tuple-element.151), channel_id=1, source_target_pairs={{24,0},{25,1},{26,2},{27,3},{28,4},{29,5},{30,6},{31,7}} | collective-permute-start | bytes 589832 | tf_op jit(solution)/shard_map/ppermute | solution.py:198
  107.8 8.4 %collective-permute-start.24 = (bf16[384,256]{1,0:T(8,128)(2,1)S(1)}, bf16[384,256]{1,0:T(8,128)(2,1)S(1)}, u32[]{:S(2)}, u32[]{:S(2)}) collective-permute-start(bf16[384,256]{1,0:T(8,128)(2,1)S(1)} %get-tuple-element.167), channel_id=1, source_target_pairs={{24,8},{25,9},{26,10},{27,11},{28,12},{29,13},{30,14},{31,15}} | collective-permute-start | bytes 589832 | tf_op jit(solution)/shard_map/ppermute | solution.py:198
  117.4 3.6 %collective-permute-start.25 = (bf16[384,512]{1,0:T(8,128)(2,1)S(1)}, bf16[384,512]{1,0:T(8,128)(2,1)S(1)}, u32[]{:S(2)}, u32[]{:S(2)}) collective-permute-start(bf16[384,512]{1,0:T(8,128)(2,1)S(1)} %get-tuple-element.182), channel_id=1, source_target_pairs={{0,8},{1,9},{2,10},{3,11},{4,12},{5,13},{6,14},{7,15},{8,0},{9,1},... | collective-permute-start | bytes 1179656 | tf_op jit(solution)/shard_map/ppermute | solution.py:198
  118.0 3.0 %collective-permute-start.26 = (bf16[384,256]{1,0:T(8,128)(2,1)S(1)}, bf16[384,256]{1,0:T(8,128)(2,1)S(1)}, u32[]{:S(2)}, u32[]{:S(2)}) collective-permute-start(bf16[384,256]{1,0:T(8,128)(2,1)S(1)} %get-tuple-element.184), channel_id=1, source_target_pairs={{24,16},{25,17},{26,18},{27,19},{28,20},{29,21},{30,22},{31,23}} | collective-permute-start | bytes 589832 | tf_op jit(solution)/shard_map/ppermute | solution.py:198
  (6 other events, 21.4 us)

commit v2 on v1

--- a/solution.py
+++ b/solution.py
@@ -16,43 +16,50 @@
 SMEM = pl.BlockSpec(memory_space=pltpu.SMEM)
 
 
-def turn_kernel(w_ref, bias_ref, gain_ref, _, out_ref, bias_out, gain_out, ws, rows, sems):
+def turn_kernel(cuts, w_ref, bias_ref, gain_ref, later_ref, first_ref, out_ref, bias_out, gain_out, _, *refs):
+    ws, rows, sems, cut_sems = refs[-4:]
     channels = w_ref.shape[-1]
     copies = [pltpu.make_async_copy(w_ref.at[k // 3, k % 3], ws.at[k], sems.at[k]) for k in range(9)]
     vectors = [pltpu.make_async_copy(ref, rows.at[pl.ds(k, 1)], sems.at[9 + k])
                for k, ref in enumerate((bias_ref, gain_ref))]
-    for copy in vectors + copies:
+    parts = [pltpu.make_async_copy(first_ref.at[pl.ds(0, n), :, pl.ds(at, width)], refs[k], cut_sems.at[k])
+             for k, (n, at, width) in enumerate(cuts)]
+    for copy in vectors + copies + parts:
         copy.start()
     for k, copy in enumerate(copies):
         copy.wait()
         for c in range(3):
             out_ref[k % 3, :, pl.ds((k // 3 * 3 + c) * channels, channels)] = jnp.transpose(ws[k, c], (1, 0))
-    for copy in vectors:
+    for copy in vectors + parts:
         copy.wait()
     turned = jnp.transpose(rows[...], (1, 0))
     bias_out[...] = turned[:, 0:1]
     gain_out[...] = turned[:, 1:2]
 
 
-def turned_weights(weight, bias, gain, ahead):
+def turned_weights(weight, bias, gain, later, first, cuts):
     channels = weight.shape[-1]
     return pl.pallas_call(
-        turn_kernel,
+        functools.partial(turn_kernel, cuts),
         out_shape=(
             jax.ShapeDtypeStruct((3, channels, 9 * channels), BF16),
             jax.ShapeDtypeStruct((channels, 1), F32),
             jax.ShapeDtypeStruct((channels, 1), F32),
+            jax.ShapeDtypeStruct(later.shape, later.dtype),
+            *(jax.ShapeDtypeStruct((n, channels, width), BF16) for n, _, width in cuts),
         ),
-        in_specs=[pl.BlockSpec(memory_space=pltpu.HBM)] * 3 + [ANY],
-        out_specs=(VMEM, VMEM, VMEM),
+        in_specs=[pl.BlockSpec(memory_space=pltpu.HBM)] * 3 + [ANY] * 2,
+        out_specs=(VMEM, VMEM, VMEM, ANY) + (ANY,) * len(cuts),
+        input_output_aliases={3: 3},
         scratch_shapes=[
             pltpu.VMEM((9, 3, channels, channels), BF16),
             pltpu.VMEM((8, channels), F32),
             pltpu.SemaphoreType.DMA((11,)),
+            pltpu.SemaphoreType.DMA((len(cuts),)),
         ],
         compiler_params=pltpu.CompilerParams(vmem_limit_bytes=VMEM_BYTES),
         cost_estimate=pl.CostEstimate(flops=0, bytes_accessed=4 * weight.size, transcendentals=0),
-    )(*(pltpu.with_memory_space_constraint(v, pltpu.HBM) for v in (weight, bias, gain)), ahead)
+    )(*(pltpu.with_memory_space_constraint(v, pltpu.HBM) for v in (weight, bias, gain)), later, first)
 
 
 def layer_kernel(cases, rows_in, own, cols, block, height, n_in, place_ref, w_ref, bias_ref, gain_ref, *refs):
@@ -138,8 +145,8 @@
         def taps(n, _):
             at = pl.multiple_of(n * step, step)
             part = xs[:, pl.ds(at + row, step)].astype(F32) + bias_ref[...]
-            for b in range(3):
-                part = part + jnp.dot(w_ref[b], buf[:, pl.ds(at + b * row, step)], preferred_element_type=F32)
+            part = lax.fori_loop(0, 3, lambda b, part: part + jnp.dot(
+                w_ref[b], buf[:, pl.ds(pl.multiple_of(at + b * row, row), step)], preferred_element_type=F32), part)
             line = top + 2 * n + lax.broadcasted_iota(jnp.int32, (1, step), 1) // row
             total[:, pl.ds(at, step)] = jnp.where(
                 jnp.logical_and(line >= 0, line < height), part, 0.0).astype(BF16)
@@ -198,22 +205,20 @@
         return lax.ppermute(value, axes, [
             (a * slabs + s, b * slabs + s + step) for a, b in pairs for s in range(slabs) if 0 <= s + step < slabs])
 
-    def around(value, pairs, rows):
-        above = moved(value[..., (own - rows) * row:], pairs, 1)
-        below = moved(value[..., :rows * row], pairs, -1)
-        return above, below
-
     def lanes(value):
         value = value.reshape(-1, block, own, cols, channels)
         return value.transpose(0, 4, 2, 1, 3).reshape(-1, channels, own * row)
 
     first = lanes(jnp.concatenate([cache_in[0], video_in[:block]], axis=0))
-    first_above, first_below = around(first, [(g, g) for g in evens], 2)
-    odd_above, odd_below = around(first[0], [(g, g) for g in odds], 1)
-    later, place, weight = lax.optimization_barrier((lanes(video_in[block:]), place, conv_weight[0]))
-    weight, bias, gain = turned_weights(weight, conv_bias, norm_gain, later)
-    later, weight = lax.optimization_barrier((later, weight))
-    later_above, later_below = around(later, [(0, 0)], 2)
+    first_below = moved(first[..., :2 * row], [(g, g) for g in evens], -1)
+    place, weight = lax.optimization_barrier((place, conv_weight[0]))
+    cuts = ((2, (own - 2) * row, 2 * row), (1, (own - 1) * row, row), (1, 0, row))
+    weight, bias, gain, later, above, odd_last, odd_first = turned_weights(
+        weight, conv_bias, norm_gain, lanes(video_in[block:]), first, cuts)
+    first_above = moved(above, [(g, g) for g in evens], 1)
+    odd_above = moved(odd_last, [(g, g) for g in odds], 1)
+    odd_below = moved(odd_first, [(g, g) for g in odds], -1)
+    later_below = moved(later[..., :2 * row], [(0, 0)], -1)
     fixed = (place, weight, bias, gain)
 
     call = functools.partial(layer_call, own=own, cols=cols, block=block, height=height)
@@ -253,13 +258,16 @@
         if 0 < tick <= blocks:
             out, *arrived[tick - 1] = lax.optimization_barrier((out, *arrived[tick - 1]))
         crossed = moved(out, across, 0)
+        if tick == 0:
+            crossed, sent = lax.optimization_barrier((crossed, later[..., (own - 2) * row:]))
+            later_above = moved(sent, [(0, 0)], 1)
 
         ins = [crossed, first, odd_above, odd_below]
-        old = [(2, None, 0, 1), (1, 0, 0, own), (3, None, 0, 1)]
+        old = [(2, 0, 0, 1), (1, 0, 0, own), (3, 0, 0, 1)]
         if tick:
             ins.append(odd_acts)
         if tick == 0:
-            ins += [later_above, later_below]
+            ins.append(later_below)
         if tick >= ticks - 2:
             ins.append(done[0] if tick < ticks - 1 else done[-1])
         cases = [(2 * p + 1, [(0, None, 0, own + 2)], old if tick == LAG * p else [(4, None, 0, own + 2)]) for p in busy]

time: 130 us -> 144 us (1.11); the launches traced: 129 us -> 142 us
  starting transfers between devices: 69.9 us -> 82.3 us
  local copies, waits for them, and re-layouts: 11.3 us -> 4.33 us
  waiting for transfers between devices: 7.84 us -> 13.7 us
  Pallas kernels: 37.2 us -> 39.2 us
    ppermute x27, starting transfers between devices: 69.9 us -> 82.3 us  [moved(): lax.ppermute(value, axes, [(a * slabs + s, b * slabs + s + step) for a, b...]
    unnamed x10 -> x2, local copies, waits for them, and re-layouts: 8.01 us -> 1.4 us
    ppermute x27, waiting for transfers between devices: 7.84 us -> 13.7 us  [moved(): lax.ppermute(value, axes, [(a * slabs + s, b * slabs + s + step) for a, b...]
    pallas_call x12, Pallas kernels: 33.1 us -> 35 us  [layer_call(): pl.pallas_call(functools.partial(layer_kernel, cases, rows_in, own, cols,...]
  transfers between devices with their start and end apart: 27 -> 27, of which waited for: 6 -> 8; matrix products, arithmetic and copies ran while one was open for 2% -> 1% of each run, Pallas kernels for 12% -> 12%
where the time goes in v2:
time: 144 us; the launch traced here: 142 us
  starting transfers between devices  82.3 us (57%)
  Pallas kernels  39.2 us (27%)
  waiting for transfers between devices  13.7 us (10%)
  local copies, waits for them, and re-layouts  4.33 us (3%)
    ppermute x27, starting transfers between devices, moved(): lax.ppermute(value, axes, [(a * slabs + s, b * slabs + s + step) for a, b...  82.3 us
    pallas_call x12, Pallas kernels, layer_call(): pl.pallas_call(functools.partial(layer_kernel, cases, rows_in, own, cols,...  35 us
    ppermute x27, waiting for transfers between devices, moved(): lax.ppermute(value, axes, [(a * slabs + s, b * slabs + s + step) for a, b...  13.7 us
    pallas_call x1, Pallas kernels, turned_weights(): pl.pallas_call(functools.partial(turn_kernel, cuts), out_shape=(jax.Shape...  4.17 us
  transfers between devices with their start and end apart: 27, of which 8 were waited for; matrix products, arithmetic and copies ran while one was open for 1% of the time, Pallas kernels for 12%

profile of v2, /device:TPU:13, one launch (start us, length us, event | category | flops | bytes accessed | tf_op | source)
XLA Modules:
  0.0 141.8 jit_solution(15226719738275849662)
XLA Ops:
  5.0 4.2 %shard_map.68 = (bf16[3,384,3456]{2,1,0:T(8,128)(2,1)S(1)}, f32[384,1]{1,0:T(8,128)S(1)}, f32[384,1]{1,0:T(8,128)S(1)}, bf16[3,384,256]{2,1,0:T(8,128)(2,1)S(1)}...) custom-call(bf16[3,3,3,384,384]{4,3,2,1,0:T(8,128)(2,1)} %bitcast.20, ...), custom_call_target="tpu_custom_call", output_to_operand_aliasing={{3}: (3, {})} | custom-call | bytes 15925248 | tf_op jit(solution)/shard_map/pallas_call | solution.py:42
  9.9 3.1 %collective-permute-start.2 = (bf16[1,384,128]{2,1,0:T(8,128)(2,1)S(1)}, bf16[1,384,128]{2,1,0:T(8,128)(2,1)S(1)}, u32[]{:S(2)}, u32[]{:S(2)}) collective-permute-start(bf16[1,384,128]{2,1,0:T(8,128)(2,1)S(1)} %get-tuple-element.105), channel_id=1, source_target_pairs={{8,9},{9,10},{10,11},{11,12},{12,13},{13,14},{14,15},{24,25},{25,2... | collective-permute-start | bytes 294920 | tf_op jit(solution)/shard_map/ppermute | solution.py:205
  13.0 3.1 %collective-permute-start.3 = (bf16[1,384,128]{2,1,0:T(8,128)(2,1)S(1)}, bf16[1,384,128]{2,1,0:T(8,128)(2,1)S(1)}, u32[]{:S(2)}, u32[]{:S(2)}) collective-permute-start(bf16[1,384,128]{2,1,0:T(8,128)(2,1)S(1)} %get-tuple-element.106), channel_id=1, source_target_pairs={{9,8},{10,9},{11,10},{12,11},{13,12},{14,13},{15,14},{25,24},{26,2... | collective-permute-start | bytes 294920 | tf_op jit(solution)/shard_map/ppermute | solution.py:205
  16.2 6.5 %collective-permute-done.3.refs_4_.refs_3_ = bf16[1,384,128]{2,1,0:T(8,128)(2,1)S(1)} collective-permute-done((bf16[1,384,128]{2,1,0:T(8,128)(2,1)S(1)}, bf16[1,384,128]{2,1,0:T(8,128)(2,1)S(1)}, u32[]{:S(2)}, u32[]{:S(2)}) %collective-permute-start.3) | collective-permute-done | bytes 98336 | tf_op jit(solution)/shard_map/ppermute | solution.py:205
  29.8 1.2 shard_map.71
  31.0 22.7 %collective-permute-start.10 = (bf16[384,512]{1,0:T(8,128)(2,1)S(1)}, bf16[384,512]{1,0:T(8,128)(2,1)S(1)}, u32[]{:S(2)}, u32[]{:S(2)}) collective-permute-start(bf16[384,512]{1,0:T(8,128)(2,1)S(1)} %get-tuple-element.126), channel_id=1, source_target_pairs={{0,8},{1,9},{2,10},{3,11},{4,12},{5,13},{6,14},{7,15},{8,0},{9,1},... | collective-permute-start | bytes 1179656 | tf_op jit(solution)/shard_map/ppermute | solution.py:205
  53.8 1.3 collective-permute-done.10.refs_0_
  58.4 1.2 shard_map.73
  59.7 23.8 %collective-permute-start.14 = (bf16[384,512]{1,0:T(8,128)(2,1)S(1)}, bf16[384,512]{1,0:T(8,128)(2,1)S(1)}, u32[]{:S(2)}, u32[]{:S(2)}) collective-permute-start(bf16[384,512]{1,0:T(8,128)(2,1)S(1)} %get-tuple-element.142), channel_id=1, source_target_pairs={{0,8},{1,9},{2,10},{3,11},{4,12},{5,13},{6,14},{7,15},{8,0},{9,1},... | collective-permute-start | bytes 1179656 | tf_op jit(solution)/shard_map/ppermute | solution.py:205
  83.5 1.3 collective-permute-done.14.refs_0_
  84.8 6.4 %shard_map.74 = (bf16[384,256]{1,0:T(8,128)(2,1)S(1)}, bf16[384,512]{1,0:T(8,128)(2,1)S(1)}, s32[2]{0:T(128)S(1)}, bf16[3,384,3456]{2,1,0:T(8,128)(2,1)S(1)}, f3...) custom-call(s32[2]{0:T(128)S(1)} %get-tuple-element.136.place_ref, ...), custom_call_target="tpu_custom_call", output_to_operand_aliasing={{3}: (1, {}), {4}: (2, {}), {5}: (3, {})} | custom-call | flops 2038431744 | tf_op jit(solution)/shard_map/pallas_call | solution.py:166
  93.3 1.2 shard_map.75
  94.5 6.4 %collective-permute-start.18 = (bf16[384,512]{1,0:T(8,128)(2,1)S(1)}, bf16[384,512]{1,0:T(8,128)(2,1)S(1)}, u32[]{:S(2)}, u32[]{:S(2)}) collective-permute-start(bf16[384,512]{1,0:T(8,128)(2,1)S(1)} %get-tuple-element.158), channel_id=1, source_target_pairs={{0,8},{1,9},{2,10},{3,11},{4,12},{5,13},{6,14},{7,15},{8,0},{9,1},... | collective-permute-start | bytes 1179656 | tf_op jit(solution)/shard_map/ppermute | solution.py:205
  100.9 1.3 collective-permute-done.18.refs_0_
  102.3 6.3 %shard_map.76 = (bf16[384,256]{1,0:T(8,128)(2,1)S(1)}, bf16[384,512]{1,0:T(8,128)(2,1)S(1)}, s32[2]{0:T(128)S(1)}, bf16[3,384,3456]{2,1,0:T(8,128)(2,1)S(1)}, f3...) custom-call(s32[2]{0:T(128)S(1)} %get-tuple-element.152.place_ref, ...), custom_call_target="tpu_custom_call", output_to_operand_aliasing={{3}: (1, {}), {4}: (2, {}), {5}: (3, {})} | custom-call | flops 2038431744 | tf_op jit(solution)/shard_map/pallas_call | solution.py:166
  110.7 1.2 shard_map.77
  111.9 6.3 %collective-permute-start.22 = (bf16[384,512]{1,0:T(8,128)(2,1)S(1)}, bf16[384,512]{1,0:T(8,128)(2,1)S(1)}, u32[]{:S(2)}, u32[]{:S(2)}) collective-permute-start(bf16[384,512]{1,0:T(8,128)(2,1)S(1)} %get-tuple-element.174), channel_id=1, source_target_pairs={{0,8},{1,9},{2,10},{3,11},{4,12},{5,13},{6,14},{7,15},{8,0},{9,1},... | collective-permute-start | bytes 1179656 | tf_op jit(solution)/shard_map/ppermute | solution.py:205
  118.2 1.3 collective-permute-start.23
  119.5 1.3 collective-permute-start.24
  120.8 1.3 collective-permute-done.23.refs_5_
  122.1 6.3 %shard_map.78 = (bf16[384,256]{1,0:T(8,128)(2,1)S(1)}, bf16[384,512]{1,0:T(8,128)(2,1)S(1)}, s32[2]{0:T(128)S(1)}, bf16[3,384,3456]{2,1,0:T(8,128)(2,1)S(1)}, f3...) custom-call(s32[2]{0:T(128)S(1)} %get-tuple-element.168.place_ref, ...), custom_call_target="tpu_custom_call", output_to_operand_aliasing={{3}: (1, {}), {4}: (2, {}), {5}: (3, {})} | custom-call | flops 2038431744 | tf_op jit(solution)/shard_map/pallas_call | solution.py:166
  128.4 1.2 shard_map.79
  130.7 1.9 %collective-permute-start.26 = (bf16[384,256]{1,0:T(8,128)(2,1)S(1)}, bf16[384,256]{1,0:T(8,128)(2,1)S(1)}, u32[]{:S(2)}, u32[]{:S(2)}) collective-permute-start(bf16[384,256]{1,0:T(8,128)(2,1)S(1)} %get-tuple-element.190), channel_id=1, source_target_pairs={{24,16},{25,17},{26,18},{27,19},{28,20},{29,21},{30,22},{31,23}} | collective-permute-start | bytes 589832 | tf_op jit(solution)/shard_map/ppermute | solution.py:205
  133.7 6.2 %shard_map.80 = (bf16[384,256]{1,0:T(8,128)(2,1)S(1)}, bf16[384,512]{1,0:T(8,128)(2,1)S(1)}, s32[2]{0:T(128)}, bf16[3,384,3456]{2,1,0:T(8,128)(2,1)S(1)}, f32[384,1]{1,0:T(8,128)S(1)}, /*index=5*/f32[384,1]{1,0:T(8,128)S(1)}) custom-call(s32[2]{0:T(128)S(1)} %get-tuple-element.184.place_ref, ...), custom_call_target="tpu_custom_call", output_to_operand_aliasing={{3}: (1, {}), {4}: (2, {}), {5}: (3, {})} | custom-call | flops 2038431744 | tf_op jit(solution)/shard_map/pallas_call | solution.py:166
  (56 shorter events, 23.3 us)
Async XLA Ops:
  2.8 19.9 %collective-permute-start.1 = (bf16[2,384,256]{2,1,0:T(8,128)(2,1)S(1)}, bf16[2,384,256]{2,1,0:T(8,128)(2,1)S(1)}, u32[]{:S(2)}, u32[]{:S(2)}) collective-permute-start(bf16[2,384,256]{2,1,0:T(8,128)(2,1)S(1)} %copy.70.first_ref.refs_0_.refs_1_), channel_id=1, source_target_pairs={{1,0},{2,1},{3,2},{4,3},{5,4},{6,5},{7,6},{17,16},{18,17},{19,18},... | collective-permute-start | bytes 1179656 | tf_op jit(solution)/shard_map/ppermute | solution.py:205
  9.2 13.5 %collective-permute-start = (bf16[2,384,256]{2,1,0:T(8,128)(2,1)S(1)}, bf16[2,384,256]{2,1,0:T(8,128)(2,1)S(1)}, u32[]{:S(2)}, u32[]{:S(2)}) collective-permute-start(bf16[2,384,256]{2,1,0:T(8,128)(2,1)S(1)} %get-tuple-element.104), channel_id=1, source_target_pairs={{0,1},{1,2},{2,3},{3,4},{4,5},{5,6},{6,7},{16,17},{17,18},{18,19},... | collective-permute-start | bytes 1179656 | tf_op jit(solution)/shard_map/ppermute | solution.py:205
  9.9 6.3 %collective-permute-start.2 = (bf16[1,384,128]{2,1,0:T(8,128)(2,1)S(1)}, bf16[1,384,128]{2,1,0:T(8,128)(2,1)S(1)}, u32[]{:S(2)}, u32[]{:S(2)}) collective-permute-start(bf16[1,384,128]{2,1,0:T(8,128)(2,1)S(1)} %get-tuple-element.105), channel_id=1, source_target_pairs={{8,9},{9,10},{10,11},{11,12},{12,13},{13,14},{14,15},{24,25},{25,2... | collective-permute-start | bytes 294920 | tf_op jit(solution)/shard_map/ppermute | solution.py:205
  13.0 9.7 %collective-permute-start.3 = (bf16[1,384,128]{2,1,0:T(8,128)(2,1)S(1)}, bf16[1,384,128]{2,1,0:T(8,128)(2,1)S(1)}, u32[]{:S(2)}, u32[]{:S(2)}) collective-permute-start(bf16[1,384,128]{2,1,0:T(8,128)(2,1)S(1)} %get-tuple-element.106), channel_id=1, source_target_pairs={{9,8},{10,9},{11,10},{12,11},{13,12},{14,13},{15,14},{25,24},{26,2... | collective-permute-start | bytes 294920 | tf_op jit(solution)/shard_map/ppermute | solution.py:205
  24.5 2.0 %collective-permute-start.5 = (bf16[3,384,256]{2,1,0:T(8,128)(2,1)S(1)}, bf16[3,384,256]{2,1,0:T(8,128)(2,1)S(1)}, u32[]{:S(2)}, u32[]{:S(2)}) collective-permute-start(bf16[3,384,256]{2,1,0:T(8,128)(2,1)S(1)} %get-tuple-element.119.refs_4_), channel_id=1, source_target_pairs={{1,0},{2,1},{3,2},{4,3},{5,4},{6,5},{7,6}} | collective-permute-start | bytes 1769480 | tf_op jit(solution)/shard_map/ppermute | solution.py:205
  25.8 4.0 %collective-permute-start.6 = (bf16[3,384,256]{2,1,0:T(8,128)(2,1)S(1)}, bf16[3,384,256]{2,1,0:T(8,128)(2,1)S(1)}, u32[]{:S(2)}, u32[]{:S(2)}) collective-permute-start(bf16[3,384,256]{2,1,0:T(8,128)(2,1)S(1)} %get-tuple-element.119.refs_4_), channel_id=1, source_target_pairs={{0,1},{1,2},{2,3},{3,4},{4,5},{5,6},{6,7}} | collective-permute-start | bytes 1769480 | tf_op jit(solution)/shard_map/ppermute | solution.py:205
  27.7 3.3 %collective-permute-start.9 = (bf16[384,256]{1,0:T(8,128)(2,1)S(1)}, bf16[384,256]{1,0:T(8,128)(2,1)S(1)}, u32[]{:S(2)}, u32[]{:S(2)}) collective-permute-start(bf16[384,256]{1,0:T(8,128)(2,1)S(1)} %get-tuple-element.125), channel_id=1, source_target_pairs={{9,16},{10,17},{11,18},{12,19},{13,20},{14,21},{15,22}} | collective-permute-start | bytes 589832 | tf_op jit(solution)/shard_map/ppermute | solution.py:205
  28.4 2.6 %collective-permute-start.8 = (bf16[384,256]{1,0:T(8,128)(2,1)S(1)}, bf16[384,256]{1,0:T(8,128)(2,1)S(1)}, u32[]{:S(2)}, u32[]{:S(2)}) collective-permute-start(bf16[384,256]{1,0:T(8,128)(2,1)S(1)} %get-tuple-element.125), channel_id=1, source_target_pairs={{8,17},{9,18},{10,19},{11,20},{12,21},{13,22},{14,23}} | collective-permute-start | bytes 589832 | tf_op jit(solution)/shard_map/ppermute | solution.py:205
  31.0 24.1 %collective-permute-start.10 = (bf16[384,512]{1,0:T(8,128)(2,1)S(1)}, bf16[384,512]{1,0:T(8,128)(2,1)S(1)}, u32[]{:S(2)}, u32[]{:S(2)}) collective-permute-start(bf16[384,512]{1,0:T(8,128)(2,1)S(1)} %get-tuple-element.126), channel_id=1, source_target_pairs={{0,8},{1,9},{2,10},{3,11},{4,12},{5,13},{6,14},{7,15},{8,0},{9,1},... | collective-permute-start | bytes 1179656 | tf_op jit(solution)/shard_map/ppermute | solution.py:205
  56.4 3.3 %collective-permute-start.13 = (bf16[384,256]{1,0:T(8,128)(2,1)S(1)}, bf16[384,256]{1,0:T(8,128)(2,1)S(1)}, u32[]{:S(2)}, u32[]{:S(2)}) collective-permute-start(bf16[384,256]{1,0:T(8,128)(2,1)S(1)} %get-tuple-element.141), channel_id=1, source_target_pairs={{9,16},{10,17},{11,18},{12,19},{13,20},{14,21},{15,22}} | collective-permute-start | bytes 589832 | tf_op jit(solution)/shard_map/ppermute | solution.py:205
  57.0 2.6 %collective-permute-start.12 = (bf16[384,256]{1,0:T(8,128)(2,1)S(1)}, bf16[384,256]{1,0:T(8,128)(2,1)S(1)}, u32[]{:S(2)}, u32[]{:S(2)}) collective-permute-start(bf16[384,256]{1,0:T(8,128)(2,1)S(1)} %get-tuple-element.141), channel_id=1, source_target_pairs={{8,17},{9,18},{10,19},{11,20},{12,21},{13,22},{14,23}} | collective-permute-start | bytes 589832 | tf_op jit(solution)/shard_map/ppermute | solution.py:205
  57.7 1.9 %collective-permute-start.11 = (bf16[384,256]{1,0:T(8,128)(2,1)S(1)}, bf16[384,256]{1,0:T(8,128)(2,1)S(1)}, u32[]{:S(2)}, u32[]{:S(2)}) collective-permute-start(bf16[384,256]{1,0:T(8,128)(2,1)S(1)} %get-tuple-element.141), channel_id=1, source_target_pairs={{8,16},{9,17},{10,18},{11,19},{12,20},{13,21},{14,22},{15,23}} | collective-permute-start | bytes 589832 | tf_op jit(solution)/shard_map/ppermute | solution.py:205
  59.7 25.2 %collective-permute-start.14 = (bf16[384,512]{1,0:T(8,128)(2,1)S(1)}, bf16[384,512]{1,0:T(8,128)(2,1)S(1)}, u32[]{:S(2)}, u32[]{:S(2)}) collective-permute-start(bf16[384,512]{1,0:T(8,128)(2,1)S(1)} %get-tuple-element.142), channel_id=1, source_target_pairs={{0,8},{1,9},{2,10},{3,11},{4,12},{5,13},{6,14},{7,15},{8,0},{9,1},... | collective-permute-start | bytes 1179656 | tf_op jit(solution)/shard_map/ppermute | solution.py:205
  91.2 3.3 %collective-permute-start.17 = (bf16[384,256]{1,0:T(8,128)(2,1)S(1)}, bf16[384,256]{1,0:T(8,128)(2,1)S(1)}, u32[]{:S(2)}, u32[]{:S(2)}) collective-permute-start(bf16[384,256]{1,0:T(8,128)(2,1)S(1)} %get-tuple-element.157), channel_id=1, source_target_pairs={{9,16},{10,17},{11,18},{12,19},{13,20},{14,21},{15,22}} | collective-permute-start | bytes 589832 | tf_op jit(solution)/shard_map/ppermute | solution.py:205
  91.9 2.6 %collective-permute-start.16 = (bf16[384,256]{1,0:T(8,128)(2,1)S(1)}, bf16[384,256]{1,0:T(8,128)(2,1)S(1)}, u32[]{:S(2)}, u32[]{:S(2)}) collective-permute-start(bf16[384,256]{1,0:T(8,128)(2,1)S(1)} %get-tuple-element.157), channel_id=1, source_target_pairs={{8,17},{9,18},{10,19},{11,20},{12,21},{13,22},{14,23}} | collective-permute-start | bytes 589832 | tf_op jit(solution)/shard_map/ppermute | solution.py:205
  92.6 1.9 %collective-permute-start.15 = (bf16[384,256]{1,0:T(8,128)(2,1)S(1)}, bf16[384,256]{1,0:T(8,128)(2,1)S(1)}, u32[]{:S(2)}, u32[]{:S(2)}) collective-permute-start(bf16[384,256]{1,0:T(8,128)(2,1)S(1)} %get-tuple-element.157), channel_id=1, source_target_pairs={{8,16},{9,17},{10,18},{11,19},{12,20},{13,21},{14,22},{15,23}} | collective-permute-start | bytes 589832 | tf_op jit(solution)/shard_map/ppermute | solution.py:205
  94.5 7.7 %collective-permute-start.18 = (bf16[384,512]{1,0:T(8,128)(2,1)S(1)}, bf16[384,512]{1,0:T(8,128)(2,1)S(1)}, u32[]{:S(2)}, u32[]{:S(2)}) collective-permute-start(bf16[384,512]{1,0:T(8,128)(2,1)S(1)} %get-tuple-element.158), channel_id=1, source_target_pairs={{0,8},{1,9},{2,10},{3,11},{4,12},{5,13},{6,14},{7,15},{8,0},{9,1},... | collective-permute-start | bytes 1179656 | tf_op jit(solution)/shard_map/ppermute | solution.py:205
  108.6 3.3 %collective-permute-start.21 = (bf16[384,256]{1,0:T(8,128)(2,1)S(1)}, bf16[384,256]{1,0:T(8,128)(2,1)S(1)}, u32[]{:S(2)}, u32[]{:S(2)}) collective-permute-start(bf16[384,256]{1,0:T(8,128)(2,1)S(1)} %get-tuple-element.173), channel_id=1, source_target_pairs={{9,16},{10,17},{11,18},{12,19},{13,20},{14,21},{15,22}} | collective-permute-start | bytes 589832 | tf_op jit(solution)/shard_map/ppermute | solution.py:205
  109.3 2.6 %collective-permute-start.20 = (bf16[384,256]{1,0:T(8,128)(2,1)S(1)}, bf16[384,256]{1,0:T(8,128)(2,1)S(1)}, u32[]{:S(2)}, u32[]{:S(2)}) collective-permute-start(bf16[384,256]{1,0:T(8,128)(2,1)S(1)} %get-tuple-element.173), channel_id=1, source_target_pairs={{8,17},{9,18},{10,19},{11,20},{12,21},{13,22},{14,23}} | collective-permute-start | bytes 589832 | tf_op jit(solution)/shard_map/ppermute | solution.py:205
  111.9 10.2 %collective-permute-start.22 = (bf16[384,512]{1,0:T(8,128)(2,1)S(1)}, bf16[384,512]{1,0:T(8,128)(2,1)S(1)}, u32[]{:S(2)}, u32[]{:S(2)}) collective-permute-start(bf16[384,512]{1,0:T(8,128)(2,1)S(1)} %get-tuple-element.174), channel_id=1, source_target_pairs={{0,8},{1,9},{2,10},{3,11},{4,12},{5,13},{6,14},{7,15},{8,0},{9,1},... | collective-permute-start | bytes 1179656 | tf_op jit(solution)/shard_map/ppermute | solution.py:205
  118.2 3.9 %collective-permute-start.23 = (bf16[384,256]{1,0:T(8,128)(2,1)S(1)}, bf16[384,256]{1,0:T(8,128)(2,1)S(1)}, u32[]{:S(2)}, u32[]{:S(2)}) collective-permute-start(bf16[384,256]{1,0:T(8,128)(2,1)S(1)} %get-tuple-element.157), channel_id=1, source_target_pairs={{24,0},{25,1},{26,2},{27,3},{28,4},{29,5},{30,6},{31,7}} | collective-permute-start | bytes 589832 | tf_op jit(solution)/shard_map/ppermute | solution.py:205
  119.5 8.9 %collective-permute-start.24 = (bf16[384,256]{1,0:T(8,128)(2,1)S(1)}, bf16[384,256]{1,0:T(8,128)(2,1)S(1)}, u32[]{:S(2)}, u32[]{:S(2)}) collective-permute-start(bf16[384,256]{1,0:T(8,128)(2,1)S(1)} %get-tuple-element.173), channel_id=1, source_target_pairs={{24,8},{25,9},{26,10},{27,11},{28,12},{29,13},{30,14},{31,15}} | collective-permute-start | bytes 589832 | tf_op jit(solution)/shard_map/ppermute | solution.py:205
  129.6 4.1 %collective-permute-start.25 = (bf16[384,512]{1,0:T(8,128)(2,1)S(1)}, bf16[384,512]{1,0:T(8,128)(2,1)S(1)}, u32[]{:S(2)}, u32[]{:S(2)}) collective-permute-start(bf16[384,512]{1,0:T(8,128)(2,1)S(1)} %get-tuple-element.188), channel_id=1, source_target_pairs={{0,8},{1,9},{2,10},{3,11},{4,12},{5,13},{6,14},{7,15},{8,0},{9,1},... | collective-permute-start | bytes 1179656 | tf_op jit(solution)/shard_map/ppermute | solution.py:205
  130.7 3.0 %collective-permute-start.26 = (bf16[384,256]{1,0:T(8,128)(2,1)S(1)}, bf16[384,256]{1,0:T(8,128)(2,1)S(1)}, u32[]{:S(2)}, u32[]{:S(2)}) collective-permute-start(bf16[384,256]{1,0:T(8,128)(2,1)S(1)} %get-tuple-element.190), channel_id=1, source_target_pairs={{24,16},{25,17},{26,18},{27,19},{28,20},{29,21},{30,22},{31,23}} | collective-permute-start | bytes 589832 | tf_op jit(solution)/shard_map/ppermute | solution.py:205
  (3 other events, 5.7 us)

commit v3 on v2

--- a/solution.py
+++ b/solution.py
@@ -64,14 +64,13 @@
 
 def layer_kernel(cases, rows_in, own, cols, block, height, n_in, place_ref, w_ref, bias_ref, gain_ref, *refs):
     ins = refs[:n_in]
-    out_ref, acts_ref, next_ref = refs[n_in:n_in + 3]
-    xs, buf, total, sems = refs[n_in + 6:]
+    out_ref, acts_ref = refs[n_in:n_in + 2]
+    xs, buf, total, sems = refs[n_in + 5:]
     channels = xs.shape[0]
     row = block * cols
     rows_out = rows_in - 2
     lanes_in, lanes_out = rows_in * row, rows_out * row
     segment, slab = place_ref[0], place_ref[1]
-    next_ref[0], next_ref[1] = segment, slab
 
     def slot(a, c):
         return (3 * a + c) * channels
@@ -145,8 +144,8 @@
         def taps(n, _):
             at = pl.multiple_of(n * step, step)
             part = xs[:, pl.ds(at + row, step)].astype(F32) + bias_ref[...]
-            part = lax.fori_loop(0, 3, lambda b, part: part + jnp.dot(
-                w_ref[b], buf[:, pl.ds(pl.multiple_of(at + b * row, row), step)], preferred_element_type=F32), part)
+            for b in range(3):
+                part = part + jnp.dot(w_ref[b], buf[:, pl.ds(at + b * row, step)], preferred_element_type=F32)
             line = top + 2 * n + lax.broadcasted_iota(jnp.int32, (1, step), 1) // row
             total[:, pl.ds(at, step)] = jnp.where(
                 jnp.logical_and(line >= 0, line < height), part, 0.0).astype(BF16)
@@ -159,8 +158,8 @@
         out_done.wait()
 
 
-def layer_call(cases, rows_in, own, cols, block, height, fixed, ins):
-    place, weight, bias, gain = fixed
+def layer_call(cases, rows_in, own, cols, block, height, place, fixed, ins):
+    weight, bias, gain = fixed
     channels = weight.shape[1]
     row = block * cols
     return pl.pallas_call(
@@ -168,14 +167,13 @@
         out_shape=(
             jax.ShapeDtypeStruct((channels, (rows_in - 2) * row), BF16),
             jax.ShapeDtypeStruct((channels, rows_in * row), BF16),
-            jax.ShapeDtypeStruct(place.shape, place.dtype),
             jax.ShapeDtypeStruct(weight.shape, weight.dtype),
             jax.ShapeDtypeStruct(bias.shape, bias.dtype),
             jax.ShapeDtypeStruct(gain.shape, gain.dtype),
         ),
         in_specs=[SMEM, VMEM, VMEM, VMEM] + [ANY] * len(ins),
-        out_specs=(ANY, ANY, SMEM, VMEM, VMEM, VMEM),
-        input_output_aliases={1: 3, 2: 4, 3: 5},
+        out_specs=(ANY, ANY, VMEM, VMEM, VMEM),
+        input_output_aliases={1: 2, 2: 3, 3: 4},
         scratch_shapes=[
             pltpu.VMEM((channels, rows_in * row), BF16),
             pltpu.VMEM((9 * channels, rows_in * row), BF16),
@@ -211,17 +209,18 @@
 
     first = lanes(jnp.concatenate([cache_in[0], video_in[:block]], axis=0))
     first_below = moved(first[..., :2 * row], [(g, g) for g in evens], -1)
+    first_above = moved(first[..., (own - 2) * row:], [(g, g) for g in evens], 1)
     place, weight = lax.optimization_barrier((place, conv_weight[0]))
-    cuts = ((2, (own - 2) * row, 2 * row), (1, (own - 1) * row, row), (1, 0, row))
-    weight, bias, gain, later, above, odd_last, odd_first = turned_weights(
+    cuts = ((1, (own - 1) * row, row), (1, 0, row))
+    weight, bias, gain, later, odd_last, odd_first = turned_weights(
         weight, conv_bias, norm_gain, lanes(video_in[block:]), first, cuts)
-    first_above = moved(above, [(g, g) for g in evens], 1)
     odd_above = moved(odd_last, [(g, g) for g in odds], 1)
     odd_below = moved(odd_first, [(g, g) for g in odds], -1)
     later_below = moved(later[..., :2 * row], [(0, 0)], -1)
-    fixed = (place, weight, bias, gain)
-
-    call = functools.partial(layer_call, own=own, cols=cols, block=block, height=height)
+    later_above = moved(later[..., (own - 2) * row:], [(0, 0)], 1)
+    fixed = (weight, bias, gain)
+
+    call = functools.partial(layer_call, own=own, cols=cols, block=block, height=height, place=place)
     across = [(g, g ^ 1) for g in range(segments)]
     hop = [(g, g + 1) for g in odds if g + 1 < segments]
     planes = segments // 2
@@ -258,16 +257,13 @@
         if 0 < tick <= blocks:
             out, *arrived[tick - 1] = lax.optimization_barrier((out, *arrived[tick - 1]))
         crossed = moved(out, across, 0)
-        if tick == 0:
-            crossed, sent = lax.optimization_barrier((crossed, later[..., (own - 2) * row:]))
-            later_above = moved(sent, [(0, 0)], 1)
 
         ins = [crossed, first, odd_above, odd_below]
         old = [(2, 0, 0, 1), (1, 0, 0, own), (3, 0, 0, 1)]
         if tick:
             ins.append(odd_acts)
         if tick == 0:
-            ins.append(later_below)
+            ins += [later_above, later_below]
         if tick >= ticks - 2:
             ins.append(done[0] if tick < ticks - 1 else done[-1])
         cases = [(2 * p + 1, [(0, None, 0, own + 2)], old if tick == LAG * p else [(4, None, 0, own + 2)]) for p in busy]

time: 144 us -> 118 us (0.82)
  starting transfers between devices: 82.3 us -> 71.2 us
  Pallas kernels: 39.2 us -> 30.4 us
  waiting for transfers between devices: 13.7 us -> 9.03 us
    ppermute x27, starting transfers between devices: 82.3 us -> 71.2 us  [moved(): lax.ppermute(value, axes, [(a * slabs + s, b * slabs + s + step) for a, b...]
    pallas_call x12, Pallas kernels: 35 us -> 26.2 us  [layer_call(): pl.pallas_call(functools.partial(layer_kernel, cases, rows_in, own, cols,...]
    ppermute x27, waiting for transfers between devices: 13.7 us -> 9.03 us  [moved(): lax.ppermute(value, axes, [(a * slabs + s, b * slabs + s + step) for a, b...]
  transfers between devices with their start and end apart: 27 -> 27, of which waited for: 8 -> 8; matrix products, arithmetic and copies ran while one was open for 1% -> 1% of each run, Pallas kernels for 12% -> 11%
where the time goes in v3:
time: 118 us; the launch traced here: 117 us
  starting transfers between devices  71.2 us (60%)
  Pallas kernels  30.4 us (26%)
  waiting for transfers between devices  9.03 us (8%)
  local copies, waits for them, and re-layouts  4.33 us (4%)
    ppermute x27, starting transfers between devices, moved(): lax.ppermute(value, axes, [(a * slabs + s, b * slabs + s + step) for a, b...  71.2 us
    pallas_call x12, Pallas kernels, layer_call(): pl.pallas_call(functools.partial(layer_kernel, cases, rows_in, own, cols,...  26.2 us
    ppermute x27, waiting for transfers between devices, moved(): lax.ppermute(value, axes, [(a * slabs + s, b * slabs + s + step) for a, b...  9.03 us
    pallas_call x1, Pallas kernels, turned_weights(): pl.pallas_call(functools.partial(turn_kernel, cuts), out_shape=(jax.Shape...  4.16 us
  transfers between devices with their start and end apart: 27, of which 8 were waited for; matrix products, arithmetic and copies ran while one was open for 1% of the time, Pallas kernels for 11%

profile of v3, /device:TPU:13, one launch (start us, length us, event | category | flops | bytes accessed | tf_op | source)
XLA Modules:
  0.0 117.1 jit_solution(16272131105181005573)
XLA Ops:
  0.6 0.9 slice.19
  1.6 1.0 pad_maximum_fusion
  4.2 1.1 slice.18
  5.7 4.2 %shard_map.68 = (bf16[3,384,3456]{2,1,0:T(8,128)(2,1)S(1)}, f32[384,1]{1,0:T(8,128)S(1)}, f32[384,1]{1,0:T(8,128)S(1)}, bf16[3,384,256]{2,1,0:T(8,128)(2,1)S(1)}...) custom-call(bf16[3,3,3,384,384]{4,3,2,1,0:T(8,128)(2,1)} %bitcast.20, ...), custom_call_target="tpu_custom_call", output_to_operand_aliasing={{3}: (3, {})} | custom-call | bytes 15925248 | tf_op jit(solution)/shard_map/pallas_call | solution.py:42
  9.9 3.1 %collective-permute-start.2 = (bf16[1,384,128]{2,1,0:T(8,128)(2,1)S(1)}, bf16[1,384,128]{2,1,0:T(8,128)(2,1)S(1)}, u32[]{:S(2)}, u32[]{:S(2)}) collective-permute-start(bf16[1,384,128]{2,1,0:T(8,128)(2,1)S(1)} %get-tuple-element.90), channel_id=1, source_target_pairs={{8,9},{9,10},{10,11},{11,12},{12,13},{13,14},{14,15},{24,25},{25,2... | collective-permute-start | bytes 294920 | tf_op jit(solution)/shard_map/ppermute | solution.py:203
  13.0 3.1 %collective-permute-start.3 = (bf16[1,384,128]{2,1,0:T(8,128)(2,1)S(1)}, bf16[1,384,128]{2,1,0:T(8,128)(2,1)S(1)}, u32[]{:S(2)}, u32[]{:S(2)}) collective-permute-start(bf16[1,384,128]{2,1,0:T(8,128)(2,1)S(1)} %get-tuple-element.91), channel_id=1, source_target_pairs={{9,8},{10,9},{11,10},{12,11},{13,12},{14,13},{15,14},{25,24},{26,2... | collective-permute-start | bytes 294920 | tf_op jit(solution)/shard_map/ppermute | solution.py:203
  20.1 1.3 %collective-permute-done.4.refs_0_ = bf16[384,512]{1,0:T(8,128)(2,1)S(1)} collective-permute-done((bf16[384,512]{1,0:T(8,128)(2,1)S(1)}, bf16[384,512]{1,0:T(8,128)(2,1)S(1)}, u32[]{:S(2)}, u32[]{:S(2)}) %collective-permute-start.4) | collective-permute-done | bytes 393248 | tf_op jit(solution)/shard_map/ppermute | solution.py:203
  24.8 24.1 %collective-permute-start.10 = (bf16[384,512]{1,0:T(8,128)(2,1)S(1)}, bf16[384,512]{1,0:T(8,128)(2,1)S(1)}, u32[]{:S(2)}, u32[]{:S(2)}) collective-permute-start(bf16[384,512]{1,0:T(8,128)(2,1)S(1)} %get-tuple-element.106), channel_id=1, source_target_pairs={{0,8},{1,9},{2,10},{3,11},{4,12},{5,13},{6,14},{7,15},{8,0},{9,1},... | collective-permute-start | bytes 1179656 | tf_op jit(solution)/shard_map/ppermute | solution.py:203
  48.9 1.3 %collective-permute-done.10.refs_0_ = bf16[384,512]{1,0:T(8,128)(2,1)S(1)} collective-permute-done((bf16[384,512]{1,0:T(8,128)(2,1)S(1)}, bf16[384,512]{1,0:T(8,128)(2,1)S(1)}, u32[]{:S(2)}, u32[]{:S(2)}) %collective-permute-start.10) | collective-permute-done | bytes 393248 | tf_op jit(solution)/shard_map/ppermute | solution.py:203
  50.2 0.8 shard_map.72
  53.7 10.4 %collective-permute-start.14 = (bf16[384,512]{1,0:T(8,128)(2,1)S(1)}, bf16[384,512]{1,0:T(8,128)(2,1)S(1)}, u32[]{:S(2)}, u32[]{:S(2)}) collective-permute-start(bf16[384,512]{1,0:T(8,128)(2,1)S(1)} %get-tuple-element.120), channel_id=1, source_target_pairs={{0,8},{1,9},{2,10},{3,11},{4,12},{5,13},{6,14},{7,15},{8,0},{9,1},... | collective-permute-start | bytes 1179656 | tf_op jit(solution)/shard_map/ppermute | solution.py:203
  64.2 1.3 %collective-permute-done.14.refs_0_ = bf16[384,512]{1,0:T(8,128)(2,1)S(1)} collective-permute-done((bf16[384,512]{1,0:T(8,128)(2,1)S(1)}, bf16[384,512]{1,0:T(8,128)(2,1)S(1)}, u32[]{:S(2)}, u32[]{:S(2)}) %collective-permute-start.14) | collective-permute-done | bytes 393248 | tf_op jit(solution)/shard_map/ppermute | solution.py:203
  65.5 5.1 %shard_map.74 = (bf16[384,256]{1,0:T(8,128)(2,1)S(1)}, bf16[384,512]{1,0:T(8,128)(2,1)S(1)}, bf16[3,384,3456]{2,1,0:T(8,128)(2,1)S(1)}, f32[384,1]{1,0:T(8,128)S(1)}, f32[384,1]{1,0:T(8,128)S(1)}) custom-call(s32[2]{0:T(128)S(1)} %pad_add_fusion.place_ref, ...), custom_call_target="tpu_custom_call", output_to_operand_aliasing={{2}: (1, {}), {3}: (2, {}), {4}: (3, {})} | custom-call | flops 2038431744 | tf_op jit(solution)/shard_map/pallas_call | solution.py:165
  73.3 7.5 %collective-permute-start.18 = (bf16[384,512]{1,0:T(8,128)(2,1)S(1)}, bf16[384,512]{1,0:T(8,128)(2,1)S(1)}, u32[]{:S(2)}, u32[]{:S(2)}) collective-permute-start(bf16[384,512]{1,0:T(8,128)(2,1)S(1)} %get-tuple-element.134), channel_id=1, source_target_pairs={{0,8},{1,9},{2,10},{3,11},{4,12},{5,13},{6,14},{7,15},{8,0},{9,1},... | collective-permute-start | bytes 1179656 | tf_op jit(solution)/shard_map/ppermute | solution.py:203
  80.8 1.3 %collective-permute-done.18.refs_0_ = bf16[384,512]{1,0:T(8,128)(2,1)S(1)} collective-permute-done((bf16[384,512]{1,0:T(8,128)(2,1)S(1)}, bf16[384,512]{1,0:T(8,128)(2,1)S(1)}, u32[]{:S(2)}, u32[]{:S(2)}) %collective-permute-start.18) | collective-permute-done | bytes 393248 | tf_op jit(solution)/shard_map/ppermute | solution.py:203
  82.2 5.5 %shard_map.76 = (bf16[384,256]{1,0:T(8,128)(2,1)S(1)}, bf16[384,512]{1,0:T(8,128)(2,1)S(1)}, bf16[3,384,3456]{2,1,0:T(8,128)(2,1)S(1)}, f32[384,1]{1,0:T(8,128)S(1)}, f32[384,1]{1,0:T(8,128)S(1)}) custom-call(s32[2]{0:T(128)S(1)} %pad_add_fusion.place_ref, ...), custom_call_target="tpu_custom_call", output_to_operand_aliasing={{2}: (1, {}), {3}: (2, {}), {4}: (3, {})} | custom-call | flops 2038431744 | tf_op jit(solution)/shard_map/pallas_call | solution.py:165
  90.3 6.3 %collective-permute-start.22 = (bf16[384,512]{1,0:T(8,128)(2,1)S(1)}, bf16[384,512]{1,0:T(8,128)(2,1)S(1)}, u32[]{:S(2)}, u32[]{:S(2)}) collective-permute-start(bf16[384,512]{1,0:T(8,128)(2,1)S(1)} %get-tuple-element.148), channel_id=1, source_target_pairs={{0,8},{1,9},{2,10},{3,11},{4,12},{5,13},{6,14},{7,15},{8,0},{9,1},... | collective-permute-start | bytes 1179656 | tf_op jit(solution)/shard_map/ppermute | solution.py:203
  96.7 1.3 %collective-permute-start.23 = (bf16[384,256]{1,0:T(8,128)(2,1)S(1)}, bf16[384,256]{1,0:T(8,128)(2,1)S(1)}, u32[]{:S(2)}, u32[]{:S(2)}) collective-permute-start(bf16[384,256]{1,0:T(8,128)(2,1)S(1)} %get-tuple-element.133), channel_id=1, source_target_pairs={{24,0},{25,1},{26,2},{27,3},{28,4},{29,5},{30,6},{31,7}} | collective-permute-start | bytes 589832 | tf_op jit(solution)/shard_map/ppermute | solution.py:203
  98.0 1.3 %collective-permute-start.24 = (bf16[384,256]{1,0:T(8,128)(2,1)S(1)}, bf16[384,256]{1,0:T(8,128)(2,1)S(1)}, u32[]{:S(2)}, u32[]{:S(2)}) collective-permute-start(bf16[384,256]{1,0:T(8,128)(2,1)S(1)} %get-tuple-element.147), channel_id=1, source_target_pairs={{24,8},{25,9},{26,10},{27,11},{28,12},{29,13},{30,14},{31,15}} | collective-permute-start | bytes 589832 | tf_op jit(solution)/shard_map/ppermute | solution.py:203
  99.3 1.3 %collective-permute-done.23.refs_5_ = bf16[384,256]{1,0:T(8,128)(2,1)S(1)} collective-permute-done((bf16[384,256]{1,0:T(8,128)(2,1)S(1)}, bf16[384,256]{1,0:T(8,128)(2,1)S(1)}, u32[]{:S(2)}, u32[]{:S(2)}) %collective-permute-start.23) | collective-permute-done | bytes 196640 | tf_op jit(solution)/shard_map/ppermute | solution.py:203
  100.6 5.2 %shard_map.78 = (bf16[384,256]{1,0:T(8,128)(2,1)S(1)}, bf16[384,512]{1,0:T(8,128)(2,1)S(1)}, bf16[3,384,3456]{2,1,0:T(8,128)(2,1)S(1)}, f32[384,1]{1,0:T(8,128)S(1)}, f32[384,1]{1,0:T(8,128)S(1)}) custom-call(s32[2]{0:T(128)S(1)} %pad_add_fusion.place_ref, ...), custom_call_target="tpu_custom_call", output_to_operand_aliasing={{2}: (1, {}), {3}: (2, {}), {4}: (3, {})} | custom-call | flops 2038431744 | tf_op jit(solution)/shard_map/pallas_call | solution.py:165
  107.1 1.9 %collective-permute-start.26 = (bf16[384,256]{1,0:T(8,128)(2,1)S(1)}, bf16[384,256]{1,0:T(8,128)(2,1)S(1)}, u32[]{:S(2)}, u32[]{:S(2)}) collective-permute-start(bf16[384,256]{1,0:T(8,128)(2,1)S(1)} %get-tuple-element.162), channel_id=1, source_target_pairs={{24,16},{25,17},{26,18},{27,19},{28,20},{29,21},{30,22},{31,23}} | collective-permute-start | bytes 589832 | tf_op jit(solution)/shard_map/ppermute | solution.py:203
  109.0 1.0 collective-permute-done.26.refs_5_
  110.0 5.2 %shard_map.80 = (bf16[384,256]{1,0:T(8,128)(2,1)S(1)}, bf16[384,512]{1,0:T(8,128)(2,1)S(1)}, bf16[3,384,3456]{2,1,0:T(8,128)(2,1)S(1)}, f32[384,1]{1,0:T(8,128)S(1)}, f32[384,1]{1,0:T(8,128)S(1)}) custom-call(s32[2]{0:T(128)S(1)} %pad_add_fusion.place_ref, ...), custom_call_target="tpu_custom_call", output_to_operand_aliasing={{2}: (1, {}), {3}: (2, {}), {4}: (3, {})} | custom-call | flops 2038431744 | tf_op jit(solution)/shard_map/pallas_call | solution.py:165
  (56 shorter events, 20.3 us)
Async XLA Ops:
  2.8 16.0 %collective-permute-start.1 = (bf16[2,384,256]{2,1,0:T(8,128)(2,1)S(1)}, bf16[2,384,256]{2,1,0:T(8,128)(2,1)S(1)}, u32[]{:S(2)}, u32[]{:S(2)}) collective-permute-start(bf16[2,384,256]{2,1,0:T(8,128)(2,1)S(1)} %copy.71.first_ref.refs_0_.refs_1_), channel_id=1, source_target_pairs={{1,0},{2,1},{3,2},{4,3},{5,4},{6,5},{7,6},{17,16},{18,17},{19,18},... | collective-permute-start | bytes 1179656 | tf_op jit(solution)/shard_map/ppermute | solution.py:203
  3.5 15.3 %collective-permute-start = (bf16[2,384,256]{2,1,0:T(8,128)(2,1)S(1)}, bf16[2,384,256]{2,1,0:T(8,128)(2,1)S(1)}, u32[]{:S(2)}, u32[]{:S(2)}) collective-permute-start(bf16[2,384,256]{2,1,0:T(8,128)(2,1)S(1)} %copy.71.first_ref.refs_0_.refs_1_), channel_id=1, source_target_pairs={{0,1},{1,2},{2,3},{3,4},{4,5},{5,6},{6,7},{16,17},{17,18},{18,19},... | collective-permute-start | bytes 1179656 | tf_op jit(solution)/shard_map/ppermute | solution.py:203
  9.9 7.7 %collective-permute-start.2 = (bf16[1,384,128]{2,1,0:T(8,128)(2,1)S(1)}, bf16[1,384,128]{2,1,0:T(8,128)(2,1)S(1)}, u32[]{:S(2)}, u32[]{:S(2)}) collective-permute-start(bf16[1,384,128]{2,1,0:T(8,128)(2,1)S(1)} %get-tuple-element.90), channel_id=1, source_target_pairs={{8,9},{9,10},{10,11},{11,12},{12,13},{13,14},{14,15},{24,25},{25,2... | collective-permute-start | bytes 294920 | tf_op jit(solution)/shard_map/ppermute | solution.py:203
  13.0 5.7 %collective-permute-start.3 = (bf16[1,384,128]{2,1,0:T(8,128)(2,1)S(1)}, bf16[1,384,128]{2,1,0:T(8,128)(2,1)S(1)}, u32[]{:S(2)}, u32[]{:S(2)}) collective-permute-start(bf16[1,384,128]{2,1,0:T(8,128)(2,1)S(1)} %get-tuple-element.91), channel_id=1, source_target_pairs={{9,8},{10,9},{11,10},{12,11},{13,12},{14,13},{15,14},{25,24},{26,2... | collective-permute-start | bytes 294920 | tf_op jit(solution)/shard_map/ppermute | solution.py:203
  16.1 4.0 %collective-permute-start.6 = (bf16[3,384,256]{2,1,0:T(8,128)(2,1)S(1)}, bf16[3,384,256]{2,1,0:T(8,128)(2,1)S(1)}, u32[]{:S(2)}, u32[]{:S(2)}) collective-permute-start(bf16[3,384,256]{2,1,0:T(8,128)(2,1)S(1)} %get-tuple-element.96.refs_4_), channel_id=1, source_target_pairs={{1,0},{2,1},{3,2},{4,3},{5,4},{6,5},{7,6}} | collective-permute-start | bytes 1769480 | tf_op jit(solution)/shard_map/ppermute | solution.py:203
  17.6 2.5 %collective-permute-start.5 = (bf16[3,384,256]{2,1,0:T(8,128)(2,1)S(1)}, bf16[3,384,256]{2,1,0:T(8,128)(2,1)S(1)}, u32[]{:S(2)}, u32[]{:S(2)}) collective-permute-start(bf16[3,384,256]{2,1,0:T(8,128)(2,1)S(1)} %get-tuple-element.96.refs_4_), channel_id=1, source_target_pairs={{0,1},{1,2},{2,3},{3,4},{4,5},{5,6},{6,7}} | collective-permute-start | bytes 1769480 | tf_op jit(solution)/shard_map/ppermute | solution.py:203
  19.4 2.0 %collective-permute-start.4 = (bf16[384,512]{1,0:T(8,128)(2,1)S(1)}, bf16[384,512]{1,0:T(8,128)(2,1)S(1)}, u32[]{:S(2)}, u32[]{:S(2)}) collective-permute-start(bf16[384,512]{1,0:T(8,128)(2,1)S(1)} %get-tuple-element.95), channel_id=1, source_target_pairs={{0,8},{1,9},{2,10},{3,11},{4,12},{5,13},{6,14},{7,15},{8,0},{9,1},... | collective-permute-start | bytes 1179656 | tf_op jit(solution)/shard_map/ppermute | solution.py:203
  22.1 2.7 %collective-permute-start.9 = (bf16[384,256]{1,0:T(8,128)(2,1)S(1)}, bf16[384,256]{1,0:T(8,128)(2,1)S(1)}, u32[]{:S(2)}, u32[]{:S(2)}) collective-permute-start(bf16[384,256]{1,0:T(8,128)(2,1)S(1)} %get-tuple-element.105), channel_id=1, source_target_pairs={{9,16},{10,17},{11,18},{12,19},{13,20},{14,21},{15,22}} | collective-permute-start | bytes 589832 | tf_op jit(solution)/shard_map/ppermute | solution.py:203
  22.8 2.0 %collective-permute-start.8 = (bf16[384,256]{1,0:T(8,128)(2,1)S(1)}, bf16[384,256]{1,0:T(8,128)(2,1)S(1)}, u32[]{:S(2)}, u32[]{:S(2)}) collective-permute-start(bf16[384,256]{1,0:T(8,128)(2,1)S(1)} %get-tuple-element.105), channel_id=1, source_target_pairs={{8,17},{9,18},{10,19},{11,20},{12,21},{13,22},{14,23}} | collective-permute-start | bytes 589832 | tf_op jit(solution)/shard_map/ppermute | solution.py:203
  24.8 25.4 %collective-permute-start.10 = (bf16[384,512]{1,0:T(8,128)(2,1)S(1)}, bf16[384,512]{1,0:T(8,128)(2,1)S(1)}, u32[]{:S(2)}, u32[]{:S(2)}) collective-permute-start(bf16[384,512]{1,0:T(8,128)(2,1)S(1)} %get-tuple-element.106), channel_id=1, source_target_pairs={{0,8},{1,9},{2,10},{3,11},{4,12},{5,13},{6,14},{7,15},{8,0},{9,1},... | collective-permute-start | bytes 1179656 | tf_op jit(solution)/shard_map/ppermute | solution.py:203
  51.0 2.7 %collective-permute-start.13 = (bf16[384,256]{1,0:T(8,128)(2,1)S(1)}, bf16[384,256]{1,0:T(8,128)(2,1)S(1)}, u32[]{:S(2)}, u32[]{:S(2)}) collective-permute-start(bf16[384,256]{1,0:T(8,128)(2,1)S(1)} %get-tuple-element.119), channel_id=1, source_target_pairs={{9,16},{10,17},{11,18},{12,19},{13,20},{14,21},{15,22}} | collective-permute-start | bytes 589832 | tf_op jit(solution)/shard_map/ppermute | solution.py:203
  51.7 2.0 %collective-permute-start.12 = (bf16[384,256]{1,0:T(8,128)(2,1)S(1)}, bf16[384,256]{1,0:T(8,128)(2,1)S(1)}, u32[]{:S(2)}, u32[]{:S(2)}) collective-permute-start(bf16[384,256]{1,0:T(8,128)(2,1)S(1)} %get-tuple-element.119), channel_id=1, source_target_pairs={{8,17},{9,18},{10,19},{11,20},{12,21},{13,22},{14,23}} | collective-permute-start | bytes 589832 | tf_op jit(solution)/shard_map/ppermute | solution.py:203
  52.4 1.4 %collective-permute-start.11 = (bf16[384,256]{1,0:T(8,128)(2,1)S(1)}, bf16[384,256]{1,0:T(8,128)(2,1)S(1)}, u32[]{:S(2)}, u32[]{:S(2)}) collective-permute-start(bf16[384,256]{1,0:T(8,128)(2,1)S(1)} %get-tuple-element.119), channel_id=1, source_target_pairs={{8,16},{9,17},{10,18},{11,19},{12,20},{13,21},{14,22},{15,23}} | collective-permute-start | bytes 589832 | tf_op jit(solution)/shard_map/ppermute | solution.py:203
  53.7 11.8 %collective-permute-start.14 = (bf16[384,512]{1,0:T(8,128)(2,1)S(1)}, bf16[384,512]{1,0:T(8,128)(2,1)S(1)}, u32[]{:S(2)}, u32[]{:S(2)}) collective-permute-start(bf16[384,512]{1,0:T(8,128)(2,1)S(1)} %get-tuple-element.120), channel_id=1, source_target_pairs={{0,8},{1,9},{2,10},{3,11},{4,12},{5,13},{6,14},{7,15},{8,0},{9,1},... | collective-permute-start | bytes 1179656 | tf_op jit(solution)/shard_map/ppermute | solution.py:203
  70.6 2.7 %collective-permute-start.17 = (bf16[384,256]{1,0:T(8,128)(2,1)S(1)}, bf16[384,256]{1,0:T(8,128)(2,1)S(1)}, u32[]{:S(2)}, u32[]{:S(2)}) collective-permute-start(bf16[384,256]{1,0:T(8,128)(2,1)S(1)} %get-tuple-element.133), channel_id=1, source_target_pairs={{9,16},{10,17},{11,18},{12,19},{13,20},{14,21},{15,22}} | collective-permute-start | bytes 589832 | tf_op jit(solution)/shard_map/ppermute | solution.py:203
  71.3 2.0 %collective-permute-start.16 = (bf16[384,256]{1,0:T(8,128)(2,1)S(1)}, bf16[384,256]{1,0:T(8,128)(2,1)S(1)}, u32[]{:S(2)}, u32[]{:S(2)}) collective-permute-start(bf16[384,256]{1,0:T(8,128)(2,1)S(1)} %get-tuple-element.133), channel_id=1, source_target_pairs={{8,17},{9,18},{10,19},{11,20},{12,21},{13,22},{14,23}} | collective-permute-start | bytes 589832 | tf_op jit(solution)/shard_map/ppermute | solution.py:203
  73.3 8.8 %collective-permute-start.18 = (bf16[384,512]{1,0:T(8,128)(2,1)S(1)}, bf16[384,512]{1,0:T(8,128)(2,1)S(1)}, u32[]{:S(2)}, u32[]{:S(2)}) collective-permute-start(bf16[384,512]{1,0:T(8,128)(2,1)S(1)} %get-tuple-element.134), channel_id=1, source_target_pairs={{0,8},{1,9},{2,10},{3,11},{4,12},{5,13},{6,14},{7,15},{8,0},{9,1},... | collective-permute-start | bytes 1179656 | tf_op jit(solution)/shard_map/ppermute | solution.py:203
  87.6 2.7 %collective-permute-start.21 = (bf16[384,256]{1,0:T(8,128)(2,1)S(1)}, bf16[384,256]{1,0:T(8,128)(2,1)S(1)}, u32[]{:S(2)}, u32[]{:S(2)}) collective-permute-start(bf16[384,256]{1,0:T(8,128)(2,1)S(1)} %get-tuple-element.147), channel_id=1, source_target_pairs={{9,16},{10,17},{11,18},{12,19},{13,20},{14,21},{15,22}} | collective-permute-start | bytes 589832 | tf_op jit(solution)/shard_map/ppermute | solution.py:203
  88.3 2.0 %collective-permute-start.20 = (bf16[384,256]{1,0:T(8,128)(2,1)S(1)}, bf16[384,256]{1,0:T(8,128)(2,1)S(1)}, u32[]{:S(2)}, u32[]{:S(2)}) collective-permute-start(bf16[384,256]{1,0:T(8,128)(2,1)S(1)} %get-tuple-element.147), channel_id=1, source_target_pairs={{8,17},{9,18},{10,19},{11,20},{12,21},{13,22},{14,23}} | collective-permute-start | bytes 589832 | tf_op jit(solution)/shard_map/ppermute | solution.py:203
  90.3 10.2 %collective-permute-start.22 = (bf16[384,512]{1,0:T(8,128)(2,1)S(1)}, bf16[384,512]{1,0:T(8,128)(2,1)S(1)}, u32[]{:S(2)}, u32[]{:S(2)}) collective-permute-start(bf16[384,512]{1,0:T(8,128)(2,1)S(1)} %get-tuple-element.148), channel_id=1, source_target_pairs={{0,8},{1,9},{2,10},{3,11},{4,12},{5,13},{6,14},{7,15},{8,0},{9,1},... | collective-permute-start | bytes 1179656 | tf_op jit(solution)/shard_map/ppermute | solution.py:203
  96.7 3.9 %collective-permute-start.23 = (bf16[384,256]{1,0:T(8,128)(2,1)S(1)}, bf16[384,256]{1,0:T(8,128)(2,1)S(1)}, u32[]{:S(2)}, u32[]{:S(2)}) collective-permute-start(bf16[384,256]{1,0:T(8,128)(2,1)S(1)} %get-tuple-element.133), channel_id=1, source_target_pairs={{24,0},{25,1},{26,2},{27,3},{28,4},{29,5},{30,6},{31,7}} | collective-permute-start | bytes 589832 | tf_op jit(solution)/shard_map/ppermute | solution.py:203
  98.0 7.8 %collective-permute-start.24 = (bf16[384,256]{1,0:T(8,128)(2,1)S(1)}, bf16[384,256]{1,0:T(8,128)(2,1)S(1)}, u32[]{:S(2)}, u32[]{:S(2)}) collective-permute-start(bf16[384,256]{1,0:T(8,128)(2,1)S(1)} %get-tuple-element.147), channel_id=1, source_target_pairs={{24,8},{25,9},{26,10},{27,11},{28,12},{29,13},{30,14},{31,15}} | collective-permute-start | bytes 589832 | tf_op jit(solution)/shard_map/ppermute | solution.py:203
  106.4 3.6 %collective-permute-start.25 = (bf16[384,512]{1,0:T(8,128)(2,1)S(1)}, bf16[384,512]{1,0:T(8,128)(2,1)S(1)}, u32[]{:S(2)}, u32[]{:S(2)}) collective-permute-start(bf16[384,512]{1,0:T(8,128)(2,1)S(1)} %get-tuple-element.160), channel_id=1, source_target_pairs={{0,8},{1,9},{2,10},{3,11},{4,12},{5,13},{6,14},{7,15},{8,0},{9,1},... | collective-permute-start | bytes 1179656 | tf_op jit(solution)/shard_map/ppermute | solution.py:203
  107.1 3.0 %collective-permute-start.26 = (bf16[384,256]{1,0:T(8,128)(2,1)S(1)}, bf16[384,256]{1,0:T(8,128)(2,1)S(1)}, u32[]{:S(2)}, u32[]{:S(2)}) collective-permute-start(bf16[384,256]{1,0:T(8,128)(2,1)S(1)} %get-tuple-element.162), channel_id=1, source_target_pairs={{24,16},{25,17},{26,18},{27,19},{28,20},{29,21},{30,22},{31,23}} | collective-permute-start | bytes 589832 | tf_op jit(solution)/shard_map/ppermute | solution.py:203
  (3 other events, 4.0 us)

commit v4 on v3

--- a/solution.py
+++ b/solution.py
@@ -251,11 +251,13 @@
             cases.append((2 * p, parts, old if b == 0 else kept))
         if tick == 0:
             ins += [odd_above, odd_below]
-        if tick == ticks - 1:
-            ins.append(done[-2])
         out, even_acts, *fixed = call(cases, own + 4, fixed=fixed, ins=ins)
-        if 0 < tick <= blocks:
-            out, *arrived[tick - 1] = lax.optimization_barrier((out, *arrived[tick - 1]))
+        hops = arrived[tick - 1] if 0 < tick <= blocks else ()
+        out, *hops = lax.optimization_barrier((out, *hops, *done[-1:]))
+        if done:
+            done[-1] = hops.pop()
+        if hops:
+            arrived[tick - 1] = hops
         crossed = moved(out, across, 0)
 
         ins = [crossed, first, odd_above, odd_below]
@@ -264,8 +266,6 @@
             ins.append(odd_acts)
         if tick == 0:
             ins += [later_above, later_below]
-        if tick >= ticks - 2:
-            ins.append(done[0] if tick < ticks - 1 else done[-1])
         cases = [(2 * p + 1, [(0, None, 0, own + 2)], old if tick == LAG * p else [(4, None, 0, own + 2)]) for p in busy]
         out, odd_acts, *fixed = call(cases, own + 2, fixed=fixed, ins=ins)
         if tick < blocks:

time: 118 us -> 119 us (level)
  transfers between devices with their start and end apart: 27 -> 27, of which waited for: 8 -> 9; matrix products, arithmetic and copies ran while one was open for 1% -> 1% of each run, Pallas kernels for 11% -> 7%
where the time goes in v4:
time: 119 us
  starting transfers between devices  72 us (61%)
  Pallas kernels  30.4 us (26%)
  waiting for transfers between devices  9.82 us (8%)
  local copies, waits for them, and re-layouts  4.33 us (4%)
    ppermute x27, starting transfers between devices, moved(): lax.ppermute(value, axes, [(a * slabs + s, b * slabs + s + step) for a, b...  72 us
    pallas_call x12, Pallas kernels, layer_call(): pl.pallas_call(functools.partial(layer_kernel, cases, rows_in, own, cols,...  26.2 us
    ppermute x27, waiting for transfers between devices, moved(): lax.ppermute(value, axes, [(a * slabs + s, b * slabs + s + step) for a, b...  9.82 us
    pallas_call x1, Pallas kernels, turned_weights(): pl.pallas_call(functools.partial(turn_kernel, cuts), out_shape=(jax.Shape...  4.16 us
  transfers between devices with their start and end apart: 27, of which 9 were waited for; matrix products, arithmetic and copies ran while one was open for 1% of the time, Pallas kernels for 7%

profile of v4, /device:TPU:13, one launch (start us, length us, event | category | flops | bytes accessed | tf_op | source)
XLA Modules:
  0.0 118.8 jit_solution(2833567724356364150)
XLA Ops:
  0.6 0.9 slice.19
  1.6 1.0 pad_maximum_fusion
  4.2 1.1 slice.18
  5.7 4.2 %shard_map.68 = (bf16[3,384,3456]{2,1,0:T(8,128)(2,1)S(1)}, f32[384,1]{1,0:T(8,128)S(1)}, f32[384,1]{1,0:T(8,128)S(1)}, bf16[3,384,256]{2,1,0:T(8,128)(2,1)S(1)}...) custom-call(bf16[3,3,3,384,384]{4,3,2,1,0:T(8,128)(2,1)} %bitcast.20, ...), custom_call_target="tpu_custom_call", output_to_operand_aliasing={{3}: (3, {})} | custom-call | bytes 15925248 | tf_op jit(solution)/shard_map/pallas_call | solution.py:42
  9.9 3.1 %collective-permute-start.2 = (bf16[1,384,128]{2,1,0:T(8,128)(2,1)S(1)}, bf16[1,384,128]{2,1,0:T(8,128)(2,1)S(1)}, u32[]{:S(2)}, u32[]{:S(2)}) collective-permute-start(bf16[1,384,128]{2,1,0:T(8,128)(2,1)S(1)} %get-tuple-element.94), channel_id=1, source_target_pairs={{8,9},{9,10},{10,11},{11,12},{12,13},{13,14},{14,15},{24,25},{25,2... | collective-permute-start | bytes 294920 | tf_op jit(solution)/shard_map/ppermute | solution.py:203
  13.0 3.1 %collective-permute-start.3 = (bf16[1,384,128]{2,1,0:T(8,128)(2,1)S(1)}, bf16[1,384,128]{2,1,0:T(8,128)(2,1)S(1)}, u32[]{:S(2)}, u32[]{:S(2)}) collective-permute-start(bf16[1,384,128]{2,1,0:T(8,128)(2,1)S(1)} %get-tuple-element.95), channel_id=1, source_target_pairs={{9,8},{10,9},{11,10},{12,11},{13,12},{14,13},{15,14},{25,24},{26,2... | collective-permute-start | bytes 294920 | tf_op jit(solution)/shard_map/ppermute | solution.py:203
  20.1 1.3 %collective-permute-done.4.refs_0_ = bf16[384,512]{1,0:T(8,128)(2,1)S(1)} collective-permute-done((bf16[384,512]{1,0:T(8,128)(2,1)S(1)}, bf16[384,512]{1,0:T(8,128)(2,1)S(1)}, u32[]{:S(2)}, u32[]{:S(2)}) %collective-permute-start.4) | collective-permute-done | bytes 393248 | tf_op jit(solution)/shard_map/ppermute | solution.py:203
  24.8 24.1 %collective-permute-start.10 = (bf16[384,512]{1,0:T(8,128)(2,1)S(1)}, bf16[384,512]{1,0:T(8,128)(2,1)S(1)}, u32[]{:S(2)}, u32[]{:S(2)}) collective-permute-start(bf16[384,512]{1,0:T(8,128)(2,1)S(1)} %get-tuple-element.110), channel_id=1, source_target_pairs={{0,8},{1,9},{2,10},{3,11},{4,12},{5,13},{6,14},{7,15},{8,0},{9,1},... | collective-permute-start | bytes 1179656 | tf_op jit(solution)/shard_map/ppermute | solution.py:203
  48.9 1.3 %collective-permute-done.10.refs_0_ = bf16[384,512]{1,0:T(8,128)(2,1)S(1)} collective-permute-done((bf16[384,512]{1,0:T(8,128)(2,1)S(1)}, bf16[384,512]{1,0:T(8,128)(2,1)S(1)}, u32[]{:S(2)}, u32[]{:S(2)}) %collective-permute-start.10) | collective-permute-done | bytes 393248 | tf_op jit(solution)/shard_map/ppermute | solution.py:203
  53.7 10.4 %collective-permute-start.14 = (bf16[384,512]{1,0:T(8,128)(2,1)S(1)}, bf16[384,512]{1,0:T(8,128)(2,1)S(1)}, u32[]{:S(2)}, u32[]{:S(2)}) collective-permute-start(bf16[384,512]{1,0:T(8,128)(2,1)S(1)} %get-tuple-element.124), channel_id=1, source_target_pairs={{0,8},{1,9},{2,10},{3,11},{4,12},{5,13},{6,14},{7,15},{8,0},{9,1},... | collective-permute-start | bytes 1179656 | tf_op jit(solution)/shard_map/ppermute | solution.py:203
  64.2 1.3 %collective-permute-done.14.refs_0_ = bf16[384,512]{1,0:T(8,128)(2,1)S(1)} collective-permute-done((bf16[384,512]{1,0:T(8,128)(2,1)S(1)}, bf16[384,512]{1,0:T(8,128)(2,1)S(1)}, u32[]{:S(2)}, u32[]{:S(2)}) %collective-permute-start.14) | collective-permute-done | bytes 393248 | tf_op jit(solution)/shard_map/ppermute | solution.py:203
  65.5 5.1 %shard_map.74 = (bf16[384,256]{1,0:T(8,128)(2,1)S(1)}, bf16[384,512]{1,0:T(8,128)(2,1)S(1)}, bf16[3,384,3456]{2,1,0:T(8,128)(2,1)S(1)}, f32[384,1]{1,0:T(8,128)S(1)}, f32[384,1]{1,0:T(8,128)S(1)}) custom-call(s32[2]{0:T(128)S(1)} %pad_add_fusion.place_ref, ...), custom_call_target="tpu_custom_call", output_to_operand_aliasing={{2}: (1, {}), {3}: (2, {}), {4}: (3, {})} | custom-call | flops 2038431744 | tf_op jit(solution)/shard_map/pallas_call | solution.py:165
  70.6 1.3 %collective-permute-start.18 = (bf16[384,256]{1,0:T(8,128)(2,1)S(1)}, bf16[384,256]{1,0:T(8,128)(2,1)S(1)}, u32[]{:S(2)}, u32[]{:S(2)}) collective-permute-start(bf16[384,256]{1,0:T(8,128)(2,1)S(1)} %get-tuple-element.137), channel_id=1, source_target_pairs={{24,0},{25,1},{26,2},{27,3},{28,4},{29,5},{30,6},{31,7}} | collective-permute-start | bytes 589832 | tf_op jit(solution)/shard_map/ppermute | solution.py:203
  74.7 6.8 %collective-permute-start.19 = (bf16[384,512]{1,0:T(8,128)(2,1)S(1)}, bf16[384,512]{1,0:T(8,128)(2,1)S(1)}, u32[]{:S(2)}, u32[]{:S(2)}) collective-permute-start(bf16[384,512]{1,0:T(8,128)(2,1)S(1)} %get-tuple-element.138), channel_id=1, source_target_pairs={{0,8},{1,9},{2,10},{3,11},{4,12},{5,13},{6,14},{7,15},{8,0},{9,1},... | collective-permute-start | bytes 1179656 | tf_op jit(solution)/shard_map/ppermute | solution.py:203
  81.5 1.3 %collective-permute-done.19.refs_0_ = bf16[384,512]{1,0:T(8,128)(2,1)S(1)} collective-permute-done((bf16[384,512]{1,0:T(8,128)(2,1)S(1)}, bf16[384,512]{1,0:T(8,128)(2,1)S(1)}, u32[]{:S(2)}, u32[]{:S(2)}) %collective-permute-start.19) | collective-permute-done | bytes 393248 | tf_op jit(solution)/shard_map/ppermute | solution.py:203
  82.9 5.5 %shard_map.76 = (bf16[384,256]{1,0:T(8,128)(2,1)S(1)}, bf16[384,512]{1,0:T(8,128)(2,1)S(1)}, bf16[3,384,3456]{2,1,0:T(8,128)(2,1)S(1)}, f32[384,1]{1,0:T(8,128)S(1)}, f32[384,1]{1,0:T(8,128)S(1)}) custom-call(s32[2]{0:T(128)S(1)} %pad_add_fusion.place_ref, ...), custom_call_target="tpu_custom_call", output_to_operand_aliasing={{2}: (1, {}), {3}: (2, {}), {4}: (3, {})} | custom-call | flops 2038431744 | tf_op jit(solution)/shard_map/pallas_call | solution.py:165
  88.3 1.3 %collective-permute-start.23 = (bf16[384,256]{1,0:T(8,128)(2,1)S(1)}, bf16[384,256]{1,0:T(8,128)(2,1)S(1)}, u32[]{:S(2)}, u32[]{:S(2)}) collective-permute-start(bf16[384,256]{1,0:T(8,128)(2,1)S(1)} %get-tuple-element.151), channel_id=1, source_target_pairs={{24,8},{25,9},{26,10},{27,11},{28,12},{29,13},{30,14},{31,15}} | collective-permute-start | bytes 589832 | tf_op jit(solution)/shard_map/ppermute | solution.py:203
  92.3 6.3 %collective-permute-start.24 = (bf16[384,512]{1,0:T(8,128)(2,1)S(1)}, bf16[384,512]{1,0:T(8,128)(2,1)S(1)}, u32[]{:S(2)}, u32[]{:S(2)}) collective-permute-start(bf16[384,512]{1,0:T(8,128)(2,1)S(1)} %get-tuple-element.152), channel_id=1, source_target_pairs={{0,8},{1,9},{2,10},{3,11},{4,12},{5,13},{6,14},{7,15},{8,0},{9,1},... | collective-permute-start | bytes 1179656 | tf_op jit(solution)/shard_map/ppermute | solution.py:203
  98.7 1.3 %collective-permute-done.24.refs_0_ = bf16[384,512]{1,0:T(8,128)(2,1)S(1)} collective-permute-done((bf16[384,512]{1,0:T(8,128)(2,1)S(1)}, bf16[384,512]{1,0:T(8,128)(2,1)S(1)}, u32[]{:S(2)}, u32[]{:S(2)}) %collective-permute-start.24) | collective-permute-done | bytes 393248 | tf_op jit(solution)/shard_map/ppermute | solution.py:203
  100.0 5.2 %shard_map.78 = (bf16[384,256]{1,0:T(8,128)(2,1)S(1)}, bf16[384,512]{1,0:T(8,128)(2,1)S(1)}, bf16[3,384,3456]{2,1,0:T(8,128)(2,1)S(1)}, f32[384,1]{1,0:T(8,128)S(1)}, f32[384,1]{1,0:T(8,128)S(1)}) custom-call(s32[2]{0:T(128)S(1)} %pad_add_fusion.place_ref, ...), custom_call_target="tpu_custom_call", output_to_operand_aliasing={{2}: (1, {}), {3}: (2, {}), {4}: (3, {})} | custom-call | flops 2038431744 | tf_op jit(solution)/shard_map/pallas_call | solution.py:165
  105.2 1.3 %collective-permute-start.25 = (bf16[384,256]{1,0:T(8,128)(2,1)S(1)}, bf16[384,256]{1,0:T(8,128)(2,1)S(1)}, u32[]{:S(2)}, u32[]{:S(2)}) collective-permute-start(bf16[384,256]{1,0:T(8,128)(2,1)S(1)} %get-tuple-element.165), channel_id=1, source_target_pairs={{24,16},{25,17},{26,18},{27,19},{28,20},{29,21},{30,22},{31,23}} | collective-permute-start | bytes 589832 | tf_op jit(solution)/shard_map/ppermute | solution.py:203
  107.6 2.7 %collective-permute-start.26 = (bf16[384,512]{1,0:T(8,128)(2,1)S(1)}, bf16[384,512]{1,0:T(8,128)(2,1)S(1)}, u32[]{:S(2)}, u32[]{:S(2)}) collective-permute-start(bf16[384,512]{1,0:T(8,128)(2,1)S(1)} %get-tuple-element.166), channel_id=1, source_target_pairs={{0,8},{1,9},{2,10},{3,11},{4,12},{5,13},{6,14},{7,15},{8,0},{9,1},... | collective-permute-start | bytes 1179656 | tf_op jit(solution)/shard_map/ppermute | solution.py:203
  110.3 1.3 %collective-permute-done.26.refs_0_ = bf16[384,512]{1,0:T(8,128)(2,1)S(1)} collective-permute-done((bf16[384,512]{1,0:T(8,128)(2,1)S(1)}, bf16[384,512]{1,0:T(8,128)(2,1)S(1)}, u32[]{:S(2)}, u32[]{:S(2)}) %collective-permute-start.26) | collective-permute-done | bytes 393248 | tf_op jit(solution)/shard_map/ppermute | solution.py:203
  111.7 5.2 %shard_map.80 = (bf16[384,256]{1,0:T(8,128)(2,1)S(1)}, bf16[384,512]{1,0:T(8,128)(2,1)S(1)}, bf16[3,384,3456]{2,1,0:T(8,128)(2,1)S(1)}, f32[384,1]{1,0:T(8,128)S(1)}, f32[384,1]{1,0:T(8,128)S(1)}) custom-call(s32[2]{0:T(128)S(1)} %pad_add_fusion.place_ref, ...), custom_call_target="tpu_custom_call", output_to_operand_aliasing={{2}: (1, {}), {3}: (2, {}), {4}: (3, {})} | custom-call | flops 2038431744 | tf_op jit(solution)/shard_map/pallas_call | solution.py:165
  (56 shorter events, 20.9 us)
Async XLA Ops:
  2.8 16.0 %collective-permute-start.1 = (bf16[2,384,256]{2,1,0:T(8,128)(2,1)S(1)}, bf16[2,384,256]{2,1,0:T(8,128)(2,1)S(1)}, u32[]{:S(2)}, u32[]{:S(2)}) collective-permute-start(bf16[2,384,256]{2,1,0:T(8,128)(2,1)S(1)} %copy.71.first_ref.refs_0_.refs_1_), channel_id=1, source_target_pairs={{1,0},{2,1},{3,2},{4,3},{5,4},{6,5},{7,6},{17,16},{18,17},{19,18},... | collective-permute-start | bytes 1179656 | tf_op jit(solution)/shard_map/ppermute | solution.py:203
  3.5 15.3 %collective-permute-start = (bf16[2,384,256]{2,1,0:T(8,128)(2,1)S(1)}, bf16[2,384,256]{2,1,0:T(8,128)(2,1)S(1)}, u32[]{:S(2)}, u32[]{:S(2)}) collective-permute-start(bf16[2,384,256]{2,1,0:T(8,128)(2,1)S(1)} %copy.71.first_ref.refs_0_.refs_1_), channel_id=1, source_target_pairs={{0,1},{1,2},{2,3},{3,4},{4,5},{5,6},{6,7},{16,17},{17,18},{18,19},... | collective-permute-start | bytes 1179656 | tf_op jit(solution)/shard_map/ppermute | solution.py:203
  9.9 7.7 %collective-permute-start.2 = (bf16[1,384,128]{2,1,0:T(8,128)(2,1)S(1)}, bf16[1,384,128]{2,1,0:T(8,128)(2,1)S(1)}, u32[]{:S(2)}, u32[]{:S(2)}) collective-permute-start(bf16[1,384,128]{2,1,0:T(8,128)(2,1)S(1)} %get-tuple-element.94), channel_id=1, source_target_pairs={{8,9},{9,10},{10,11},{11,12},{12,13},{13,14},{14,15},{24,25},{25,2... | collective-permute-start | bytes 294920 | tf_op jit(solution)/shard_map/ppermute | solution.py:203
  13.0 5.7 %collective-permute-start.3 = (bf16[1,384,128]{2,1,0:T(8,128)(2,1)S(1)}, bf16[1,384,128]{2,1,0:T(8,128)(2,1)S(1)}, u32[]{:S(2)}, u32[]{:S(2)}) collective-permute-start(bf16[1,384,128]{2,1,0:T(8,128)(2,1)S(1)} %get-tuple-element.95), channel_id=1, source_target_pairs={{9,8},{10,9},{11,10},{12,11},{13,12},{14,13},{15,14},{25,24},{26,2... | collective-permute-start | bytes 294920 | tf_op jit(solution)/shard_map/ppermute | solution.py:203
  16.1 4.0 %collective-permute-start.6 = (bf16[3,384,256]{2,1,0:T(8,128)(2,1)S(1)}, bf16[3,384,256]{2,1,0:T(8,128)(2,1)S(1)}, u32[]{:S(2)}, u32[]{:S(2)}) collective-permute-start(bf16[3,384,256]{2,1,0:T(8,128)(2,1)S(1)} %get-tuple-element.100.refs_4_), channel_id=1, source_target_pairs={{1,0},{2,1},{3,2},{4,3},{5,4},{6,5},{7,6}} | collective-permute-start | bytes 1769480 | tf_op jit(solution)/shard_map/ppermute | solution.py:203
  17.6 2.5 %collective-permute-start.5 = (bf16[3,384,256]{2,1,0:T(8,128)(2,1)S(1)}, bf16[3,384,256]{2,1,0:T(8,128)(2,1)S(1)}, u32[]{:S(2)}, u32[]{:S(2)}) collective-permute-start(bf16[3,384,256]{2,1,0:T(8,128)(2,1)S(1)} %get-tuple-element.100.refs_4_), channel_id=1, source_target_pairs={{0,1},{1,2},{2,3},{3,4},{4,5},{5,6},{6,7}} | collective-permute-start | bytes 1769480 | tf_op jit(solution)/shard_map/ppermute | solution.py:203
  19.4 2.0 %collective-permute-start.4 = (bf16[384,512]{1,0:T(8,128)(2,1)S(1)}, bf16[384,512]{1,0:T(8,128)(2,1)S(1)}, u32[]{:S(2)}, u32[]{:S(2)}) collective-permute-start(bf16[384,512]{1,0:T(8,128)(2,1)S(1)} %get-tuple-element.99), channel_id=1, source_target_pairs={{0,8},{1,9},{2,10},{3,11},{4,12},{5,13},{6,14},{7,15},{8,0},{9,1},... | collective-permute-start | bytes 1179656 | tf_op jit(solution)/shard_map/ppermute | solution.py:203
  22.1 2.7 %collective-permute-start.9 = (bf16[384,256]{1,0:T(8,128)(2,1)S(1)}, bf16[384,256]{1,0:T(8,128)(2,1)S(1)}, u32[]{:S(2)}, u32[]{:S(2)}) collective-permute-start(bf16[384,256]{1,0:T(8,128)(2,1)S(1)} %get-tuple-element.109), channel_id=1, source_target_pairs={{9,16},{10,17},{11,18},{12,19},{13,20},{14,21},{15,22}} | collective-permute-start | bytes 589832 | tf_op jit(solution)/shard_map/ppermute | solution.py:203
  22.8 2.0 %collective-permute-start.8 = (bf16[384,256]{1,0:T(8,128)(2,1)S(1)}, bf16[384,256]{1,0:T(8,128)(2,1)S(1)}, u32[]{:S(2)}, u32[]{:S(2)}) collective-permute-start(bf16[384,256]{1,0:T(8,128)(2,1)S(1)} %get-tuple-element.109), channel_id=1, source_target_pairs={{8,17},{9,18},{10,19},{11,20},{12,21},{13,22},{14,23}} | collective-permute-start | bytes 589832 | tf_op jit(solution)/shard_map/ppermute | solution.py:203
  24.8 25.4 %collective-permute-start.10 = (bf16[384,512]{1,0:T(8,128)(2,1)S(1)}, bf16[384,512]{1,0:T(8,128)(2,1)S(1)}, u32[]{:S(2)}, u32[]{:S(2)}) collective-permute-start(bf16[384,512]{1,0:T(8,128)(2,1)S(1)} %get-tuple-element.110), channel_id=1, source_target_pairs={{0,8},{1,9},{2,10},{3,11},{4,12},{5,13},{6,14},{7,15},{8,0},{9,1},... | collective-permute-start | bytes 1179656 | tf_op jit(solution)/shard_map/ppermute | solution.py:203
  51.0 2.7 %collective-permute-start.13 = (bf16[384,256]{1,0:T(8,128)(2,1)S(1)}, bf16[384,256]{1,0:T(8,128)(2,1)S(1)}, u32[]{:S(2)}, u32[]{:S(2)}) collective-permute-start(bf16[384,256]{1,0:T(8,128)(2,1)S(1)} %get-tuple-element.123), channel_id=1, source_target_pairs={{9,16},{10,17},{11,18},{12,19},{13,20},{14,21},{15,22}} | collective-permute-start | bytes 589832 | tf_op jit(solution)/shard_map/ppermute | solution.py:203
  51.7 2.0 %collective-permute-start.12 = (bf16[384,256]{1,0:T(8,128)(2,1)S(1)}, bf16[384,256]{1,0:T(8,128)(2,1)S(1)}, u32[]{:S(2)}, u32[]{:S(2)}) collective-permute-start(bf16[384,256]{1,0:T(8,128)(2,1)S(1)} %get-tuple-element.123), channel_id=1, source_target_pairs={{8,17},{9,18},{10,19},{11,20},{12,21},{13,22},{14,23}} | collective-permute-start | bytes 589832 | tf_op jit(solution)/shard_map/ppermute | solution.py:203
  53.7 11.8 %collective-permute-start.14 = (bf16[384,512]{1,0:T(8,128)(2,1)S(1)}, bf16[384,512]{1,0:T(8,128)(2,1)S(1)}, u32[]{:S(2)}, u32[]{:S(2)}) collective-permute-start(bf16[384,512]{1,0:T(8,128)(2,1)S(1)} %get-tuple-element.124), channel_id=1, source_target_pairs={{0,8},{1,9},{2,10},{3,11},{4,12},{5,13},{6,14},{7,15},{8,0},{9,1},... | collective-permute-start | bytes 1179656 | tf_op jit(solution)/shard_map/ppermute | solution.py:203
  70.6 4.0 %collective-permute-start.18 = (bf16[384,256]{1,0:T(8,128)(2,1)S(1)}, bf16[384,256]{1,0:T(8,128)(2,1)S(1)}, u32[]{:S(2)}, u32[]{:S(2)}) collective-permute-start(bf16[384,256]{1,0:T(8,128)(2,1)S(1)} %get-tuple-element.137), channel_id=1, source_target_pairs={{24,0},{25,1},{26,2},{27,3},{28,4},{29,5},{30,6},{31,7}} | collective-permute-start | bytes 589832 | tf_op jit(solution)/shard_map/ppermute | solution.py:203
  71.9 2.7 %collective-permute-start.17 = (bf16[384,256]{1,0:T(8,128)(2,1)S(1)}, bf16[384,256]{1,0:T(8,128)(2,1)S(1)}, u32[]{:S(2)}, u32[]{:S(2)}) collective-permute-start(bf16[384,256]{1,0:T(8,128)(2,1)S(1)} %get-tuple-element.137), channel_id=1, source_target_pairs={{9,16},{10,17},{11,18},{12,19},{13,20},{14,21},{15,22}} | collective-permute-start | bytes 589832 | tf_op jit(solution)/shard_map/ppermute | solution.py:203
  72.6 2.0 %collective-permute-start.16 = (bf16[384,256]{1,0:T(8,128)(2,1)S(1)}, bf16[384,256]{1,0:T(8,128)(2,1)S(1)}, u32[]{:S(2)}, u32[]{:S(2)}) collective-permute-start(bf16[384,256]{1,0:T(8,128)(2,1)S(1)} %get-tuple-element.137), channel_id=1, source_target_pairs={{8,17},{9,18},{10,19},{11,20},{12,21},{13,22},{14,23}} | collective-permute-start | bytes 589832 | tf_op jit(solution)/shard_map/ppermute | solution.py:203
  73.3 1.4 %collective-permute-start.15 = (bf16[384,256]{1,0:T(8,128)(2,1)S(1)}, bf16[384,256]{1,0:T(8,128)(2,1)S(1)}, u32[]{:S(2)}, u32[]{:S(2)}) collective-permute-start(bf16[384,256]{1,0:T(8,128)(2,1)S(1)} %get-tuple-element.137), channel_id=1, source_target_pairs={{8,16},{9,17},{10,18},{11,19},{12,20},{13,21},{14,22},{15,23}} | collective-permute-start | bytes 589832 | tf_op jit(solution)/shard_map/ppermute | solution.py:203
  74.7 8.2 %collective-permute-start.19 = (bf16[384,512]{1,0:T(8,128)(2,1)S(1)}, bf16[384,512]{1,0:T(8,128)(2,1)S(1)}, u32[]{:S(2)}, u32[]{:S(2)}) collective-permute-start(bf16[384,512]{1,0:T(8,128)(2,1)S(1)} %get-tuple-element.138), channel_id=1, source_target_pairs={{0,8},{1,9},{2,10},{3,11},{4,12},{5,13},{6,14},{7,15},{8,0},{9,1},... | collective-permute-start | bytes 1179656 | tf_op jit(solution)/shard_map/ppermute | solution.py:203
  88.3 4.0 %collective-permute-start.23 = (bf16[384,256]{1,0:T(8,128)(2,1)S(1)}, bf16[384,256]{1,0:T(8,128)(2,1)S(1)}, u32[]{:S(2)}, u32[]{:S(2)}) collective-permute-start(bf16[384,256]{1,0:T(8,128)(2,1)S(1)} %get-tuple-element.151), channel_id=1, source_target_pairs={{24,8},{25,9},{26,10},{27,11},{28,12},{29,13},{30,14},{31,15}} | collective-permute-start | bytes 589832 | tf_op jit(solution)/shard_map/ppermute | solution.py:203
  89.6 2.7 %collective-permute-start.22 = (bf16[384,256]{1,0:T(8,128)(2,1)S(1)}, bf16[384,256]{1,0:T(8,128)(2,1)S(1)}, u32[]{:S(2)}, u32[]{:S(2)}) collective-permute-start(bf16[384,256]{1,0:T(8,128)(2,1)S(1)} %get-tuple-element.151), channel_id=1, source_target_pairs={{9,16},{10,17},{11,18},{12,19},{13,20},{14,21},{15,22}} | collective-permute-start | bytes 589832 | tf_op jit(solution)/shard_map/ppermute | solution.py:203
  90.3 2.0 %collective-permute-start.21 = (bf16[384,256]{1,0:T(8,128)(2,1)S(1)}, bf16[384,256]{1,0:T(8,128)(2,1)S(1)}, u32[]{:S(2)}, u32[]{:S(2)}) collective-permute-start(bf16[384,256]{1,0:T(8,128)(2,1)S(1)} %get-tuple-element.151), channel_id=1, source_target_pairs={{8,17},{9,18},{10,19},{11,20},{12,21},{13,22},{14,23}} | collective-permute-start | bytes 589832 | tf_op jit(solution)/shard_map/ppermute | solution.py:203
  92.3 7.7 %collective-permute-start.24 = (bf16[384,512]{1,0:T(8,128)(2,1)S(1)}, bf16[384,512]{1,0:T(8,128)(2,1)S(1)}, u32[]{:S(2)}, u32[]{:S(2)}) collective-permute-start(bf16[384,512]{1,0:T(8,128)(2,1)S(1)} %get-tuple-element.152), channel_id=1, source_target_pairs={{0,8},{1,9},{2,10},{3,11},{4,12},{5,13},{6,14},{7,15},{8,0},{9,1},... | collective-permute-start | bytes 1179656 | tf_op jit(solution)/shard_map/ppermute | solution.py:203
  105.2 2.4 %collective-permute-start.25 = (bf16[384,256]{1,0:T(8,128)(2,1)S(1)}, bf16[384,256]{1,0:T(8,128)(2,1)S(1)}, u32[]{:S(2)}, u32[]{:S(2)}) collective-permute-start(bf16[384,256]{1,0:T(8,128)(2,1)S(1)} %get-tuple-element.165), channel_id=1, source_target_pairs={{24,16},{25,17},{26,18},{27,19},{28,20},{29,21},{30,22},{31,23}} | collective-permute-start | bytes 589832 | tf_op jit(solution)/shard_map/ppermute | solution.py:203
  107.6 4.1 %collective-permute-start.26 = (bf16[384,512]{1,0:T(8,128)(2,1)S(1)}, bf16[384,512]{1,0:T(8,128)(2,1)S(1)}, u32[]{:S(2)}, u32[]{:S(2)}) collective-permute-start(bf16[384,512]{1,0:T(8,128)(2,1)S(1)} %get-tuple-element.166), channel_id=1, source_target_pairs={{0,8},{1,9},{2,10},{3,11},{4,12},{5,13},{6,14},{7,15},{8,0},{9,1},... | collective-permute-start | bytes 1179656 | tf_op jit(solution)/shard_map/ppermute | solution.py:203
  (3 other events, 4.0 us)

commit v5 on v3

--- a/solution.py
+++ b/solution.py
@@ -62,7 +62,7 @@
     )(*(pltpu.with_memory_space_constraint(v, pltpu.HBM) for v in (weight, bias, gain)), later, first)
 
 
-def layer_kernel(cases, rows_in, own, cols, block, height, n_in, place_ref, w_ref, bias_ref, gain_ref, *refs):
+def layer_kernel(cases, rows_in, own, cols, block, height, n_in, back, place_ref, w_ref, bias_ref, gain_ref, *refs):
     ins = refs[:n_in]
     out_ref, acts_ref = refs[n_in:n_in + 2]
     xs, buf, total, sems = refs[n_in + 5:]
@@ -80,6 +80,13 @@
         return ins[at] if index is None else ins[at].at[index]
 
     active = functools.reduce(jnp.logical_or, [segment == g for g, _, _ in cases])
+    if back is not None:
+        @pl.when(segment == back[0])
+        def _():
+            copy = pltpu.make_async_copy(ins[back[1]], out_ref.at[:, pl.ds(0, ins[back[1]].shape[1])], sems.at[0])
+            copy.start()
+            copy.wait()
+
     for g, x_parts, before in cases:
         @pl.when(segment == g)
         def _():
@@ -158,12 +165,12 @@
         out_done.wait()
 
 
-def layer_call(cases, rows_in, own, cols, block, height, place, fixed, ins):
+def layer_call(cases, rows_in, own, cols, block, height, place, fixed, ins, back=None):
     weight, bias, gain = fixed
     channels = weight.shape[1]
     row = block * cols
     return pl.pallas_call(
-        functools.partial(layer_kernel, cases, rows_in, own, cols, block, height, len(ins)),
+        functools.partial(layer_kernel, cases, rows_in, own, cols, block, height, len(ins), back),
         out_shape=(
             jax.ShapeDtypeStruct((channels, (rows_in - 2) * row), BF16),
             jax.ShapeDtypeStruct((channels, rows_in * row), BF16),
@@ -207,17 +214,16 @@
         value = value.reshape(-1, block, own, cols, channels)
         return value.transpose(0, 4, 2, 1, 3).reshape(-1, channels, own * row)
 
-    first = lanes(jnp.concatenate([cache_in[0], video_in[:block]], axis=0))
+    first = lanes(jnp.concatenate([cache_in[0], video_in[:2 * block]], axis=0))
     first_below = moved(first[..., :2 * row], [(g, g) for g in evens], -1)
     first_above = moved(first[..., (own - 2) * row:], [(g, g) for g in evens], 1)
     place, weight = lax.optimization_barrier((place, conv_weight[0]))
     cuts = ((1, (own - 1) * row, row), (1, 0, row))
     weight, bias, gain, later, odd_last, odd_first = turned_weights(
-        weight, conv_bias, norm_gain, lanes(video_in[block:]), first, cuts)
+        weight, conv_bias, norm_gain, lanes(video_in[2 * block:]), first, cuts)
     odd_above = moved(odd_last, [(g, g) for g in odds], 1)
     odd_below = moved(odd_first, [(g, g) for g in odds], -1)
     later_below = moved(later[..., :2 * row], [(0, 0)], -1)
-    later_above = moved(later[..., (own - 2) * row:], [(0, 0)], 1)
     fixed = (weight, bias, gain)
 
     call = functools.partial(layer_call, own=own, cols=cols, block=block, height=height, place=place)
@@ -238,41 +244,54 @@
         cases = []
         for p in busy:
             b = tick - LAG * p
-            if p == 0 and b == 0:
-                parts = [(1, 1, 0, 2), (0, 1, 0, own), (2, 1, 0, 2)]
+            if p == 0 and b < 2:
+                parts = [(1, b + 1, 0, 2), (0, b + 1, 0, own), (2, b + 1, 0, 2)]
             else:
                 n = len(ins)
                 if p == 0:
                     ins += [later, later_above, later_below]
-                    parts = [(n + 1, b - 1, 0, 2), (n, b - 1, 0, own), (n + 2, b - 1, 0, 2)]
+                    parts = [(n + 1, b - 2, 0, 2), (n, b - 2, 0, own), (n + 2, b - 2, 0, 2)]
                 else:
                     ins += list(arrived[b])
                     parts = [(n + 1, None, 0, 2), (n, None, 0, own), (n + 2, None, 0, 2)]
             cases.append((2 * p, parts, old if b == 0 else kept))
         if tick == 0:
             ins += [odd_above, odd_below]
+        back = None
         if tick == ticks - 1:
-            ins.append(done[-2])
-        out, even_acts, *fixed = call(cases, own + 4, fixed=fixed, ins=ins)
+            back = (segments - 1, len(ins))
+            ins.append(out)
+        out, even_acts, *fixed = call(cases, own + 4, fixed=fixed, ins=ins, back=back)
+        sent = list(arrived[tick - 1]) if 0 < tick <= blocks else []
+        if tick == 1:
+            sent.append(later_below)
+        if tick == ticks - 2:
+            sent += done
+        out, *sent = lax.optimization_barrier((out, *sent))
+        if tick == ticks - 2:
+            done = sent[len(sent) - len(done):]
         if 0 < tick <= blocks:
-            out, *arrived[tick - 1] = lax.optimization_barrier((out, *arrived[tick - 1]))
+            arrived[tick - 1] = sent[:3]
+        if tick == 1:
+            later_below = sent[3]
         crossed = moved(out, across, 0)
+        if tick == 1:
+            crossed, above = lax.optimization_barrier((crossed, later[..., (own - 2) * row:]))
+            later_above = moved(above, [(0, 0)], 1)
+        if tick == ticks - 1:
+            done[-1] = crossed[:, :own * row]
 
         ins = [crossed, first, odd_above, odd_below]
         old = [(2, 0, 0, 1), (1, 0, 0, own), (3, 0, 0, 1)]
         if tick:
             ins.append(odd_acts)
-        if tick == 0:
-            ins += [later_above, later_below]
-        if tick >= ticks - 2:
-            ins.append(done[0] if tick < ticks - 1 else done[-1])
         cases = [(2 * p + 1, [(0, None, 0, own + 2)], old if tick == LAG * p else [(4, None, 0, own + 2)]) for p in busy]
         out, odd_acts, *fixed = call(cases, own + 2, fixed=fixed, ins=ins)
         if tick < blocks:
             arrived.append((moved(out, hop, 0), moved(out[:, (own - 2) * row:], hop, 1), moved(out[:, :2 * row], hop, -1)))
         b = tick - LAG * (planes - 1)
         if 0 <= b < blocks:
-            done.append(out if b == segments - 1 else moved(out, [(segments - 1, b)], 0))
+            done.append(out if b >= segments - 2 else moved(out, [(segments - 1, b)], 0))
         for p in busy:
             if tick - LAG * p == blocks - 1:
                 even_cache[p] = even_acts[:, 2 * row:(2 + own) * row]

time: 118 us -> 119 us (level)
  waiting for transfers between devices: 9.03 us -> 14.7 us
  starting transfers between devices: 71.2 us -> 67.3 us
    ppermute x27 -> x26, waiting for transfers between devices: 9.03 us -> 14.7 us  [moved(): lax.ppermute(value, axes, [(a * slabs + s, b * slabs + s + step) for a, b...]
    ppermute x27 -> x26, starting transfers between devices: 71.2 us -> 67.3 us  [moved(): lax.ppermute(value, axes, [(a * slabs + s, b * slabs + s + step) for a, b...]
  transfers between devices with their start and end apart: 27 -> 26, of which waited for: 8 -> 8; matrix products, arithmetic and copies ran while one was open for 1% -> 0% of each run, Pallas kernels for 11% -> 11%
where the time goes in v5:
time: 119 us; the launch traced here: 118 us
  starting transfers between devices  67.3 us (57%)
  Pallas kernels  30.4 us (26%)
  waiting for transfers between devices  14.7 us (12%)
  local copies, waits for them, and re-layouts  3.47 us (3%)
    ppermute x26, starting transfers between devices, moved(): lax.ppermute(value, axes, [(a * slabs + s, b * slabs + s + step) for a, b...  67.3 us
    pallas_call x12, Pallas kernels, layer_call(): pl.pallas_call(functools.partial(layer_kernel, cases, rows_in, own, cols,...  26.2 us
    ppermute x26, waiting for transfers between devices, moved(): lax.ppermute(value, axes, [(a * slabs + s, b * slabs + s + step) for a, b...  14.7 us
    pallas_call x1, Pallas kernels, turned_weights(): pl.pallas_call(functools.partial(turn_kernel, cuts), out_shape=(jax.Shape...  4.16 us
  transfers between devices with their start and end apart: 26, of which 8 were waited for; matrix products, arithmetic and copies ran while one was open for 0% of the time, Pallas kernels for 11%

profile of v5, /device:TPU:13, one launch (start us, length us, event | category | flops | bytes accessed | tf_op | source)
XLA Modules:
  0.0 118.2 jit_solution(2857398065210586217)
XLA Ops:
  0.6 1.2 %fusion = (bf16[4,2,64,384]{3,2,1,0:T(8,128)(2,1)S(1)}, bf16[4,2,64,384]{3,2,1,0:T(8,128)(2,1)S(1)}) fusion(bf16[8,2,64,384]{3,2,1,0:T(8,128)(2,1)} %param.5), kind=kLoop, calls=%fused_computation.4 | loop fusion | bytes 1572864 | tf_op jit(solution)/shard_map/slice | solution.py:217
  1.8 1.0 pad_maximum_fusion
  4.9 4.2 %shard_map.68 = (bf16[3,384,3456]{2,1,0:T(8,128)(2,1)S(1)}, f32[384,1]{1,0:T(8,128)S(1)}, f32[384,1]{1,0:T(8,128)S(1)}, bf16[2,384,256]{2,1,0:T(8,128)(2,1)S(1)}...) custom-call(bf16[3,3,3,384,384]{4,3,2,1,0:T(8,128)(2,1)} %bitcast.20, ...), custom_call_target="tpu_custom_call", output_to_operand_aliasing={{3}: (3, {})} | custom-call | bytes 15925248 | tf_op jit(solution)/shard_map/pallas_call | solution.py:42
  9.1 3.1 %collective-permute-start.2 = (bf16[1,384,128]{2,1,0:T(8,128)(2,1)S(1)}, bf16[1,384,128]{2,1,0:T(8,128)(2,1)S(1)}, u32[]{:S(2)}, u32[]{:S(2)}) collective-permute-start(bf16[1,384,128]{2,1,0:T(8,128)(2,1)S(1)} %get-tuple-element.95), channel_id=1, source_target_pairs={{8,9},{9,10},{10,11},{11,12},{12,13},{13,14},{14,15},{24,25},{25,2... | collective-permute-start | bytes 294920 | tf_op jit(solution)/shard_map/ppermute | solution.py:210
  12.2 3.1 %collective-permute-start.3 = (bf16[1,384,128]{2,1,0:T(8,128)(2,1)S(1)}, bf16[1,384,128]{2,1,0:T(8,128)(2,1)S(1)}, u32[]{:S(2)}, u32[]{:S(2)}) collective-permute-start(bf16[1,384,128]{2,1,0:T(8,128)(2,1)S(1)} %get-tuple-element.96), channel_id=1, source_target_pairs={{9,8},{10,9},{11,10},{12,11},{13,12},{14,13},{15,14},{25,24},{26,2... | collective-permute-start | bytes 294920 | tf_op jit(solution)/shard_map/ppermute | solution.py:210
  15.3 6.7 %collective-permute-done.2.refs_3_.refs_2_ = bf16[1,384,128]{2,1,0:T(8,128)(2,1)S(1)} collective-permute-done((bf16[1,384,128]{2,1,0:T(8,128)(2,1)S(1)}, bf16[1,384,128]{2,1,0:T(8,128)(2,1)S(1)}, u32[]{:S(2)}, u32[]{:S(2)}) %collective-permute-start.2) | collective-permute-done | bytes 98336 | tf_op jit(solution)/shard_map/ppermute | solution.py:210
  22.6 3.1 %collective-permute-start.4 = (bf16[384,512]{1,0:T(8,128)(2,1)S(1)}, bf16[384,512]{1,0:T(8,128)(2,1)S(1)}, u32[]{:S(2)}, u32[]{:S(2)}) collective-permute-start(bf16[384,512]{1,0:T(8,128)(2,1)S(1)} %get-tuple-element.100), channel_id=1, source_target_pairs={{0,8},{1,9},{2,10},{3,11},{4,12},{5,13},{6,14},{7,15},{8,0},{9,1},... | collective-permute-start | bytes 1179656 | tf_op jit(solution)/shard_map/ppermute | solution.py:210
  30.3 18.5 %collective-permute-start.9 = (bf16[384,512]{1,0:T(8,128)(2,1)S(1)}, bf16[384,512]{1,0:T(8,128)(2,1)S(1)}, u32[]{:S(2)}, u32[]{:S(2)}) collective-permute-start(bf16[384,512]{1,0:T(8,128)(2,1)S(1)} %get-tuple-element.111), channel_id=1, source_target_pairs={{0,8},{1,9},{2,10},{3,11},{4,12},{5,13},{6,14},{7,15},{8,0},{9,1},... | collective-permute-start | bytes 1179656 | tf_op jit(solution)/shard_map/ppermute | solution.py:210
  48.8 1.3 %collective-permute-done.9.refs_0_ = bf16[384,512]{1,0:T(8,128)(2,1)S(1)} collective-permute-done((bf16[384,512]{1,0:T(8,128)(2,1)S(1)}, bf16[384,512]{1,0:T(8,128)(2,1)S(1)}, u32[]{:S(2)}, u32[]{:S(2)}) %collective-permute-start.9) | collective-permute-done | bytes 393248 | tf_op jit(solution)/shard_map/ppermute | solution.py:210
  50.8 0.8 shard_map.72
  54.4 10.4 %collective-permute-start.14 = (bf16[384,512]{1,0:T(8,128)(2,1)S(1)}, bf16[384,512]{1,0:T(8,128)(2,1)S(1)}, u32[]{:S(2)}, u32[]{:S(2)}) collective-permute-start(bf16[384,512]{1,0:T(8,128)(2,1)S(1)} %get-tuple-element.128), channel_id=1, source_target_pairs={{0,8},{1,9},{2,10},{3,11},{4,12},{5,13},{6,14},{7,15},{8,0},{9,1},... | collective-permute-start | bytes 1179656 | tf_op jit(solution)/shard_map/ppermute | solution.py:210
  64.7 1.3 %collective-permute-done.14.refs_0_ = bf16[384,512]{1,0:T(8,128)(2,1)S(1)} collective-permute-done((bf16[384,512]{1,0:T(8,128)(2,1)S(1)}, bf16[384,512]{1,0:T(8,128)(2,1)S(1)}, u32[]{:S(2)}, u32[]{:S(2)}) %collective-permute-start.14) | collective-permute-done | bytes 393248 | tf_op jit(solution)/shard_map/ppermute | solution.py:210
  66.1 5.1 %shard_map.74 = (bf16[384,256]{1,0:T(8,128)(2,1)S(1)}, bf16[384,512]{1,0:T(8,128)(2,1)S(1)}, bf16[3,384,3456]{2,1,0:T(8,128)(2,1)S(1)}, f32[384,1]{1,0:T(8,128)S(1)}, f32[384,1]{1,0:T(8,128)S(1)}) custom-call(s32[2]{0:T(128)S(1)} %pad_add_fusion.place_ref, ...), custom_call_target="tpu_custom_call", output_to_operand_aliasing={{2}: (1, {}), {3}: (2, {}), {4}: (3, {})} | custom-call | flops 2038431744 | tf_op jit(solution)/shard_map/pallas_call | solution.py:172
  73.9 10.0 %collective-permute-start.18 = (bf16[384,512]{1,0:T(8,128)(2,1)S(1)}, bf16[384,512]{1,0:T(8,128)(2,1)S(1)}, u32[]{:S(2)}, u32[]{:S(2)}) collective-permute-start(bf16[384,512]{1,0:T(8,128)(2,1)S(1)} %get-tuple-element.142), channel_id=1, source_target_pairs={{0,8},{1,9},{2,10},{3,11},{4,12},{5,13},{6,14},{7,15},{8,0},{9,1},... | collective-permute-start | bytes 1179656 | tf_op jit(solution)/shard_map/ppermute | solution.py:210
  84.0 1.3 %collective-permute-start.22 = (bf16[384,256]{1,0:T(8,128)(2,1)S(1)}, bf16[384,256]{1,0:T(8,128)(2,1)S(1)}, u32[]{:S(2)}, u32[]{:S(2)}) collective-permute-start(bf16[384,256]{1,0:T(8,128)(2,1)S(1)} %get-tuple-element.141), channel_id=1, source_target_pairs={{24,0},{25,1},{26,2},{27,3},{28,4},{29,5},{30,6},{31,7}} | collective-permute-start | bytes 589832 | tf_op jit(solution)/shard_map/ppermute | solution.py:210
  85.3 5.5 %shard_map.76 = (bf16[384,256]{1,0:T(8,128)(2,1)S(1)}, bf16[384,512]{1,0:T(8,128)(2,1)S(1)}, bf16[3,384,3456]{2,1,0:T(8,128)(2,1)S(1)}, f32[384,1]{1,0:T(8,128)S(1)}, f32[384,1]{1,0:T(8,128)S(1)}) custom-call(s32[2]{0:T(128)S(1)} %pad_add_fusion.place_ref, ...), custom_call_target="tpu_custom_call", output_to_operand_aliasing={{2}: (1, {}), {3}: (2, {}), {4}: (3, {})} | custom-call | flops 2038431744 | tf_op jit(solution)/shard_map/pallas_call | solution.py:172
  92.8 3.0 %collective-permute-start.23 = (bf16[384,256]{1,0:T(8,128)(2,1)S(1)}, bf16[384,256]{1,0:T(8,128)(2,1)S(1)}, u32[]{:S(2)}, u32[]{:S(2)}) collective-permute-start(bf16[384,256]{1,0:T(8,128)(2,1)S(1)} %get-tuple-element.155), channel_id=1, source_target_pairs={{24,8},{25,9},{26,10},{27,11},{28,12},{29,13},{30,14},{31,15}} | collective-permute-start | bytes 589832 | tf_op jit(solution)/shard_map/ppermute | solution.py:210
  96.6 1.9 %collective-permute-done.23 = bf16[384,256]{1,0:T(8,128)(2,1)S(1)} collective-permute-done((bf16[384,256]{1,0:T(8,128)(2,1)S(1)}, bf16[384,256]{1,0:T(8,128)(2,1)S(1)}, u32[]{:S(2)}, u32[]{:S(2)}) %collective-permute-start.23) | collective-permute-done | bytes 196640 | tf_op jit(solution)/shard_map/ppermute | solution.py:210
  98.5 0.9 collective-permute-start.24
  99.3 1.3 %collective-permute-done.24.refs_0_ = bf16[384,512]{1,0:T(8,128)(2,1)S(1)} collective-permute-done((bf16[384,512]{1,0:T(8,128)(2,1)S(1)}, bf16[384,512]{1,0:T(8,128)(2,1)S(1)}, u32[]{:S(2)}, u32[]{:S(2)}) %collective-permute-start.24) | collective-permute-done | bytes 393248 | tf_op jit(solution)/shard_map/ppermute | solution.py:210
  100.7 5.2 %shard_map.78 = (bf16[384,256]{1,0:T(8,128)(2,1)S(1)}, bf16[384,512]{1,0:T(8,128)(2,1)S(1)}, bf16[3,384,3456]{2,1,0:T(8,128)(2,1)S(1)}, f32[384,1]{1,0:T(8,128)S(1)}, f32[384,1]{1,0:T(8,128)S(1)}) custom-call(s32[2]{0:T(128)S(1)} %pad_add_fusion.place_ref, ...), custom_call_target="tpu_custom_call", output_to_operand_aliasing={{2}: (1, {}), {3}: (2, {}), {4}: (3, {})} | custom-call | flops 2038431744 | tf_op jit(solution)/shard_map/pallas_call | solution.py:172
  106.6 3.1 %collective-permute-start.25 = (bf16[384,512]{1,0:T(8,128)(2,1)S(1)}, bf16[384,512]{1,0:T(8,128)(2,1)S(1)}, u32[]{:S(2)}, u32[]{:S(2)}) collective-permute-start(bf16[384,512]{1,0:T(8,128)(2,1)S(1)} %get-tuple-element.169), channel_id=1, source_target_pairs={{0,8},{1,9},{2,10},{3,11},{4,12},{5,13},{6,14},{7,15},{8,0},{9,1},... | collective-permute-start | bytes 1179656 | tf_op jit(solution)/shard_map/ppermute | solution.py:210
  109.7 1.3 %collective-permute-done.25.refs_0_ = bf16[384,512]{1,0:T(8,128)(2,1)S(1)} collective-permute-done((bf16[384,512]{1,0:T(8,128)(2,1)S(1)}, bf16[384,512]{1,0:T(8,128)(2,1)S(1)}, u32[]{:S(2)}, u32[]{:S(2)}) %collective-permute-start.25) | collective-permute-done | bytes 393248 | tf_op jit(solution)/shard_map/ppermute | solution.py:210
  111.1 5.2 %shard_map.80 = (bf16[384,256]{1,0:T(8,128)(2,1)S(1)}, bf16[384,512]{1,0:T(8,128)(2,1)S(1)}, bf16[3,384,3456]{2,1,0:T(8,128)(2,1)S(1)}, f32[384,1]{1,0:T(8,128)S(1)}, f32[384,1]{1,0:T(8,128)S(1)}) custom-call(s32[2]{0:T(128)S(1)} %pad_add_fusion.place_ref, ...), custom_call_target="tpu_custom_call", output_to_operand_aliasing={{2}: (1, {}), {3}: (2, {}), {4}: (3, {})} | custom-call | flops 2038431744 | tf_op jit(solution)/shard_map/pallas_call | solution.py:172
  (57 shorter events, 18.5 us)
Async XLA Ops:
  3.2 18.8 %collective-permute-start = (bf16[3,384,256]{2,1,0:T(8,128)(2,1)S(1)}, bf16[3,384,256]{2,1,0:T(8,128)(2,1)S(1)}, u32[]{:S(2)}, u32[]{:S(2)}) collective-permute-start(bf16[3,384,256]{2,1,0:T(8,128)(2,1)S(1)} %copy.71.first_ref.refs_0_.refs_1_), channel_id=1, source_target_pairs={{0,1},{1,2},{2,3},{3,4},{4,5},{5,6},{6,7},{16,17},{17,18},{18,19},... | collective-permute-start | bytes 1769480 | tf_op jit(solution)/shard_map/ppermute | solution.py:210
  3.9 18.1 %collective-permute-start.1 = (bf16[3,384,256]{2,1,0:T(8,128)(2,1)S(1)}, bf16[3,384,256]{2,1,0:T(8,128)(2,1)S(1)}, u32[]{:S(2)}, u32[]{:S(2)}) collective-permute-start(bf16[3,384,256]{2,1,0:T(8,128)(2,1)S(1)} %copy.71.first_ref.refs_0_.refs_1_), channel_id=1, source_target_pairs={{1,0},{2,1},{3,2},{4,3},{5,4},{6,5},{7,6},{17,16},{18,17},{19,18},... | collective-permute-start | bytes 1769480 | tf_op jit(solution)/shard_map/ppermute | solution.py:210
  9.1 12.9 %collective-permute-start.2 = (bf16[1,384,128]{2,1,0:T(8,128)(2,1)S(1)}, bf16[1,384,128]{2,1,0:T(8,128)(2,1)S(1)}, u32[]{:S(2)}, u32[]{:S(2)}) collective-permute-start(bf16[1,384,128]{2,1,0:T(8,128)(2,1)S(1)} %get-tuple-element.95), channel_id=1, source_target_pairs={{8,9},{9,10},{10,11},{11,12},{12,13},{13,14},{14,15},{24,25},{25,2... | collective-permute-start | bytes 294920 | tf_op jit(solution)/shard_map/ppermute | solution.py:210
  12.2 9.7 %collective-permute-start.3 = (bf16[1,384,128]{2,1,0:T(8,128)(2,1)S(1)}, bf16[1,384,128]{2,1,0:T(8,128)(2,1)S(1)}, u32[]{:S(2)}, u32[]{:S(2)}) collective-permute-start(bf16[1,384,128]{2,1,0:T(8,128)(2,1)S(1)} %get-tuple-element.96), channel_id=1, source_target_pairs={{9,8},{10,9},{11,10},{12,11},{13,12},{14,13},{15,14},{25,24},{26,2... | collective-permute-start | bytes 294920 | tf_op jit(solution)/shard_map/ppermute | solution.py:210
  22.6 4.4 %collective-permute-start.4 = (bf16[384,512]{1,0:T(8,128)(2,1)S(1)}, bf16[384,512]{1,0:T(8,128)(2,1)S(1)}, u32[]{:S(2)}, u32[]{:S(2)}) collective-permute-start(bf16[384,512]{1,0:T(8,128)(2,1)S(1)} %get-tuple-element.100), channel_id=1, source_target_pairs={{0,8},{1,9},{2,10},{3,11},{4,12},{5,13},{6,14},{7,15},{8,0},{9,1},... | collective-permute-start | bytes 1179656 | tf_op jit(solution)/shard_map/ppermute | solution.py:210
  25.6 4.7 %collective-permute-start.8 = (bf16[2,384,256]{2,1,0:T(8,128)(2,1)S(1)}, bf16[2,384,256]{2,1,0:T(8,128)(2,1)S(1)}, u32[]{:S(2)}, u32[]{:S(2)}) collective-permute-start(bf16[2,384,256]{2,1,0:T(8,128)(2,1)S(1)} %get-tuple-element.118.refs_4_), channel_id=1, source_target_pairs={{1,0},{2,1},{3,2},{4,3},{5,4},{6,5},{7,6}} | collective-permute-start | bytes 1179656 | tf_op jit(solution)/shard_map/ppermute | solution.py:210
  27.6 2.7 %collective-permute-start.5 = (bf16[384,256]{1,0:T(8,128)(2,1)S(1)}, bf16[384,256]{1,0:T(8,128)(2,1)S(1)}, u32[]{:S(2)}, u32[]{:S(2)}) collective-permute-start(bf16[384,256]{1,0:T(8,128)(2,1)S(1)} %get-tuple-element.109), channel_id=1, source_target_pairs={{8,16},{9,17},{10,18},{11,19},{12,20},{13,21},{14,22},{15,23}} | collective-permute-start | bytes 589832 | tf_op jit(solution)/shard_map/ppermute | solution.py:210
  28.3 2.0 %collective-permute-start.6 = (bf16[384,256]{1,0:T(8,128)(2,1)S(1)}, bf16[384,256]{1,0:T(8,128)(2,1)S(1)}, u32[]{:S(2)}, u32[]{:S(2)}) collective-permute-start(bf16[384,256]{1,0:T(8,128)(2,1)S(1)} %get-tuple-element.109), channel_id=1, source_target_pairs={{8,17},{9,18},{10,19},{11,20},{12,21},{13,22},{14,23}} | collective-permute-start | bytes 589832 | tf_op jit(solution)/shard_map/ppermute | solution.py:210
  30.3 19.8 %collective-permute-start.9 = (bf16[384,512]{1,0:T(8,128)(2,1)S(1)}, bf16[384,512]{1,0:T(8,128)(2,1)S(1)}, u32[]{:S(2)}, u32[]{:S(2)}) collective-permute-start(bf16[384,512]{1,0:T(8,128)(2,1)S(1)} %get-tuple-element.111), channel_id=1, source_target_pairs={{0,8},{1,9},{2,10},{3,11},{4,12},{5,13},{6,14},{7,15},{8,0},{9,1},... | collective-permute-start | bytes 1179656 | tf_op jit(solution)/shard_map/ppermute | solution.py:210
  50.2 3.5 %collective-permute-start.10 = (bf16[2,384,256]{2,1,0:T(8,128)(2,1)S(1)}, bf16[2,384,256]{2,1,0:T(8,128)(2,1)S(1)}, u32[]{:S(2)}, u32[]{:S(2)}) collective-permute-start(bf16[2,384,256]{2,1,0:T(8,128)(2,1)S(1)} %get-tuple-element.118.refs_4_), channel_id=1, source_target_pairs={{0,1},{1,2},{2,3},{3,4},{4,5},{5,6},{6,7}} | collective-permute-start | bytes 1179656 | tf_op jit(solution)/shard_map/ppermute | solution.py:210
  51.6 2.7 %collective-permute-start.11 = (bf16[384,256]{1,0:T(8,128)(2,1)S(1)}, bf16[384,256]{1,0:T(8,128)(2,1)S(1)}, u32[]{:S(2)}, u32[]{:S(2)}) collective-permute-start(bf16[384,256]{1,0:T(8,128)(2,1)S(1)} %get-tuple-element.127), channel_id=1, source_target_pairs={{8,16},{9,17},{10,18},{11,19},{12,20},{13,21},{14,22},{15,23}} | collective-permute-start | bytes 589832 | tf_op jit(solution)/shard_map/ppermute | solution.py:210
  52.3 2.0 %collective-permute-start.12 = (bf16[384,256]{1,0:T(8,128)(2,1)S(1)}, bf16[384,256]{1,0:T(8,128)(2,1)S(1)}, u32[]{:S(2)}, u32[]{:S(2)}) collective-permute-start(bf16[384,256]{1,0:T(8,128)(2,1)S(1)} %get-tuple-element.127), channel_id=1, source_target_pairs={{8,17},{9,18},{10,19},{11,20},{12,21},{13,22},{14,23}} | collective-permute-start | bytes 589832 | tf_op jit(solution)/shard_map/ppermute | solution.py:210
  53.0 1.4 %collective-permute-start.13 = (bf16[384,256]{1,0:T(8,128)(2,1)S(1)}, bf16[384,256]{1,0:T(8,128)(2,1)S(1)}, u32[]{:S(2)}, u32[]{:S(2)}) collective-permute-start(bf16[384,256]{1,0:T(8,128)(2,1)S(1)} %get-tuple-element.127), channel_id=1, source_target_pairs={{9,16},{10,17},{11,18},{12,19},{13,20},{14,21},{15,22}} | collective-permute-start | bytes 589832 | tf_op jit(solution)/shard_map/ppermute | solution.py:210
  54.4 11.7 %collective-permute-start.14 = (bf16[384,512]{1,0:T(8,128)(2,1)S(1)}, bf16[384,512]{1,0:T(8,128)(2,1)S(1)}, u32[]{:S(2)}, u32[]{:S(2)}) collective-permute-start(bf16[384,512]{1,0:T(8,128)(2,1)S(1)} %get-tuple-element.128), channel_id=1, source_target_pairs={{0,8},{1,9},{2,10},{3,11},{4,12},{5,13},{6,14},{7,15},{8,0},{9,1},... | collective-permute-start | bytes 1179656 | tf_op jit(solution)/shard_map/ppermute | solution.py:210
  71.2 2.7 %collective-permute-start.15 = (bf16[384,256]{1,0:T(8,128)(2,1)S(1)}, bf16[384,256]{1,0:T(8,128)(2,1)S(1)}, u32[]{:S(2)}, u32[]{:S(2)}) collective-permute-start(bf16[384,256]{1,0:T(8,128)(2,1)S(1)} %get-tuple-element.141), channel_id=1, source_target_pairs={{8,16},{9,17},{10,18},{11,19},{12,20},{13,21},{14,22},{15,23}} | collective-permute-start | bytes 589832 | tf_op jit(solution)/shard_map/ppermute | solution.py:210
  71.9 2.0 %collective-permute-start.16 = (bf16[384,256]{1,0:T(8,128)(2,1)S(1)}, bf16[384,256]{1,0:T(8,128)(2,1)S(1)}, u32[]{:S(2)}, u32[]{:S(2)}) collective-permute-start(bf16[384,256]{1,0:T(8,128)(2,1)S(1)} %get-tuple-element.141), channel_id=1, source_target_pairs={{8,17},{9,18},{10,19},{11,20},{12,21},{13,22},{14,23}} | collective-permute-start | bytes 589832 | tf_op jit(solution)/shard_map/ppermute | solution.py:210
  73.9 11.4 %collective-permute-start.18 = (bf16[384,512]{1,0:T(8,128)(2,1)S(1)}, bf16[384,512]{1,0:T(8,128)(2,1)S(1)}, u32[]{:S(2)}, u32[]{:S(2)}) collective-permute-start(bf16[384,512]{1,0:T(8,128)(2,1)S(1)} %get-tuple-element.142), channel_id=1, source_target_pairs={{0,8},{1,9},{2,10},{3,11},{4,12},{5,13},{6,14},{7,15},{8,0},{9,1},... | collective-permute-start | bytes 1179656 | tf_op jit(solution)/shard_map/ppermute | solution.py:210
  84.0 12.6 %collective-permute-start.22 = (bf16[384,256]{1,0:T(8,128)(2,1)S(1)}, bf16[384,256]{1,0:T(8,128)(2,1)S(1)}, u32[]{:S(2)}, u32[]{:S(2)}) collective-permute-start(bf16[384,256]{1,0:T(8,128)(2,1)S(1)} %get-tuple-element.141), channel_id=1, source_target_pairs={{24,0},{25,1},{26,2},{27,3},{28,4},{29,5},{30,6},{31,7}} | collective-permute-start | bytes 589832 | tf_op jit(solution)/shard_map/ppermute | solution.py:210
  90.8 5.8 %collective-permute-start.19 = (bf16[384,256]{1,0:T(8,128)(2,1)S(1)}, bf16[384,256]{1,0:T(8,128)(2,1)S(1)}, u32[]{:S(2)}, u32[]{:S(2)}) collective-permute-start(bf16[384,256]{1,0:T(8,128)(2,1)S(1)} %get-tuple-element.155), channel_id=1, source_target_pairs={{8,16},{9,17},{10,18},{11,19},{12,20},{13,21},{14,22},{15,23}} | collective-permute-start | bytes 589832 | tf_op jit(solution)/shard_map/ppermute | solution.py:210
  91.5 5.1 %collective-permute-start.20 = (bf16[384,256]{1,0:T(8,128)(2,1)S(1)}, bf16[384,256]{1,0:T(8,128)(2,1)S(1)}, u32[]{:S(2)}, u32[]{:S(2)}) collective-permute-start(bf16[384,256]{1,0:T(8,128)(2,1)S(1)} %get-tuple-element.155), channel_id=1, source_target_pairs={{8,17},{9,18},{10,19},{11,20},{12,21},{13,22},{14,23}} | collective-permute-start | bytes 589832 | tf_op jit(solution)/shard_map/ppermute | solution.py:210
  92.1 4.4 %collective-permute-start.21 = (bf16[384,256]{1,0:T(8,128)(2,1)S(1)}, bf16[384,256]{1,0:T(8,128)(2,1)S(1)}, u32[]{:S(2)}, u32[]{:S(2)}) collective-permute-start(bf16[384,256]{1,0:T(8,128)(2,1)S(1)} %get-tuple-element.155), channel_id=1, source_target_pairs={{9,16},{10,17},{11,18},{12,19},{13,20},{14,21},{15,22}} | collective-permute-start | bytes 589832 | tf_op jit(solution)/shard_map/ppermute | solution.py:210
  92.8 5.6 %collective-permute-start.23 = (bf16[384,256]{1,0:T(8,128)(2,1)S(1)}, bf16[384,256]{1,0:T(8,128)(2,1)S(1)}, u32[]{:S(2)}, u32[]{:S(2)}) collective-permute-start(bf16[384,256]{1,0:T(8,128)(2,1)S(1)} %get-tuple-element.155), channel_id=1, source_target_pairs={{24,8},{25,9},{26,10},{27,11},{28,12},{29,13},{30,14},{31,15}} | collective-permute-start | bytes 589832 | tf_op jit(solution)/shard_map/ppermute | solution.py:210
  98.5 2.2 %collective-permute-start.24 = (bf16[384,512]{1,0:T(8,128)(2,1)S(1)}, bf16[384,512]{1,0:T(8,128)(2,1)S(1)}, u32[]{:S(2)}, u32[]{:S(2)}) collective-permute-start(bf16[384,512]{1,0:T(8,128)(2,1)S(1)} %get-tuple-element.156), channel_id=1, source_target_pairs={{0,8},{1,9},{2,10},{3,11},{4,12},{5,13},{6,14},{7,15},{8,0},{9,1},... | collective-permute-start | bytes 1179656 | tf_op jit(solution)/shard_map/ppermute | solution.py:210
  106.6 4.5 %collective-permute-start.25 = (bf16[384,512]{1,0:T(8,128)(2,1)S(1)}, bf16[384,512]{1,0:T(8,128)(2,1)S(1)}, u32[]{:S(2)}, u32[]{:S(2)}) collective-permute-start(bf16[384,512]{1,0:T(8,128)(2,1)S(1)} %get-tuple-element.169), channel_id=1, source_target_pairs={{0,8},{1,9},{2,10},{3,11},{4,12},{5,13},{6,14},{7,15},{8,0},{9,1},... | collective-permute-start | bytes 1179656 | tf_op jit(solution)/shard_map/ppermute | solution.py:210
  (4 other events, 86.0 us)

commit v6 on v5

--- a/solution.py
+++ b/solution.py
@@ -214,13 +214,13 @@
         value = value.reshape(-1, block, own, cols, channels)
         return value.transpose(0, 4, 2, 1, 3).reshape(-1, channels, own * row)
 
-    first = lanes(jnp.concatenate([cache_in[0], video_in[:2 * block]], axis=0))
+    first = lanes(jnp.concatenate([cache_in[0], video_in[:block]], axis=0))
     first_below = moved(first[..., :2 * row], [(g, g) for g in evens], -1)
     first_above = moved(first[..., (own - 2) * row:], [(g, g) for g in evens], 1)
     place, weight = lax.optimization_barrier((place, conv_weight[0]))
     cuts = ((1, (own - 1) * row, row), (1, 0, row))
     weight, bias, gain, later, odd_last, odd_first = turned_weights(
-        weight, conv_bias, norm_gain, lanes(video_in[2 * block:]), first, cuts)
+        weight, conv_bias, norm_gain, lanes(video_in[block:]), first, cuts)
     odd_above = moved(odd_last, [(g, g) for g in odds], 1)
     odd_below = moved(odd_first, [(g, g) for g in odds], -1)
     later_below = moved(later[..., :2 * row], [(0, 0)], -1)
@@ -244,13 +244,13 @@
         cases = []
         for p in busy:
             b = tick - LAG * p
-            if p == 0 and b < 2:
-                parts = [(1, b + 1, 0, 2), (0, b + 1, 0, own), (2, b + 1, 0, 2)]
+            if p == 0 and b == 0:
+                parts = [(1, 1, 0, 2), (0, 1, 0, own), (2, 1, 0, 2)]
             else:
                 n = len(ins)
                 if p == 0:
                     ins += [later, later_above, later_below]
-                    parts = [(n + 1, b - 2, 0, 2), (n, b - 2, 0, own), (n + 2, b - 2, 0, 2)]
+                    parts = [(n + 1, b - 1, 0, 2), (n, b - 1, 0, own), (n + 2, b - 1, 0, 2)]
                 else:
                     ins += list(arrived[b])
                     parts = [(n + 1, None, 0, 2), (n, None, 0, own), (n + 2, None, 0, 2)]
@@ -260,22 +260,22 @@
         back = None
         if tick == ticks - 1:
             back = (segments - 1, len(ins))
-            ins.append(out)
+            ins.append(done[-1])
         out, even_acts, *fixed = call(cases, own + 4, fixed=fixed, ins=ins, back=back)
         sent = list(arrived[tick - 1]) if 0 < tick <= blocks else []
-        if tick == 1:
-            sent.append(later_below)
-        if tick == ticks - 2:
-            sent += done
+        if tick == 0:
+            sent = [later_below]
+        elif tick == ticks - 1:
+            sent = done[:-1]
         out, *sent = lax.optimization_barrier((out, *sent))
-        if tick == ticks - 2:
-            done = sent[len(sent) - len(done):]
-        if 0 < tick <= blocks:
-            arrived[tick - 1] = sent[:3]
-        if tick == 1:
-            later_below = sent[3]
+        if tick == 0:
+            later_below, = sent
+        elif tick == ticks - 1:
+            done[:-1] = sent
+        elif tick <= blocks:
+            arrived[tick - 1] = sent
         crossed = moved(out, across, 0)
-        if tick == 1:
+        if tick == 0:
             crossed, above = lax.optimization_barrier((crossed, later[..., (own - 2) * row:]))
             later_above = moved(above, [(0, 0)], 1)
         if tick == ticks - 1:
@@ -291,7 +291,10 @@
             arrived.append((moved(out, hop, 0), moved(out[:, (own - 2) * row:], hop, 1), moved(out[:, :2 * row], hop, -1)))
         b = tick - LAG * (planes - 1)
         if 0 <= b < blocks:
-            done.append(out if b >= segments - 2 else moved(out, [(segments - 1, b)], 0))
+            done.append(out)
+            if b == segments - 2:
+                done = list(lax.optimization_barrier(tuple(done)))
+                done[:-1] = [moved(d, [(segments - 1, k)], 0) for k, d in enumerate(done[:-1])]
         for p in busy:
             if tick - LAG * p == blocks - 1:
                 even_cache[p] = even_acts[:, 2 * row:(2 + own) * row]

time: 119 us -> 125 us (1.050)
  starting transfers between devices: 67.3 us -> 73.9 us
    ppermute x26, starting transfers between devices: 67.3 us -> 73.9 us  [moved(): lax.ppermute(value, axes, [(a * slabs + s, b * slabs + s + step) for a, b...]
  transfers between devices with their start and end apart: 26 -> 26, of which waited for: 8 -> 10; matrix products, arithmetic and copies ran while one was open for 0% -> 1% of each run, Pallas kernels for 11% -> 7%
where the time goes in v6:
time: 125 us
  starting transfers between devices  73.9 us (59%)
  Pallas kernels  30.2 us (24%)
  waiting for transfers between devices  13.9 us (11%)
  local copies, waits for them, and re-layouts  4.34 us (3%)
    ppermute x26, starting transfers between devices, moved(): lax.ppermute(value, axes, [(a * slabs + s, b * slabs + s + step) for a, b...  73.9 us
    pallas_call x12, Pallas kernels, layer_call(): pl.pallas_call(functools.partial(layer_kernel, cases, rows_in, own, cols,...  26 us
    ppermute x26, waiting for transfers between devices, moved(): lax.ppermute(value, axes, [(a * slabs + s, b * slabs + s + step) for a, b...  13.9 us
    pallas_call x1, Pallas kernels, turned_weights(): pl.pallas_call(functools.partial(turn_kernel, cuts), out_shape=(jax.Shape...  4.16 us
  transfers between devices with their start and end apart: 26, of which 10 were waited for; matrix products, arithmetic and copies ran while one was open for 1% of the time, Pallas kernels for 7%

profile of v6, /device:TPU:13, one launch (start us, length us, event | category | flops | bytes accessed | tf_op | source)
XLA Modules:
  0.0 124.6 jit_solution(5347783374820676779)
XLA Ops:
  0.6 0.9 slice.22
  1.6 1.0 pad_maximum_fusion
  4.2 1.1 slice.21
  5.7 4.2 %shard_map.68 = (bf16[3,384,3456]{2,1,0:T(8,128)(2,1)S(1)}, f32[384,1]{1,0:T(8,128)S(1)}, f32[384,1]{1,0:T(8,128)S(1)}, bf16[3,384,256]{2,1,0:T(8,128)(2,1)S(1)}...) custom-call(bf16[3,3,3,384,384]{4,3,2,1,0:T(8,128)(2,1)} %bitcast.20, ...), custom_call_target="tpu_custom_call", output_to_operand_aliasing={{3}: (3, {})} | custom-call | bytes 15925248 | tf_op jit(solution)/shard_map/pallas_call | solution.py:42
  10.6 3.1 %collective-permute-start.2 = (bf16[1,384,128]{2,1,0:T(8,128)(2,1)S(1)}, bf16[1,384,128]{2,1,0:T(8,128)(2,1)S(1)}, u32[]{:S(2)}, u32[]{:S(2)}) collective-permute-start(bf16[1,384,128]{2,1,0:T(8,128)(2,1)S(1)} %get-tuple-element.100), channel_id=1, source_target_pairs={{8,9},{9,10},{10,11},{11,12},{12,13},{13,14},{14,15},{24,25},{25,2... | collective-permute-start | bytes 294920 | tf_op jit(solution)/shard_map/ppermute | solution.py:210
  13.7 3.1 %collective-permute-start.3 = (bf16[1,384,128]{2,1,0:T(8,128)(2,1)S(1)}, bf16[1,384,128]{2,1,0:T(8,128)(2,1)S(1)}, u32[]{:S(2)}, u32[]{:S(2)}) collective-permute-start(bf16[1,384,128]{2,1,0:T(8,128)(2,1)S(1)} %get-tuple-element.101), channel_id=1, source_target_pairs={{9,8},{10,9},{11,10},{12,11},{13,12},{14,13},{15,14},{25,24},{26,2... | collective-permute-start | bytes 294920 | tf_op jit(solution)/shard_map/ppermute | solution.py:210
  17.7 1.4 %collective-permute-done.3.refs_4_.refs_3_ = bf16[1,384,128]{2,1,0:T(8,128)(2,1)S(1)} collective-permute-done((bf16[1,384,128]{2,1,0:T(8,128)(2,1)S(1)}, bf16[1,384,128]{2,1,0:T(8,128)(2,1)S(1)}, u32[]{:S(2)}, u32[]{:S(2)}) %collective-permute-start.3) | collective-permute-done | bytes 98336 | tf_op jit(solution)/shard_map/ppermute | solution.py:210
  19.8 1.7 %collective-permute-done.5.refs_0_ = bf16[384,512]{1,0:T(8,128)(2,1)S(1)} collective-permute-done((bf16[384,512]{1,0:T(8,128)(2,1)S(1)}, bf16[384,512]{1,0:T(8,128)(2,1)S(1)}, u32[]{:S(2)}, u32[]{:S(2)}) %collective-permute-start.5) | collective-permute-done | bytes 393248 | tf_op jit(solution)/shard_map/ppermute | solution.py:210
  25.6 21.9 %collective-permute-start.10 = (bf16[384,512]{1,0:T(8,128)(2,1)S(1)}, bf16[384,512]{1,0:T(8,128)(2,1)S(1)}, u32[]{:S(2)}, u32[]{:S(2)}) collective-permute-start(bf16[384,512]{1,0:T(8,128)(2,1)S(1)} %get-tuple-element.120), channel_id=1, source_target_pairs={{0,8},{1,9},{2,10},{3,11},{4,12},{5,13},{6,14},{7,15},{8,0},{9,1},... | collective-permute-start | bytes 1179656 | tf_op jit(solution)/shard_map/ppermute | solution.py:210
  47.5 1.3 %collective-permute-done.10.refs_0_ = bf16[384,512]{1,0:T(8,128)(2,1)S(1)} collective-permute-done((bf16[384,512]{1,0:T(8,128)(2,1)S(1)}, bf16[384,512]{1,0:T(8,128)(2,1)S(1)}, u32[]{:S(2)}, u32[]{:S(2)}) %collective-permute-start.10) | collective-permute-done | bytes 393248 | tf_op jit(solution)/shard_map/ppermute | solution.py:210
  52.4 19.0 %collective-permute-start.14 = (bf16[384,512]{1,0:T(8,128)(2,1)S(1)}, bf16[384,512]{1,0:T(8,128)(2,1)S(1)}, u32[]{:S(2)}, u32[]{:S(2)}) collective-permute-start(bf16[384,512]{1,0:T(8,128)(2,1)S(1)} %get-tuple-element.134), channel_id=1, source_target_pairs={{0,8},{1,9},{2,10},{3,11},{4,12},{5,13},{6,14},{7,15},{8,0},{9,1},... | collective-permute-start | bytes 1179656 | tf_op jit(solution)/shard_map/ppermute | solution.py:210
  71.4 1.3 %collective-permute-done.14.refs_0_ = bf16[384,512]{1,0:T(8,128)(2,1)S(1)} collective-permute-done((bf16[384,512]{1,0:T(8,128)(2,1)S(1)}, bf16[384,512]{1,0:T(8,128)(2,1)S(1)}, u32[]{:S(2)}, u32[]{:S(2)}) %collective-permute-start.14) | collective-permute-done | bytes 393248 | tf_op jit(solution)/shard_map/ppermute | solution.py:210
  72.8 5.1 %shard_map.74 = (bf16[384,256]{1,0:T(8,128)(2,1)S(1)}, bf16[384,512]{1,0:T(8,128)(2,1)S(1)}, bf16[3,384,3456]{2,1,0:T(8,128)(2,1)S(1)}, f32[384,1]{1,0:T(8,128)S(1)}, f32[384,1]{1,0:T(8,128)S(1)}) custom-call(s32[2]{0:T(128)S(1)} %pad_add_fusion.place_ref, ...), custom_call_target="tpu_custom_call", output_to_operand_aliasing={{2}: (1, {}), {3}: (2, {}), {4}: (3, {})} | custom-call | flops 2038431744 | tf_op jit(solution)/shard_map/pallas_call | solution.py:172
  80.6 5.9 %collective-permute-start.18 = (bf16[384,512]{1,0:T(8,128)(2,1)S(1)}, bf16[384,512]{1,0:T(8,128)(2,1)S(1)}, u32[]{:S(2)}, u32[]{:S(2)}) collective-permute-start(bf16[384,512]{1,0:T(8,128)(2,1)S(1)} %get-tuple-element.148), channel_id=1, source_target_pairs={{0,8},{1,9},{2,10},{3,11},{4,12},{5,13},{6,14},{7,15},{8,0},{9,1},... | collective-permute-start | bytes 1179656 | tf_op jit(solution)/shard_map/ppermute | solution.py:210
  86.5 1.3 %collective-permute-done.18.refs_0_ = bf16[384,512]{1,0:T(8,128)(2,1)S(1)} collective-permute-done((bf16[384,512]{1,0:T(8,128)(2,1)S(1)}, bf16[384,512]{1,0:T(8,128)(2,1)S(1)}, u32[]{:S(2)}, u32[]{:S(2)}) %collective-permute-start.18) | collective-permute-done | bytes 393248 | tf_op jit(solution)/shard_map/ppermute | solution.py:210
  87.8 5.4 %shard_map.76 = (bf16[384,256]{1,0:T(8,128)(2,1)S(1)}, bf16[384,512]{1,0:T(8,128)(2,1)S(1)}, bf16[3,384,3456]{2,1,0:T(8,128)(2,1)S(1)}, f32[384,1]{1,0:T(8,128)S(1)}, f32[384,1]{1,0:T(8,128)S(1)}) custom-call(s32[2]{0:T(128)S(1)} %pad_add_fusion.place_ref, ...), custom_call_target="tpu_custom_call", output_to_operand_aliasing={{2}: (1, {}), {3}: (2, {}), {4}: (3, {})} | custom-call | flops 2038431744 | tf_op jit(solution)/shard_map/pallas_call | solution.py:172
  95.9 7.4 %collective-permute-start.22 = (bf16[384,512]{1,0:T(8,128)(2,1)S(1)}, bf16[384,512]{1,0:T(8,128)(2,1)S(1)}, u32[]{:S(2)}, u32[]{:S(2)}) collective-permute-start(bf16[384,512]{1,0:T(8,128)(2,1)S(1)} %get-tuple-element.162), channel_id=1, source_target_pairs={{0,8},{1,9},{2,10},{3,11},{4,12},{5,13},{6,14},{7,15},{8,0},{9,1},... | collective-permute-start | bytes 1179656 | tf_op jit(solution)/shard_map/ppermute | solution.py:210
  103.3 1.3 %collective-permute-done.22.refs_0_ = bf16[384,512]{1,0:T(8,128)(2,1)S(1)} collective-permute-done((bf16[384,512]{1,0:T(8,128)(2,1)S(1)}, bf16[384,512]{1,0:T(8,128)(2,1)S(1)}, u32[]{:S(2)}, u32[]{:S(2)}) %collective-permute-start.22) | collective-permute-done | bytes 393248 | tf_op jit(solution)/shard_map/ppermute | solution.py:210
  104.7 5.2 %shard_map.78 = (bf16[384,256]{1,0:T(8,128)(2,1)S(1)}, bf16[384,512]{1,0:T(8,128)(2,1)S(1)}, bf16[3,384,3456]{2,1,0:T(8,128)(2,1)S(1)}, f32[384,1]{1,0:T(8,128)S(1)}, f32[384,1]{1,0:T(8,128)S(1)}) custom-call(s32[2]{0:T(128)S(1)} %pad_add_fusion.place_ref, ...), custom_call_target="tpu_custom_call", output_to_operand_aliasing={{2}: (1, {}), {3}: (2, {}), {4}: (3, {})} | custom-call | flops 2038431744 | tf_op jit(solution)/shard_map/pallas_call | solution.py:172
  109.9 1.3 %collective-permute-start.23 = (bf16[384,256]{1,0:T(8,128)(2,1)S(1)}, bf16[384,256]{1,0:T(8,128)(2,1)S(1)}, u32[]{:S(2)}, u32[]{:S(2)}) collective-permute-start(bf16[384,256]{1,0:T(8,128)(2,1)S(1)} %get-tuple-element.177), channel_id=1, source_target_pairs={{24,0},{25,1},{26,2},{27,3},{28,4},{29,5},{30,6},{31,7}} | collective-permute-start | bytes 589832 | tf_op jit(solution)/shard_map/ppermute | solution.py:210
  111.2 1.3 %collective-permute-start.24 = (bf16[384,256]{1,0:T(8,128)(2,1)S(1)}, bf16[384,256]{1,0:T(8,128)(2,1)S(1)}, u32[]{:S(2)}, u32[]{:S(2)}) collective-permute-start(bf16[384,256]{1,0:T(8,128)(2,1)S(1)} %get-tuple-element.178), channel_id=1, source_target_pairs={{24,8},{25,9},{26,10},{27,11},{28,12},{29,13},{30,14},{31,15}} | collective-permute-start | bytes 589832 | tf_op jit(solution)/shard_map/ppermute | solution.py:210
  113.8 2.1 %collective-permute-done.24 = bf16[384,256]{1,0:T(8,128)(2,1)S(1)} collective-permute-done((bf16[384,256]{1,0:T(8,128)(2,1)S(1)}, bf16[384,256]{1,0:T(8,128)(2,1)S(1)}, u32[]{:S(2)}, u32[]{:S(2)}) %collective-permute-start.24) | collective-permute-done | bytes 196640 | tf_op jit(solution)/shard_map/ppermute | solution.py:210
  115.9 1.7 %collective-permute-done.25.refs_0_ = bf16[384,512]{1,0:T(8,128)(2,1)S(1)} collective-permute-done((bf16[384,512]{1,0:T(8,128)(2,1)S(1)}, bf16[384,512]{1,0:T(8,128)(2,1)S(1)}, u32[]{:S(2)}, u32[]{:S(2)}) %collective-permute-start.25) | collective-permute-done | bytes 393248 | tf_op jit(solution)/shard_map/ppermute | solution.py:210
  117.6 5.2 %shard_map.80 = (bf16[384,256]{1,0:T(8,128)(2,1)S(1)}, bf16[384,512]{1,0:T(8,128)(2,1)S(1)}, bf16[3,384,3456]{2,1,0:T(8,128)(2,1)S(1)}, f32[384,1]{1,0:T(8,128)S(1)}, f32[384,1]{1,0:T(8,128)S(1)}) custom-call(s32[2]{0:T(128)S(1)} %pad_add_fusion.place_ref, ...), custom_call_target="tpu_custom_call", output_to_operand_aliasing={{2}: (1, {}), {3}: (2, {}), {4}: (3, {})} | custom-call | flops 2038431744 | tf_op jit(solution)/shard_map/pallas_call | solution.py:172
  (58 shorter events, 20.2 us)
Async XLA Ops:
  2.8 16.3 %collective-permute-start.1 = (bf16[2,384,256]{2,1,0:T(8,128)(2,1)S(1)}, bf16[2,384,256]{2,1,0:T(8,128)(2,1)S(1)}, u32[]{:S(2)}, u32[]{:S(2)}) collective-permute-start(bf16[2,384,256]{2,1,0:T(8,128)(2,1)S(1)} %copy.71.first_ref.refs_0_.refs_1_), channel_id=1, source_target_pairs={{1,0},{2,1},{3,2},{4,3},{5,4},{6,5},{7,6},{17,16},{18,17},{19,18},... | collective-permute-start | bytes 1179656 | tf_op jit(solution)/shard_map/ppermute | solution.py:210
  3.5 15.6 %collective-permute-start = (bf16[2,384,256]{2,1,0:T(8,128)(2,1)S(1)}, bf16[2,384,256]{2,1,0:T(8,128)(2,1)S(1)}, u32[]{:S(2)}, u32[]{:S(2)}) collective-permute-start(bf16[2,384,256]{2,1,0:T(8,128)(2,1)S(1)} %copy.71.first_ref.refs_0_.refs_1_), channel_id=1, source_target_pairs={{0,1},{1,2},{2,3},{3,4},{4,5},{5,6},{6,7},{16,17},{17,18},{18,19},... | collective-permute-start | bytes 1179656 | tf_op jit(solution)/shard_map/ppermute | solution.py:210
  9.9 9.8 %collective-permute-start.4 = (bf16[3,384,256]{2,1,0:T(8,128)(2,1)S(1)}, bf16[3,384,256]{2,1,0:T(8,128)(2,1)S(1)}, u32[]{:S(2)}, u32[]{:S(2)}) collective-permute-start(bf16[3,384,256]{2,1,0:T(8,128)(2,1)S(1)} %get-tuple-element.113.refs_4_), channel_id=1, source_target_pairs={{1,0},{2,1},{3,2},{4,3},{5,4},{6,5},{7,6}} | collective-permute-start | bytes 1769480 | tf_op jit(solution)/shard_map/ppermute | solution.py:210
  10.6 7.1 %collective-permute-start.2 = (bf16[1,384,128]{2,1,0:T(8,128)(2,1)S(1)}, bf16[1,384,128]{2,1,0:T(8,128)(2,1)S(1)}, u32[]{:S(2)}, u32[]{:S(2)}) collective-permute-start(bf16[1,384,128]{2,1,0:T(8,128)(2,1)S(1)} %get-tuple-element.100), channel_id=1, source_target_pairs={{8,9},{9,10},{10,11},{11,12},{12,13},{13,14},{14,15},{24,25},{25,2... | collective-permute-start | bytes 294920 | tf_op jit(solution)/shard_map/ppermute | solution.py:210
  13.7 5.4 %collective-permute-start.3 = (bf16[1,384,128]{2,1,0:T(8,128)(2,1)S(1)}, bf16[1,384,128]{2,1,0:T(8,128)(2,1)S(1)}, u32[]{:S(2)}, u32[]{:S(2)}) collective-permute-start(bf16[1,384,128]{2,1,0:T(8,128)(2,1)S(1)} %get-tuple-element.101), channel_id=1, source_target_pairs={{9,8},{10,9},{11,10},{12,11},{13,12},{14,13},{15,14},{25,24},{26,2... | collective-permute-start | bytes 294920 | tf_op jit(solution)/shard_map/ppermute | solution.py:210
  19.7 1.8 %collective-permute-start.5 = (bf16[384,512]{1,0:T(8,128)(2,1)S(1)}, bf16[384,512]{1,0:T(8,128)(2,1)S(1)}, u32[]{:S(2)}, u32[]{:S(2)}) collective-permute-start(bf16[384,512]{1,0:T(8,128)(2,1)S(1)} %get-tuple-element.107), channel_id=1, source_target_pairs={{0,8},{1,9},{2,10},{3,11},{4,12},{5,13},{6,14},{7,15},{8,0},{9,1},... | collective-permute-start | bytes 1179656 | tf_op jit(solution)/shard_map/ppermute | solution.py:210
  21.5 3.4 %collective-permute-start.6 = (bf16[3,384,256]{2,1,0:T(8,128)(2,1)S(1)}, bf16[3,384,256]{2,1,0:T(8,128)(2,1)S(1)}, u32[]{:S(2)}, u32[]{:S(2)}) collective-permute-start(bf16[3,384,256]{2,1,0:T(8,128)(2,1)S(1)} %get-tuple-element.113.refs_4_), channel_id=1, source_target_pairs={{0,1},{1,2},{2,3},{3,4},{4,5},{5,6},{6,7}} | collective-permute-start | bytes 1769480 | tf_op jit(solution)/shard_map/ppermute | solution.py:210
  22.9 2.7 %collective-permute-start.9 = (bf16[384,256]{1,0:T(8,128)(2,1)S(1)}, bf16[384,256]{1,0:T(8,128)(2,1)S(1)}, u32[]{:S(2)}, u32[]{:S(2)}) collective-permute-start(bf16[384,256]{1,0:T(8,128)(2,1)S(1)} %get-tuple-element.119), channel_id=1, source_target_pairs={{9,16},{10,17},{11,18},{12,19},{13,20},{14,21},{15,22}} | collective-permute-start | bytes 589832 | tf_op jit(solution)/shard_map/ppermute | solution.py:210
  23.5 2.0 %collective-permute-start.8 = (bf16[384,256]{1,0:T(8,128)(2,1)S(1)}, bf16[384,256]{1,0:T(8,128)(2,1)S(1)}, u32[]{:S(2)}, u32[]{:S(2)}) collective-permute-start(bf16[384,256]{1,0:T(8,128)(2,1)S(1)} %get-tuple-element.119), channel_id=1, source_target_pairs={{8,17},{9,18},{10,19},{11,20},{12,21},{13,22},{14,23}} | collective-permute-start | bytes 589832 | tf_op jit(solution)/shard_map/ppermute | solution.py:210
  25.6 23.3 %collective-permute-start.10 = (bf16[384,512]{1,0:T(8,128)(2,1)S(1)}, bf16[384,512]{1,0:T(8,128)(2,1)S(1)}, u32[]{:S(2)}, u32[]{:S(2)}) collective-permute-start(bf16[384,512]{1,0:T(8,128)(2,1)S(1)} %get-tuple-element.120), channel_id=1, source_target_pairs={{0,8},{1,9},{2,10},{3,11},{4,12},{5,13},{6,14},{7,15},{8,0},{9,1},... | collective-permute-start | bytes 1179656 | tf_op jit(solution)/shard_map/ppermute | solution.py:210
  49.7 2.7 %collective-permute-start.13 = (bf16[384,256]{1,0:T(8,128)(2,1)S(1)}, bf16[384,256]{1,0:T(8,128)(2,1)S(1)}, u32[]{:S(2)}, u32[]{:S(2)}) collective-permute-start(bf16[384,256]{1,0:T(8,128)(2,1)S(1)} %get-tuple-element.133), channel_id=1, source_target_pairs={{9,16},{10,17},{11,18},{12,19},{13,20},{14,21},{15,22}} | collective-permute-start | bytes 589832 | tf_op jit(solution)/shard_map/ppermute | solution.py:210
  50.4 2.0 %collective-permute-start.12 = (bf16[384,256]{1,0:T(8,128)(2,1)S(1)}, bf16[384,256]{1,0:T(8,128)(2,1)S(1)}, u32[]{:S(2)}, u32[]{:S(2)}) collective-permute-start(bf16[384,256]{1,0:T(8,128)(2,1)S(1)} %get-tuple-element.133), channel_id=1, source_target_pairs={{8,17},{9,18},{10,19},{11,20},{12,21},{13,22},{14,23}} | collective-permute-start | bytes 589832 | tf_op jit(solution)/shard_map/ppermute | solution.py:210
  51.0 1.4 %collective-permute-start.11 = (bf16[384,256]{1,0:T(8,128)(2,1)S(1)}, bf16[384,256]{1,0:T(8,128)(2,1)S(1)}, u32[]{:S(2)}, u32[]{:S(2)}) collective-permute-start(bf16[384,256]{1,0:T(8,128)(2,1)S(1)} %get-tuple-element.133), channel_id=1, source_target_pairs={{8,16},{9,17},{10,18},{11,19},{12,20},{13,21},{14,22},{15,23}} | collective-permute-start | bytes 589832 | tf_op jit(solution)/shard_map/ppermute | solution.py:210
  52.4 20.4 %collective-permute-start.14 = (bf16[384,512]{1,0:T(8,128)(2,1)S(1)}, bf16[384,512]{1,0:T(8,128)(2,1)S(1)}, u32[]{:S(2)}, u32[]{:S(2)}) collective-permute-start(bf16[384,512]{1,0:T(8,128)(2,1)S(1)} %get-tuple-element.134), channel_id=1, source_target_pairs={{0,8},{1,9},{2,10},{3,11},{4,12},{5,13},{6,14},{7,15},{8,0},{9,1},... | collective-permute-start | bytes 1179656 | tf_op jit(solution)/shard_map/ppermute | solution.py:210
  77.8 2.7 %collective-permute-start.17 = (bf16[384,256]{1,0:T(8,128)(2,1)S(1)}, bf16[384,256]{1,0:T(8,128)(2,1)S(1)}, u32[]{:S(2)}, u32[]{:S(2)}) collective-permute-start(bf16[384,256]{1,0:T(8,128)(2,1)S(1)} %get-tuple-element.177), channel_id=1, source_target_pairs={{9,16},{10,17},{11,18},{12,19},{13,20},{14,21},{15,22}} | collective-permute-start | bytes 589832 | tf_op jit(solution)/shard_map/ppermute | solution.py:210
  78.5 2.0 %collective-permute-start.16 = (bf16[384,256]{1,0:T(8,128)(2,1)S(1)}, bf16[384,256]{1,0:T(8,128)(2,1)S(1)}, u32[]{:S(2)}, u32[]{:S(2)}) collective-permute-start(bf16[384,256]{1,0:T(8,128)(2,1)S(1)} %get-tuple-element.177), channel_id=1, source_target_pairs={{8,17},{9,18},{10,19},{11,20},{12,21},{13,22},{14,23}} | collective-permute-start | bytes 589832 | tf_op jit(solution)/shard_map/ppermute | solution.py:210
  79.2 1.4 %collective-permute-start.15 = (bf16[384,256]{1,0:T(8,128)(2,1)S(1)}, bf16[384,256]{1,0:T(8,128)(2,1)S(1)}, u32[]{:S(2)}, u32[]{:S(2)}) collective-permute-start(bf16[384,256]{1,0:T(8,128)(2,1)S(1)} %get-tuple-element.177), channel_id=1, source_target_pairs={{8,16},{9,17},{10,18},{11,19},{12,20},{13,21},{14,22},{15,23}} | collective-permute-start | bytes 589832 | tf_op jit(solution)/shard_map/ppermute | solution.py:210
  80.6 7.2 %collective-permute-start.18 = (bf16[384,512]{1,0:T(8,128)(2,1)S(1)}, bf16[384,512]{1,0:T(8,128)(2,1)S(1)}, u32[]{:S(2)}, u32[]{:S(2)}) collective-permute-start(bf16[384,512]{1,0:T(8,128)(2,1)S(1)} %get-tuple-element.148), channel_id=1, source_target_pairs={{0,8},{1,9},{2,10},{3,11},{4,12},{5,13},{6,14},{7,15},{8,0},{9,1},... | collective-permute-start | bytes 1179656 | tf_op jit(solution)/shard_map/ppermute | solution.py:210
  93.2 2.7 %collective-permute-start.21 = (bf16[384,256]{1,0:T(8,128)(2,1)S(1)}, bf16[384,256]{1,0:T(8,128)(2,1)S(1)}, u32[]{:S(2)}, u32[]{:S(2)}) collective-permute-start(bf16[384,256]{1,0:T(8,128)(2,1)S(1)} %get-tuple-element.178), channel_id=1, source_target_pairs={{9,16},{10,17},{11,18},{12,19},{13,20},{14,21},{15,22}} | collective-permute-start | bytes 589832 | tf_op jit(solution)/shard_map/ppermute | solution.py:210
  93.9 2.0 %collective-permute-start.20 = (bf16[384,256]{1,0:T(8,128)(2,1)S(1)}, bf16[384,256]{1,0:T(8,128)(2,1)S(1)}, u32[]{:S(2)}, u32[]{:S(2)}) collective-permute-start(bf16[384,256]{1,0:T(8,128)(2,1)S(1)} %get-tuple-element.178), channel_id=1, source_target_pairs={{8,17},{9,18},{10,19},{11,20},{12,21},{13,22},{14,23}} | collective-permute-start | bytes 589832 | tf_op jit(solution)/shard_map/ppermute | solution.py:210
  95.9 8.8 %collective-permute-start.22 = (bf16[384,512]{1,0:T(8,128)(2,1)S(1)}, bf16[384,512]{1,0:T(8,128)(2,1)S(1)}, u32[]{:S(2)}, u32[]{:S(2)}) collective-permute-start(bf16[384,512]{1,0:T(8,128)(2,1)S(1)} %get-tuple-element.162), channel_id=1, source_target_pairs={{0,8},{1,9},{2,10},{3,11},{4,12},{5,13},{6,14},{7,15},{8,0},{9,1},... | collective-permute-start | bytes 1179656 | tf_op jit(solution)/shard_map/ppermute | solution.py:210
  109.9 3.9 %collective-permute-start.23 = (bf16[384,256]{1,0:T(8,128)(2,1)S(1)}, bf16[384,256]{1,0:T(8,128)(2,1)S(1)}, u32[]{:S(2)}, u32[]{:S(2)}) collective-permute-start(bf16[384,256]{1,0:T(8,128)(2,1)S(1)} %get-tuple-element.177), channel_id=1, source_target_pairs={{24,0},{25,1},{26,2},{27,3},{28,4},{29,5},{30,6},{31,7}} | collective-permute-start | bytes 589832 | tf_op jit(solution)/shard_map/ppermute | solution.py:210
  111.2 4.7 %collective-permute-start.24 = (bf16[384,256]{1,0:T(8,128)(2,1)S(1)}, bf16[384,256]{1,0:T(8,128)(2,1)S(1)}, u32[]{:S(2)}, u32[]{:S(2)}) collective-permute-start(bf16[384,256]{1,0:T(8,128)(2,1)S(1)} %get-tuple-element.178), channel_id=1, source_target_pairs={{24,8},{25,9},{26,10},{27,11},{28,12},{29,13},{30,14},{31,15}} | collective-permute-start | bytes 589832 | tf_op jit(solution)/shard_map/ppermute | solution.py:210
  115.9 1.7 %collective-permute-start.25 = (bf16[384,512]{1,0:T(8,128)(2,1)S(1)}, bf16[384,512]{1,0:T(8,128)(2,1)S(1)}, u32[]{:S(2)}, u32[]{:S(2)}) collective-permute-start(bf16[384,512]{1,0:T(8,128)(2,1)S(1)} %get-tuple-element.179), channel_id=1, source_target_pairs={{0,8},{1,9},{2,10},{3,11},{4,12},{5,13},{6,14},{7,15},{8,0},{9,1},... | collective-permute-start | bytes 1179656 | tf_op jit(solution)/shard_map/ppermute | solution.py:210
  (4 other events, 62.8 us)

commit v7 on v6

--- a/solution.py
+++ b/solution.py
@@ -16,7 +16,9 @@
 SMEM = pl.BlockSpec(memory_space=pltpu.SMEM)
 
 
-def turn_kernel(cuts, w_ref, bias_ref, gain_ref, later_ref, first_ref, out_ref, bias_out, gain_out, _, *refs):
+def turn_kernel(cuts, w_ref, bias_ref, gain_ref, first_ref, *refs):
+    out_ref, bias_out, gain_out = refs[2:5]
+    refs = refs[7:]
     ws, rows, sems, cut_sems = refs[-4:]
     channels = w_ref.shape[-1]
     copies = [pltpu.make_async_copy(w_ref.at[k // 3, k % 3], ws.at[k], sems.at[k]) for k in range(9)]
@@ -37,7 +39,7 @@
     gain_out[...] = turned[:, 1:2]
 
 
-def turned_weights(weight, bias, gain, later, first, cuts):
+def turned_weights(weight, bias, gain, first, later, cuts):
     channels = weight.shape[-1]
     return pl.pallas_call(
         functools.partial(turn_kernel, cuts),
@@ -45,12 +47,12 @@
             jax.ShapeDtypeStruct((3, channels, 9 * channels), BF16),
             jax.ShapeDtypeStruct((channels, 1), F32),
             jax.ShapeDtypeStruct((channels, 1), F32),
-            jax.ShapeDtypeStruct(later.shape, later.dtype),
+            *(jax.ShapeDtypeStruct(v.shape, v.dtype) for v in later),
             *(jax.ShapeDtypeStruct((n, channels, width), BF16) for n, _, width in cuts),
         ),
-        in_specs=[pl.BlockSpec(memory_space=pltpu.HBM)] * 3 + [ANY] * 2,
-        out_specs=(VMEM, VMEM, VMEM, ANY) + (ANY,) * len(cuts),
-        input_output_aliases={3: 3},
+        in_specs=[pl.BlockSpec(memory_space=pltpu.HBM)] * 3 + [ANY] * 3,
+        out_specs=(VMEM, VMEM, VMEM, ANY, ANY) + (ANY,) * len(cuts),
+        input_output_aliases={4: 3, 5: 4},
         scratch_shapes=[
             pltpu.VMEM((9, 3, channels, channels), BF16),
             pltpu.VMEM((8, channels), F32),
@@ -59,7 +61,7 @@
         ],
         compiler_params=pltpu.CompilerParams(vmem_limit_bytes=VMEM_BYTES),
         cost_estimate=pl.CostEstimate(flops=0, bytes_accessed=4 * weight.size, transcendentals=0),
-    )(*(pltpu.with_memory_space_constraint(v, pltpu.HBM) for v in (weight, bias, gain)), later, first)
+    )(*(pltpu.with_memory_space_constraint(v, pltpu.HBM) for v in (weight, bias, gain)), first, *later)
 
 
 def layer_kernel(cases, rows_in, own, cols, block, height, n_in, back, place_ref, w_ref, bias_ref, gain_ref, *refs):
@@ -219,11 +221,12 @@
     first_above = moved(first[..., (own - 2) * row:], [(g, g) for g in evens], 1)
     place, weight = lax.optimization_barrier((place, conv_weight[0]))
     cuts = ((1, (own - 1) * row, row), (1, 0, row))
-    weight, bias, gain, later, odd_last, odd_first = turned_weights(
-        weight, conv_bias, norm_gain, lanes(video_in[block:]), first, cuts)
+    weight, bias, gain, second, later, odd_last, odd_first = turned_weights(
+        weight, conv_bias, norm_gain, first, (lanes(video_in[block:2 * block]), lanes(video_in[2 * block:])), cuts)
     odd_above = moved(odd_last, [(g, g) for g in odds], 1)
     odd_below = moved(odd_first, [(g, g) for g in odds], -1)
-    later_below = moved(later[..., :2 * row], [(0, 0)], -1)
+    second_below, later_below = (moved(v[..., :2 * row], [(0, 0)], -1) for v in (second, later))
+    second_above, later_above = (moved(v[..., (own - 2) * row:], [(0, 0)], 1) for v in (second, later))
     fixed = (weight, bias, gain)
 
     call = functools.partial(layer_call, own=own, cols=cols, block=block, height=height, place=place)
@@ -249,8 +252,9 @@
             else:
                 n = len(ins)
                 if p == 0:
-                    ins += [later, later_above, later_below]
-                    parts = [(n + 1, b - 1, 0, 2), (n, b - 1, 0, own), (n + 2, b - 1, 0, 2)]
+                    ins += [second, second_above, second_below] if b == 1 else [later, later_above, later_below]
+                    k = max(b - 2, 0)
+                    parts = [(n + 1, k, 0, 2), (n, k, 0, own), (n + 2, k, 0, 2)]
                 else:
                     ins += list(arrived[b])
                     parts = [(n + 1, None, 0, 2), (n, None, 0, own), (n + 2, None, 0, 2)]
@@ -263,21 +267,18 @@
             ins.append(done[-1])
         out, even_acts, *fixed = call(cases, own + 4, fixed=fixed, ins=ins, back=back)
         sent = list(arrived[tick - 1]) if 0 < tick <= blocks else []
+        sent += [(second_below, second_above), (later_below, later_above)][tick] if tick < 2 else []
+        final = done[-1:] if tick < ticks - 1 else []
+        out, *sent = lax.optimization_barrier((out, *sent, *final))
+        if final:
+            done[-1] = sent.pop()
         if tick == 0:
-            sent = [later_below]
-        elif tick == ticks - 1:
-            sent = done[:-1]
-        out, *sent = lax.optimization_barrier((out, *sent))
-        if tick == 0:
-            later_below, = sent
-        elif tick == ticks - 1:
-            done[:-1] = sent
+            second_below, second_above = sent
         elif tick <= blocks:
-            arrived[tick - 1] = sent
+            arrived[tick - 1] = sent[:3]
+        if tick == 1:
+            later_below, later_above = sent[3:]
         crossed = moved(out, across, 0)
-        if tick == 0:
-            crossed, above = lax.optimization_barrier((crossed, later[..., (own - 2) * row:]))
-            later_above = moved(above, [(0, 0)], 1)
         if tick == ticks - 1:
             done[-1] = crossed[:, :own * row]
 
@@ -291,10 +292,7 @@
             arrived.append((moved(out, hop, 0), moved(out[:, (own - 2) * row:], hop, 1), moved(out[:, :2 * row], hop, -1)))
         b = tick - LAG * (planes - 1)
         if 0 <= b < blocks:
-            done.append(out)
-            if b == segments - 2:
-                done = list(lax.optimization_barrier(tuple(done)))
-                done[:-1] = [moved(d, [(segments - 1, k)], 0) for k, d in enumerate(done[:-1])]
+            done.append(out if b >= segments - 2 else moved(out, [(segments - 1, b)], 0))
         for p in busy:
             if tick - LAG * p == blocks - 1:
                 even_cache[p] = even_acts[:, 2 * row:(2 + own) * row]

time: 125 us -> 120 us (0.960)
  waiting for transfers between devices: 13.9 us -> 8.13 us
    ppermute x26 -> x28, waiting for transfers between devices: 13.9 us -> 8.13 us  [moved(): lax.ppermute(value, axes, [(a * slabs + s, b * slabs + s + step) for a, b...]
    ppermute x26 -> x28, starting transfers between devices: 73.9 us -> 74.2 us  [moved(): lax.ppermute(value, axes, [(a * slabs + s, b * slabs + s + step) for a, b...]
  transfers between devices with their start and end apart: 26 -> 28, of which waited for: 10 -> 7; matrix products, arithmetic and copies ran while one was open for 1% -> 1% of each run, Pallas kernels for 7% -> 7%
where the time goes in v7:
time: 120 us
  starting transfers between devices  74.2 us (62%)
  Pallas kernels  30.4 us (25%)
  waiting for transfers between devices  8.13 us (7%)
  local copies, waits for them, and re-layouts  4.44 us (4%)
    ppermute x28, starting transfers between devices, moved(): lax.ppermute(value, axes, [(a * slabs + s, b * slabs + s + step) for a, b...  74.2 us
    pallas_call x12, Pallas kernels, layer_call(): pl.pallas_call(functools.partial(layer_kernel, cases, rows_in, own, cols,...  26.2 us
    ppermute x28, waiting for transfers between devices, moved(): lax.ppermute(value, axes, [(a * slabs + s, b * slabs + s + step) for a, b...  8.13 us
    pallas_call x1, Pallas kernels, turned_weights(): pl.pallas_call(functools.partial(turn_kernel, cuts), out_shape=(jax.Shape...  4.16 us
  transfers between devices with their start and end apart: 28, of which 7 were waited for; matrix products, arithmetic and copies ran while one was open for 1% of the time, Pallas kernels for 7%

profile of v7, /device:TPU:13, one launch (start us, length us, event | category | flops | bytes accessed | tf_op | source)
XLA Modules:
  0.0 119.5 jit_solution(799271411930193039)
XLA Ops:
  0.6 1.1 fusion
  1.7 1.0 pad_maximum_fusion
  4.3 1.0 slice.26
  5.8 4.2 %shard_map.68 = (bf16[3,384,3456]{2,1,0:T(8,128)(2,1)S(1)}, f32[384,1]{1,0:T(8,128)S(1)}, f32[384,1]{1,0:T(8,128)S(1)}, bf16[1,384,256]{2,1,0:T(8,128)(2,1)S(1)}...) custom-call(bf16[3,3,3,384,384]{4,3,2,1,0:T(8,128)(2,1)} %bitcast.25, ...), custom_call_target="tpu_custom_call", output_to_operand_aliasing={{3}: (4, {}), {4}: (5, {})} | custom-call | bytes 15925248 | tf_op jit(solution)/shard_map/pallas_call | solution.py:44
  10.0 3.1 %collective-permute-start.2 = (bf16[1,384,128]{2,1,0:T(8,128)(2,1)S(1)}, bf16[1,384,128]{2,1,0:T(8,128)(2,1)S(1)}, u32[]{:S(2)}, u32[]{:S(2)}) collective-permute-start(bf16[1,384,128]{2,1,0:T(8,128)(2,1)S(1)} %get-tuple-element.98), channel_id=1, source_target_pairs={{8,9},{9,10},{10,11},{11,12},{12,13},{13,14},{14,15},{24,25},{25,2... | collective-permute-start | bytes 294920 | tf_op jit(solution)/shard_map/ppermute | solution.py:212
  13.1 3.1 %collective-permute-start.3 = (bf16[1,384,128]{2,1,0:T(8,128)(2,1)S(1)}, bf16[1,384,128]{2,1,0:T(8,128)(2,1)S(1)}, u32[]{:S(2)}, u32[]{:S(2)}) collective-permute-start(bf16[1,384,128]{2,1,0:T(8,128)(2,1)S(1)} %get-tuple-element.99), channel_id=1, source_target_pairs={{9,8},{10,9},{11,10},{12,11},{13,12},{14,13},{15,14},{25,24},{26,2... | collective-permute-start | bytes 294920 | tf_op jit(solution)/shard_map/ppermute | solution.py:212
  16.9 0.8 collective-permute-done.2.refs_3_.refs_2_
  25.0 23.8 %collective-permute-start.12 = (bf16[384,512]{1,0:T(8,128)(2,1)S(1)}, bf16[384,512]{1,0:T(8,128)(2,1)S(1)}, u32[]{:S(2)}, u32[]{:S(2)}) collective-permute-start(bf16[384,512]{1,0:T(8,128)(2,1)S(1)} %get-tuple-element.118), channel_id=1, source_target_pairs={{0,8},{1,9},{2,10},{3,11},{4,12},{5,13},{6,14},{7,15},{8,0},{9,1},... | collective-permute-start | bytes 1179656 | tf_op jit(solution)/shard_map/ppermute | solution.py:212
  48.8 1.3 %collective-permute-done.12.refs_0_ = bf16[384,512]{1,0:T(8,128)(2,1)S(1)} collective-permute-done((bf16[384,512]{1,0:T(8,128)(2,1)S(1)}, bf16[384,512]{1,0:T(8,128)(2,1)S(1)}, u32[]{:S(2)}, u32[]{:S(2)}) %collective-permute-start.12) | collective-permute-done | bytes 393248 | tf_op jit(solution)/shard_map/ppermute | solution.py:212
  50.2 0.8 shard_map.72
  53.7 11.9 %collective-permute-start.16 = (bf16[384,512]{1,0:T(8,128)(2,1)S(1)}, bf16[384,512]{1,0:T(8,128)(2,1)S(1)}, u32[]{:S(2)}, u32[]{:S(2)}) collective-permute-start(bf16[384,512]{1,0:T(8,128)(2,1)S(1)} %get-tuple-element.134), channel_id=1, source_target_pairs={{0,8},{1,9},{2,10},{3,11},{4,12},{5,13},{6,14},{7,15},{8,0},{9,1},... | collective-permute-start | bytes 1179656 | tf_op jit(solution)/shard_map/ppermute | solution.py:212
  65.6 1.3 %collective-permute-done.16.refs_0_ = bf16[384,512]{1,0:T(8,128)(2,1)S(1)} collective-permute-done((bf16[384,512]{1,0:T(8,128)(2,1)S(1)}, bf16[384,512]{1,0:T(8,128)(2,1)S(1)}, u32[]{:S(2)}, u32[]{:S(2)}) %collective-permute-start.16) | collective-permute-done | bytes 393248 | tf_op jit(solution)/shard_map/ppermute | solution.py:212
  66.9 5.1 %shard_map.74 = (bf16[384,256]{1,0:T(8,128)(2,1)S(1)}, bf16[384,512]{1,0:T(8,128)(2,1)S(1)}, bf16[3,384,3456]{2,1,0:T(8,128)(2,1)S(1)}, f32[384,1]{1,0:T(8,128)S(1)}, f32[384,1]{1,0:T(8,128)S(1)}) custom-call(s32[2]{0:T(128)S(1)} %pad_add_fusion.place_ref, ...), custom_call_target="tpu_custom_call", output_to_operand_aliasing={{2}: (1, {}), {3}: (2, {}), {4}: (3, {})} | custom-call | flops 2038431744 | tf_op jit(solution)/shard_map/pallas_call | solution.py:174
  72.0 1.3 %collective-permute-start.20 = (bf16[384,256]{1,0:T(8,128)(2,1)S(1)}, bf16[384,256]{1,0:T(8,128)(2,1)S(1)}, u32[]{:S(2)}, u32[]{:S(2)}) collective-permute-start(bf16[384,256]{1,0:T(8,128)(2,1)S(1)} %get-tuple-element.147), channel_id=1, source_target_pairs={{24,0},{25,1},{26,2},{27,3},{28,4},{29,5},{30,6},{31,7}} | collective-permute-start | bytes 589832 | tf_op jit(solution)/shard_map/ppermute | solution.py:212
  76.1 7.1 %collective-permute-start.21 = (bf16[384,512]{1,0:T(8,128)(2,1)S(1)}, bf16[384,512]{1,0:T(8,128)(2,1)S(1)}, u32[]{:S(2)}, u32[]{:S(2)}) collective-permute-start(bf16[384,512]{1,0:T(8,128)(2,1)S(1)} %get-tuple-element.148), channel_id=1, source_target_pairs={{0,8},{1,9},{2,10},{3,11},{4,12},{5,13},{6,14},{7,15},{8,0},{9,1},... | collective-permute-start | bytes 1179656 | tf_op jit(solution)/shard_map/ppermute | solution.py:212
  83.1 1.3 %collective-permute-done.21.refs_0_ = bf16[384,512]{1,0:T(8,128)(2,1)S(1)} collective-permute-done((bf16[384,512]{1,0:T(8,128)(2,1)S(1)}, bf16[384,512]{1,0:T(8,128)(2,1)S(1)}, u32[]{:S(2)}, u32[]{:S(2)}) %collective-permute-start.21) | collective-permute-done | bytes 393248 | tf_op jit(solution)/shard_map/ppermute | solution.py:212
  84.5 5.5 %shard_map.76 = (bf16[384,256]{1,0:T(8,128)(2,1)S(1)}, bf16[384,512]{1,0:T(8,128)(2,1)S(1)}, bf16[3,384,3456]{2,1,0:T(8,128)(2,1)S(1)}, f32[384,1]{1,0:T(8,128)S(1)}, f32[384,1]{1,0:T(8,128)S(1)}) custom-call(s32[2]{0:T(128)S(1)} %pad_add_fusion.place_ref, ...), custom_call_target="tpu_custom_call", output_to_operand_aliasing={{2}: (1, {}), {3}: (2, {}), {4}: (3, {})} | custom-call | flops 2038431744 | tf_op jit(solution)/shard_map/pallas_call | solution.py:174
  89.9 1.3 %collective-permute-start.25 = (bf16[384,256]{1,0:T(8,128)(2,1)S(1)}, bf16[384,256]{1,0:T(8,128)(2,1)S(1)}, u32[]{:S(2)}, u32[]{:S(2)}) collective-permute-start(bf16[384,256]{1,0:T(8,128)(2,1)S(1)} %get-tuple-element.161), channel_id=1, source_target_pairs={{24,8},{25,9},{26,10},{27,11},{28,12},{29,13},{30,14},{31,15}} | collective-permute-start | bytes 589832 | tf_op jit(solution)/shard_map/ppermute | solution.py:212
  94.0 6.7 %collective-permute-start.26 = (bf16[384,512]{1,0:T(8,128)(2,1)S(1)}, bf16[384,512]{1,0:T(8,128)(2,1)S(1)}, u32[]{:S(2)}, u32[]{:S(2)}) collective-permute-start(bf16[384,512]{1,0:T(8,128)(2,1)S(1)} %get-tuple-element.162), channel_id=1, source_target_pairs={{0,8},{1,9},{2,10},{3,11},{4,12},{5,13},{6,14},{7,15},{8,0},{9,1},... | collective-permute-start | bytes 1179656 | tf_op jit(solution)/shard_map/ppermute | solution.py:212
  100.7 1.3 %collective-permute-done.26.refs_0_ = bf16[384,512]{1,0:T(8,128)(2,1)S(1)} collective-permute-done((bf16[384,512]{1,0:T(8,128)(2,1)S(1)}, bf16[384,512]{1,0:T(8,128)(2,1)S(1)}, u32[]{:S(2)}, u32[]{:S(2)}) %collective-permute-start.26) | collective-permute-done | bytes 393248 | tf_op jit(solution)/shard_map/ppermute | solution.py:212
  102.0 5.2 %shard_map.78 = (bf16[384,256]{1,0:T(8,128)(2,1)S(1)}, bf16[384,512]{1,0:T(8,128)(2,1)S(1)}, bf16[3,384,3456]{2,1,0:T(8,128)(2,1)S(1)}, f32[384,1]{1,0:T(8,128)S(1)}, f32[384,1]{1,0:T(8,128)S(1)}) custom-call(s32[2]{0:T(128)S(1)} %pad_add_fusion.place_ref, ...), custom_call_target="tpu_custom_call", output_to_operand_aliasing={{2}: (1, {}), {3}: (2, {}), {4}: (3, {})} | custom-call | flops 2038431744 | tf_op jit(solution)/shard_map/pallas_call | solution.py:174
  107.9 3.1 %collective-permute-start.27 = (bf16[384,512]{1,0:T(8,128)(2,1)S(1)}, bf16[384,512]{1,0:T(8,128)(2,1)S(1)}, u32[]{:S(2)}, u32[]{:S(2)}) collective-permute-start(bf16[384,512]{1,0:T(8,128)(2,1)S(1)} %get-tuple-element.175), channel_id=1, source_target_pairs={{0,8},{1,9},{2,10},{3,11},{4,12},{5,13},{6,14},{7,15},{8,0},{9,1},... | collective-permute-start | bytes 1179656 | tf_op jit(solution)/shard_map/ppermute | solution.py:212
  111.1 1.3 %collective-permute-done.27.refs_0_ = bf16[384,512]{1,0:T(8,128)(2,1)S(1)} collective-permute-done((bf16[384,512]{1,0:T(8,128)(2,1)S(1)}, bf16[384,512]{1,0:T(8,128)(2,1)S(1)}, u32[]{:S(2)}, u32[]{:S(2)}) %collective-permute-start.27) | collective-permute-done | bytes 393248 | tf_op jit(solution)/shard_map/ppermute | solution.py:212
  112.4 5.2 %shard_map.80 = (bf16[384,256]{1,0:T(8,128)(2,1)S(1)}, bf16[384,512]{1,0:T(8,128)(2,1)S(1)}, bf16[3,384,3456]{2,1,0:T(8,128)(2,1)S(1)}, f32[384,1]{1,0:T(8,128)S(1)}, f32[384,1]{1,0:T(8,128)S(1)}) custom-call(s32[2]{0:T(128)S(1)} %pad_add_fusion.place_ref, ...), custom_call_target="tpu_custom_call", output_to_operand_aliasing={{2}: (1, {}), {3}: (2, {}), {4}: (3, {})} | custom-call | flops 2038431744 | tf_op jit(solution)/shard_map/pallas_call | solution.py:174
  (60 shorter events, 20.4 us)
Async XLA Ops:
  2.9 16.0 %collective-permute-start.1 = (bf16[2,384,256]{2,1,0:T(8,128)(2,1)S(1)}, bf16[2,384,256]{2,1,0:T(8,128)(2,1)S(1)}, u32[]{:S(2)}, u32[]{:S(2)}) collective-permute-start(bf16[2,384,256]{2,1,0:T(8,128)(2,1)S(1)} %copy.77.first_ref.refs_0_.refs_1_), channel_id=1, source_target_pairs={{1,0},{2,1},{3,2},{4,3},{5,4},{6,5},{7,6},{17,16},{18,17},{19,18},... | collective-permute-start | bytes 1179656 | tf_op jit(solution)/shard_map/ppermute | solution.py:212
  3.6 15.3 %collective-permute-start = (bf16[2,384,256]{2,1,0:T(8,128)(2,1)S(1)}, bf16[2,384,256]{2,1,0:T(8,128)(2,1)S(1)}, u32[]{:S(2)}, u32[]{:S(2)}) collective-permute-start(bf16[2,384,256]{2,1,0:T(8,128)(2,1)S(1)} %copy.77.first_ref.refs_0_.refs_1_), channel_id=1, source_target_pairs={{0,1},{1,2},{2,3},{3,4},{4,5},{5,6},{6,7},{16,17},{17,18},{18,19},... | collective-permute-start | bytes 1179656 | tf_op jit(solution)/shard_map/ppermute | solution.py:212
  10.0 7.7 %collective-permute-start.2 = (bf16[1,384,128]{2,1,0:T(8,128)(2,1)S(1)}, bf16[1,384,128]{2,1,0:T(8,128)(2,1)S(1)}, u32[]{:S(2)}, u32[]{:S(2)}) collective-permute-start(bf16[1,384,128]{2,1,0:T(8,128)(2,1)S(1)} %get-tuple-element.98), channel_id=1, source_target_pairs={{8,9},{9,10},{10,11},{11,12},{12,13},{13,14},{14,15},{24,25},{25,2... | collective-permute-start | bytes 294920 | tf_op jit(solution)/shard_map/ppermute | solution.py:212
  13.1 5.8 %collective-permute-start.3 = (bf16[1,384,128]{2,1,0:T(8,128)(2,1)S(1)}, bf16[1,384,128]{2,1,0:T(8,128)(2,1)S(1)}, u32[]{:S(2)}, u32[]{:S(2)}) collective-permute-start(bf16[1,384,128]{2,1,0:T(8,128)(2,1)S(1)} %get-tuple-element.99), channel_id=1, source_target_pairs={{9,8},{10,9},{11,10},{12,11},{13,12},{14,13},{15,14},{25,24},{26,2... | collective-permute-start | bytes 294920 | tf_op jit(solution)/shard_map/ppermute | solution.py:212
  16.2 3.3 %collective-permute-start.5 = (bf16[1,384,256]{2,1,0:T(8,128)(2,1)S(1)}, bf16[1,384,256]{2,1,0:T(8,128)(2,1)S(1)}, u32[]{:S(2)}, u32[]{:S(2)}) collective-permute-start(bf16[1,384,256]{2,1,0:T(8,128)(2,1)S(1)} %get-tuple-element.104.refs_4_), channel_id=1, source_target_pairs={{0,1},{1,2},{2,3},{3,4},{4,5},{5,6},{6,7}} | collective-permute-start | bytes 589832 | tf_op jit(solution)/shard_map/ppermute | solution.py:212
  17.7 1.9 %collective-permute-start.4 = (bf16[1,384,256]{2,1,0:T(8,128)(2,1)S(1)}, bf16[1,384,256]{2,1,0:T(8,128)(2,1)S(1)}, u32[]{:S(2)}, u32[]{:S(2)}) collective-permute-start(bf16[1,384,256]{2,1,0:T(8,128)(2,1)S(1)} %get-tuple-element.104.refs_4_), channel_id=1, source_target_pairs={{1,0},{2,1},{3,2},{4,3},{5,4},{6,5},{7,6}} | collective-permute-start | bytes 589832 | tf_op jit(solution)/shard_map/ppermute | solution.py:212
  19.5 2.1 %collective-permute-start.6 = (bf16[384,512]{1,0:T(8,128)(2,1)S(1)}, bf16[384,512]{1,0:T(8,128)(2,1)S(1)}, u32[]{:S(2)}, u32[]{:S(2)}) collective-permute-start(bf16[384,512]{1,0:T(8,128)(2,1)S(1)} %get-tuple-element.105), channel_id=1, source_target_pairs={{0,8},{1,9},{2,10},{3,11},{4,12},{5,13},{6,14},{7,15},{8,0},{9,1},... | collective-permute-start | bytes 1179656 | tf_op jit(solution)/shard_map/ppermute | solution.py:212
  20.2 4.7 %collective-permute-start.11 = (bf16[2,384,256]{2,1,0:T(8,128)(2,1)S(1)}, bf16[2,384,256]{2,1,0:T(8,128)(2,1)S(1)}, u32[]{:S(2)}, u32[]{:S(2)}) collective-permute-start(bf16[2,384,256]{2,1,0:T(8,128)(2,1)S(1)} %get-tuple-element.117.refs_4_), channel_id=1, source_target_pairs={{0,1},{1,2},{2,3},{3,4},{4,5},{5,6},{6,7}} | collective-permute-start | bytes 1179656 | tf_op jit(solution)/shard_map/ppermute | solution.py:212
  20.9 4.0 %collective-permute-start.10 = (bf16[2,384,256]{2,1,0:T(8,128)(2,1)S(1)}, bf16[2,384,256]{2,1,0:T(8,128)(2,1)S(1)}, u32[]{:S(2)}, u32[]{:S(2)}) collective-permute-start(bf16[2,384,256]{2,1,0:T(8,128)(2,1)S(1)} %get-tuple-element.117.refs_4_), channel_id=1, source_target_pairs={{1,0},{2,1},{3,2},{4,3},{5,4},{6,5},{7,6}} | collective-permute-start | bytes 1179656 | tf_op jit(solution)/shard_map/ppermute | solution.py:212
  22.2 2.7 %collective-permute-start.9 = (bf16[384,256]{1,0:T(8,128)(2,1)S(1)}, bf16[384,256]{1,0:T(8,128)(2,1)S(1)}, u32[]{:S(2)}, u32[]{:S(2)}) collective-permute-start(bf16[384,256]{1,0:T(8,128)(2,1)S(1)} %get-tuple-element.116), channel_id=1, source_target_pairs={{9,16},{10,17},{11,18},{12,19},{13,20},{14,21},{15,22}} | collective-permute-start | bytes 589832 | tf_op jit(solution)/shard_map/ppermute | solution.py:212
  22.9 2.0 %collective-permute-start.8 = (bf16[384,256]{1,0:T(8,128)(2,1)S(1)}, bf16[384,256]{1,0:T(8,128)(2,1)S(1)}, u32[]{:S(2)}, u32[]{:S(2)}) collective-permute-start(bf16[384,256]{1,0:T(8,128)(2,1)S(1)} %get-tuple-element.116), channel_id=1, source_target_pairs={{8,17},{9,18},{10,19},{11,20},{12,21},{13,22},{14,23}} | collective-permute-start | bytes 589832 | tf_op jit(solution)/shard_map/ppermute | solution.py:212
  25.0 25.2 %collective-permute-start.12 = (bf16[384,512]{1,0:T(8,128)(2,1)S(1)}, bf16[384,512]{1,0:T(8,128)(2,1)S(1)}, u32[]{:S(2)}, u32[]{:S(2)}) collective-permute-start(bf16[384,512]{1,0:T(8,128)(2,1)S(1)} %get-tuple-element.118), channel_id=1, source_target_pairs={{0,8},{1,9},{2,10},{3,11},{4,12},{5,13},{6,14},{7,15},{8,0},{9,1},... | collective-permute-start | bytes 1179656 | tf_op jit(solution)/shard_map/ppermute | solution.py:212
  51.0 2.7 %collective-permute-start.15 = (bf16[384,256]{1,0:T(8,128)(2,1)S(1)}, bf16[384,256]{1,0:T(8,128)(2,1)S(1)}, u32[]{:S(2)}, u32[]{:S(2)}) collective-permute-start(bf16[384,256]{1,0:T(8,128)(2,1)S(1)} %get-tuple-element.133), channel_id=1, source_target_pairs={{9,16},{10,17},{11,18},{12,19},{13,20},{14,21},{15,22}} | collective-permute-start | bytes 589832 | tf_op jit(solution)/shard_map/ppermute | solution.py:212
  51.7 2.0 %collective-permute-start.14 = (bf16[384,256]{1,0:T(8,128)(2,1)S(1)}, bf16[384,256]{1,0:T(8,128)(2,1)S(1)}, u32[]{:S(2)}, u32[]{:S(2)}) collective-permute-start(bf16[384,256]{1,0:T(8,128)(2,1)S(1)} %get-tuple-element.133), channel_id=1, source_target_pairs={{8,17},{9,18},{10,19},{11,20},{12,21},{13,22},{14,23}} | collective-permute-start | bytes 589832 | tf_op jit(solution)/shard_map/ppermute | solution.py:212
  53.7 13.2 %collective-permute-start.16 = (bf16[384,512]{1,0:T(8,128)(2,1)S(1)}, bf16[384,512]{1,0:T(8,128)(2,1)S(1)}, u32[]{:S(2)}, u32[]{:S(2)}) collective-permute-start(bf16[384,512]{1,0:T(8,128)(2,1)S(1)} %get-tuple-element.134), channel_id=1, source_target_pairs={{0,8},{1,9},{2,10},{3,11},{4,12},{5,13},{6,14},{7,15},{8,0},{9,1},... | collective-permute-start | bytes 1179656 | tf_op jit(solution)/shard_map/ppermute | solution.py:212
  72.0 4.0 %collective-permute-start.20 = (bf16[384,256]{1,0:T(8,128)(2,1)S(1)}, bf16[384,256]{1,0:T(8,128)(2,1)S(1)}, u32[]{:S(2)}, u32[]{:S(2)}) collective-permute-start(bf16[384,256]{1,0:T(8,128)(2,1)S(1)} %get-tuple-element.147), channel_id=1, source_target_pairs={{24,0},{25,1},{26,2},{27,3},{28,4},{29,5},{30,6},{31,7}} | collective-permute-start | bytes 589832 | tf_op jit(solution)/shard_map/ppermute | solution.py:212
  73.3 2.7 %collective-permute-start.19 = (bf16[384,256]{1,0:T(8,128)(2,1)S(1)}, bf16[384,256]{1,0:T(8,128)(2,1)S(1)}, u32[]{:S(2)}, u32[]{:S(2)}) collective-permute-start(bf16[384,256]{1,0:T(8,128)(2,1)S(1)} %get-tuple-element.147), channel_id=1, source_target_pairs={{9,16},{10,17},{11,18},{12,19},{13,20},{14,21},{15,22}} | collective-permute-start | bytes 589832 | tf_op jit(solution)/shard_map/ppermute | solution.py:212
  74.0 2.0 %collective-permute-start.18 = (bf16[384,256]{1,0:T(8,128)(2,1)S(1)}, bf16[384,256]{1,0:T(8,128)(2,1)S(1)}, u32[]{:S(2)}, u32[]{:S(2)}) collective-permute-start(bf16[384,256]{1,0:T(8,128)(2,1)S(1)} %get-tuple-element.147), channel_id=1, source_target_pairs={{8,17},{9,18},{10,19},{11,20},{12,21},{13,22},{14,23}} | collective-permute-start | bytes 589832 | tf_op jit(solution)/shard_map/ppermute | solution.py:212
  76.1 8.4 %collective-permute-start.21 = (bf16[384,512]{1,0:T(8,128)(2,1)S(1)}, bf16[384,512]{1,0:T(8,128)(2,1)S(1)}, u32[]{:S(2)}, u32[]{:S(2)}) collective-permute-start(bf16[384,512]{1,0:T(8,128)(2,1)S(1)} %get-tuple-element.148), channel_id=1, source_target_pairs={{0,8},{1,9},{2,10},{3,11},{4,12},{5,13},{6,14},{7,15},{8,0},{9,1},... | collective-permute-start | bytes 1179656 | tf_op jit(solution)/shard_map/ppermute | solution.py:212
  89.9 4.0 %collective-permute-start.25 = (bf16[384,256]{1,0:T(8,128)(2,1)S(1)}, bf16[384,256]{1,0:T(8,128)(2,1)S(1)}, u32[]{:S(2)}, u32[]{:S(2)}) collective-permute-start(bf16[384,256]{1,0:T(8,128)(2,1)S(1)} %get-tuple-element.161), channel_id=1, source_target_pairs={{24,8},{25,9},{26,10},{27,11},{28,12},{29,13},{30,14},{31,15}} | collective-permute-start | bytes 589832 | tf_op jit(solution)/shard_map/ppermute | solution.py:212
  91.3 2.7 %collective-permute-start.24 = (bf16[384,256]{1,0:T(8,128)(2,1)S(1)}, bf16[384,256]{1,0:T(8,128)(2,1)S(1)}, u32[]{:S(2)}, u32[]{:S(2)}) collective-permute-start(bf16[384,256]{1,0:T(8,128)(2,1)S(1)} %get-tuple-element.161), channel_id=1, source_target_pairs={{9,16},{10,17},{11,18},{12,19},{13,20},{14,21},{15,22}} | collective-permute-start | bytes 589832 | tf_op jit(solution)/shard_map/ppermute | solution.py:212
  91.9 2.0 %collective-permute-start.23 = (bf16[384,256]{1,0:T(8,128)(2,1)S(1)}, bf16[384,256]{1,0:T(8,128)(2,1)S(1)}, u32[]{:S(2)}, u32[]{:S(2)}) collective-permute-start(bf16[384,256]{1,0:T(8,128)(2,1)S(1)} %get-tuple-element.161), channel_id=1, source_target_pairs={{8,17},{9,18},{10,19},{11,20},{12,21},{13,22},{14,23}} | collective-permute-start | bytes 589832 | tf_op jit(solution)/shard_map/ppermute | solution.py:212
  94.0 8.1 %collective-permute-start.26 = (bf16[384,512]{1,0:T(8,128)(2,1)S(1)}, bf16[384,512]{1,0:T(8,128)(2,1)S(1)}, u32[]{:S(2)}, u32[]{:S(2)}) collective-permute-start(bf16[384,512]{1,0:T(8,128)(2,1)S(1)} %get-tuple-element.162), channel_id=1, source_target_pairs={{0,8},{1,9},{2,10},{3,11},{4,12},{5,13},{6,14},{7,15},{8,0},{9,1},... | collective-permute-start | bytes 1179656 | tf_op jit(solution)/shard_map/ppermute | solution.py:212
  107.9 4.5 %collective-permute-start.27 = (bf16[384,512]{1,0:T(8,128)(2,1)S(1)}, bf16[384,512]{1,0:T(8,128)(2,1)S(1)}, u32[]{:S(2)}, u32[]{:S(2)}) collective-permute-start(bf16[384,512]{1,0:T(8,128)(2,1)S(1)} %get-tuple-element.175), channel_id=1, source_target_pairs={{0,8},{1,9},{2,10},{3,11},{4,12},{5,13},{6,14},{7,15},{8,0},{9,1},... | collective-permute-start | bytes 1179656 | tf_op jit(solution)/shard_map/ppermute | solution.py:212
  (4 other events, 5.4 us)

commit v8 on v6

--- a/solution.py
+++ b/solution.py
@@ -224,6 +224,7 @@
     odd_above = moved(odd_last, [(g, g) for g in odds], 1)
     odd_below = moved(odd_first, [(g, g) for g in odds], -1)
     later_below = moved(later[..., :2 * row], [(0, 0)], -1)
+    later_above = moved(later[..., (own - 2) * row:], [(0, 0)], 1)
     fixed = (weight, bias, gain)
 
     call = functools.partial(layer_call, own=own, cols=cols, block=block, height=height, place=place)
@@ -263,21 +264,14 @@
             ins.append(done[-1])
         out, even_acts, *fixed = call(cases, own + 4, fixed=fixed, ins=ins, back=back)
         sent = list(arrived[tick - 1]) if 0 < tick <= blocks else []
-        if tick == 0:
-            sent = [later_below]
-        elif tick == ticks - 1:
-            sent = done[:-1]
-        out, *sent = lax.optimization_barrier((out, *sent))
-        if tick == 0:
-            later_below, = sent
-        elif tick == ticks - 1:
-            done[:-1] = sent
-        elif tick <= blocks:
-            arrived[tick - 1] = sent
+        if tick == ticks - 2:
+            sent += [moved(d, [(segments - 1, k)], 0) for k, d in enumerate(done)]
+        if sent:
+            out, *sent = lax.optimization_barrier((out, *sent))
+            arrived[tick - 1] = sent[:3]
+        if tick == ticks - 2:
+            done = sent[3:]
         crossed = moved(out, across, 0)
-        if tick == 0:
-            crossed, above = lax.optimization_barrier((crossed, later[..., (own - 2) * row:]))
-            later_above = moved(above, [(0, 0)], 1)
         if tick == ticks - 1:
             done[-1] = crossed[:, :own * row]
 
@@ -285,6 +279,8 @@
         old = [(2, 0, 0, 1), (1, 0, 0, own), (3, 0, 0, 1)]
         if tick:
             ins.append(odd_acts)
+        if tick == 0:
+            ins += [later_above, later_below]
         cases = [(2 * p + 1, [(0, None, 0, own + 2)], old if tick == LAG * p else [(4, None, 0, own + 2)]) for p in busy]
         out, odd_acts, *fixed = call(cases, own + 2, fixed=fixed, ins=ins)
         if tick < blocks:
@@ -292,9 +288,6 @@
         b = tick - LAG * (planes - 1)
         if 0 <= b < blocks:
             done.append(out)
-            if b == segments - 2:
-                done = list(lax.optimization_barrier(tuple(done)))
-                done[:-1] = [moved(d, [(segments - 1, k)], 0) for k, d in enumerate(done[:-1])]
         for p in busy:
             if tick - LAG * p == blocks - 1:
                 even_cache[p] = even_acts[:, 2 * row:(2 + own) * row]

time: 125 us -> 117 us (0.936)
  waiting for transfers between devices: 13.9 us -> 8.11 us
  starting transfers between devices: 73.9 us -> 71.7 us
    ppermute x26, waiting for transfers between devices: 13.9 us -> 8.11 us  [moved(): lax.ppermute(value, axes, [(a * slabs + s, b * slabs + s + step) for a, b...]
    ppermute x26, starting transfers between devices: 73.9 us -> 71.7 us  [moved(): lax.ppermute(value, axes, [(a * slabs + s, b * slabs + s + step) for a, b...]
  transfers between devices with their start and end apart: 26 -> 26, of which waited for: 10 -> 8; matrix products, arithmetic and copies ran while one was open for 1% -> 1% of each run, Pallas kernels for 7% -> 11%
where the time goes in v8:
time: 117 us
  starting transfers between devices  71.7 us (61%)
  Pallas kernels  30.4 us (26%)
  waiting for transfers between devices  8.11 us (7%)
  local copies, waits for them, and re-layouts  4.33 us (4%)
    ppermute x26, starting transfers between devices, moved(): lax.ppermute(value, axes, [(a * slabs + s, b * slabs + s + step) for a, b...  71.7 us
    pallas_call x12, Pallas kernels, layer_call(): pl.pallas_call(functools.partial(layer_kernel, cases, rows_in, own, cols,...  26.2 us
    ppermute x26, waiting for transfers between devices, moved(): lax.ppermute(value, axes, [(a * slabs + s, b * slabs + s + step) for a, b...  8.11 us
    pallas_call x1, Pallas kernels, turned_weights(): pl.pallas_call(functools.partial(turn_kernel, cuts), out_shape=(jax.Shape...  4.16 us
  transfers between devices with their start and end apart: 26, of which 8 were waited for; matrix products, arithmetic and copies ran while one was open for 1% of the time, Pallas kernels for 11%

profile of v8, /device:TPU:13, one launch (start us, length us, event | category | flops | bytes accessed | tf_op | source)
XLA Modules:
  0.0 116.8 jit_solution(4032890193110517925)
XLA Ops:
  0.6 0.9 slice.22
  1.6 1.0 pad_maximum_fusion
  4.2 1.1 slice.21
  5.7 4.2 %shard_map.68 = (bf16[3,384,3456]{2,1,0:T(8,128)(2,1)S(1)}, f32[384,1]{1,0:T(8,128)S(1)}, f32[384,1]{1,0:T(8,128)S(1)}, bf16[3,384,256]{2,1,0:T(8,128)(2,1)S(1)}...) custom-call(bf16[3,3,3,384,384]{4,3,2,1,0:T(8,128)(2,1)} %bitcast.20, ...), custom_call_target="tpu_custom_call", output_to_operand_aliasing={{3}: (3, {})} | custom-call | bytes 15925248 | tf_op jit(solution)/shard_map/pallas_call | solution.py:42
  9.9 3.1 %collective-permute-start.2 = (bf16[1,384,128]{2,1,0:T(8,128)(2,1)S(1)}, bf16[1,384,128]{2,1,0:T(8,128)(2,1)S(1)}, u32[]{:S(2)}, u32[]{:S(2)}) collective-permute-start(bf16[1,384,128]{2,1,0:T(8,128)(2,1)S(1)} %get-tuple-element.92), channel_id=1, source_target_pairs={{8,9},{9,10},{10,11},{11,12},{12,13},{13,14},{14,15},{24,25},{25,2... | collective-permute-start | bytes 294920 | tf_op jit(solution)/shard_map/ppermute | solution.py:210
  13.0 3.1 %collective-permute-start.3 = (bf16[1,384,128]{2,1,0:T(8,128)(2,1)S(1)}, bf16[1,384,128]{2,1,0:T(8,128)(2,1)S(1)}, u32[]{:S(2)}, u32[]{:S(2)}) collective-permute-start(bf16[1,384,128]{2,1,0:T(8,128)(2,1)S(1)} %get-tuple-element.93), channel_id=1, source_target_pairs={{9,8},{10,9},{11,10},{12,11},{13,12},{14,13},{15,14},{25,24},{26,2... | collective-permute-start | bytes 294920 | tf_op jit(solution)/shard_map/ppermute | solution.py:210
  16.8 0.8 collective-permute-done.2.refs_3_.refs_2_
  20.1 1.3 %collective-permute-done.4.refs_0_ = bf16[384,512]{1,0:T(8,128)(2,1)S(1)} collective-permute-done((bf16[384,512]{1,0:T(8,128)(2,1)S(1)}, bf16[384,512]{1,0:T(8,128)(2,1)S(1)}, u32[]{:S(2)}, u32[]{:S(2)}) %collective-permute-start.4) | collective-permute-done | bytes 393248 | tf_op jit(solution)/shard_map/ppermute | solution.py:210
  24.8 24.1 %collective-permute-start.10 = (bf16[384,512]{1,0:T(8,128)(2,1)S(1)}, bf16[384,512]{1,0:T(8,128)(2,1)S(1)}, u32[]{:S(2)}, u32[]{:S(2)}) collective-permute-start(bf16[384,512]{1,0:T(8,128)(2,1)S(1)} %get-tuple-element.108), channel_id=1, source_target_pairs={{0,8},{1,9},{2,10},{3,11},{4,12},{5,13},{6,14},{7,15},{8,0},{9,1},... | collective-permute-start | bytes 1179656 | tf_op jit(solution)/shard_map/ppermute | solution.py:210
  48.9 1.3 %collective-permute-done.10.refs_0_ = bf16[384,512]{1,0:T(8,128)(2,1)S(1)} collective-permute-done((bf16[384,512]{1,0:T(8,128)(2,1)S(1)}, bf16[384,512]{1,0:T(8,128)(2,1)S(1)}, u32[]{:S(2)}, u32[]{:S(2)}) %collective-permute-start.10) | collective-permute-done | bytes 393248 | tf_op jit(solution)/shard_map/ppermute | solution.py:210
  50.2 0.8 shard_map.72
  53.7 10.4 %collective-permute-start.14 = (bf16[384,512]{1,0:T(8,128)(2,1)S(1)}, bf16[384,512]{1,0:T(8,128)(2,1)S(1)}, u32[]{:S(2)}, u32[]{:S(2)}) collective-permute-start(bf16[384,512]{1,0:T(8,128)(2,1)S(1)} %get-tuple-element.122), channel_id=1, source_target_pairs={{0,8},{1,9},{2,10},{3,11},{4,12},{5,13},{6,14},{7,15},{8,0},{9,1},... | collective-permute-start | bytes 1179656 | tf_op jit(solution)/shard_map/ppermute | solution.py:210
  64.2 1.3 %collective-permute-done.14.refs_0_ = bf16[384,512]{1,0:T(8,128)(2,1)S(1)} collective-permute-done((bf16[384,512]{1,0:T(8,128)(2,1)S(1)}, bf16[384,512]{1,0:T(8,128)(2,1)S(1)}, u32[]{:S(2)}, u32[]{:S(2)}) %collective-permute-start.14) | collective-permute-done | bytes 393248 | tf_op jit(solution)/shard_map/ppermute | solution.py:210
  65.5 5.1 %shard_map.74 = (bf16[384,256]{1,0:T(8,128)(2,1)S(1)}, bf16[384,512]{1,0:T(8,128)(2,1)S(1)}, bf16[3,384,3456]{2,1,0:T(8,128)(2,1)S(1)}, f32[384,1]{1,0:T(8,128)S(1)}, f32[384,1]{1,0:T(8,128)S(1)}) custom-call(s32[2]{0:T(128)S(1)} %pad_add_fusion.place_ref, ...), custom_call_target="tpu_custom_call", output_to_operand_aliasing={{2}: (1, {}), {3}: (2, {}), {4}: (3, {})} | custom-call | flops 2038431744 | tf_op jit(solution)/shard_map/pallas_call | solution.py:172
  73.3 7.5 %collective-permute-start.18 = (bf16[384,512]{1,0:T(8,128)(2,1)S(1)}, bf16[384,512]{1,0:T(8,128)(2,1)S(1)}, u32[]{:S(2)}, u32[]{:S(2)}) collective-permute-start(bf16[384,512]{1,0:T(8,128)(2,1)S(1)} %get-tuple-element.136), channel_id=1, source_target_pairs={{0,8},{1,9},{2,10},{3,11},{4,12},{5,13},{6,14},{7,15},{8,0},{9,1},... | collective-permute-start | bytes 1179656 | tf_op jit(solution)/shard_map/ppermute | solution.py:210
  80.8 1.3 %collective-permute-start.22 = (bf16[384,256]{1,0:T(8,128)(2,1)S(1)}, bf16[384,256]{1,0:T(8,128)(2,1)S(1)}, u32[]{:S(2)}, u32[]{:S(2)}) collective-permute-start(bf16[384,256]{1,0:T(8,128)(2,1)S(1)} %get-tuple-element.135), channel_id=1, source_target_pairs={{24,0},{25,1},{26,2},{27,3},{28,4},{29,5},{30,6},{31,7}} | collective-permute-start | bytes 589832 | tf_op jit(solution)/shard_map/ppermute | solution.py:210
  82.2 5.5 %shard_map.76 = (bf16[384,256]{1,0:T(8,128)(2,1)S(1)}, bf16[384,512]{1,0:T(8,128)(2,1)S(1)}, bf16[3,384,3456]{2,1,0:T(8,128)(2,1)S(1)}, f32[384,1]{1,0:T(8,128)S(1)}, f32[384,1]{1,0:T(8,128)S(1)}) custom-call(s32[2]{0:T(128)S(1)} %pad_add_fusion.place_ref, ...), custom_call_target="tpu_custom_call", output_to_operand_aliasing={{2}: (1, {}), {3}: (2, {}), {4}: (3, {})} | custom-call | flops 2038431744 | tf_op jit(solution)/shard_map/pallas_call | solution.py:172
  87.6 1.3 %collective-permute-start.23 = (bf16[384,256]{1,0:T(8,128)(2,1)S(1)}, bf16[384,256]{1,0:T(8,128)(2,1)S(1)}, u32[]{:S(2)}, u32[]{:S(2)}) collective-permute-start(bf16[384,256]{1,0:T(8,128)(2,1)S(1)} %get-tuple-element.149), channel_id=1, source_target_pairs={{24,8},{25,9},{26,10},{27,11},{28,12},{29,13},{30,14},{31,15}} | collective-permute-start | bytes 589832 | tf_op jit(solution)/shard_map/ppermute | solution.py:210
  91.7 6.3 %collective-permute-start.24 = (bf16[384,512]{1,0:T(8,128)(2,1)S(1)}, bf16[384,512]{1,0:T(8,128)(2,1)S(1)}, u32[]{:S(2)}, u32[]{:S(2)}) collective-permute-start(bf16[384,512]{1,0:T(8,128)(2,1)S(1)} %get-tuple-element.150), channel_id=1, source_target_pairs={{0,8},{1,9},{2,10},{3,11},{4,12},{5,13},{6,14},{7,15},{8,0},{9,1},... | collective-permute-start | bytes 1179656 | tf_op jit(solution)/shard_map/ppermute | solution.py:210
  98.0 1.3 %collective-permute-done.24.refs_0_ = bf16[384,512]{1,0:T(8,128)(2,1)S(1)} collective-permute-done((bf16[384,512]{1,0:T(8,128)(2,1)S(1)}, bf16[384,512]{1,0:T(8,128)(2,1)S(1)}, u32[]{:S(2)}, u32[]{:S(2)}) %collective-permute-start.24) | collective-permute-done | bytes 393248 | tf_op jit(solution)/shard_map/ppermute | solution.py:210
  99.3 5.2 %shard_map.78 = (bf16[384,256]{1,0:T(8,128)(2,1)S(1)}, bf16[384,512]{1,0:T(8,128)(2,1)S(1)}, bf16[3,384,3456]{2,1,0:T(8,128)(2,1)S(1)}, f32[384,1]{1,0:T(8,128)S(1)}, f32[384,1]{1,0:T(8,128)S(1)}) custom-call(s32[2]{0:T(128)S(1)} %pad_add_fusion.place_ref, ...), custom_call_target="tpu_custom_call", output_to_operand_aliasing={{2}: (1, {}), {3}: (2, {}), {4}: (3, {})} | custom-call | flops 2038431744 | tf_op jit(solution)/shard_map/pallas_call | solution.py:172
  105.2 3.1 %collective-permute-start.25 = (bf16[384,512]{1,0:T(8,128)(2,1)S(1)}, bf16[384,512]{1,0:T(8,128)(2,1)S(1)}, u32[]{:S(2)}, u32[]{:S(2)}) collective-permute-start(bf16[384,512]{1,0:T(8,128)(2,1)S(1)} %get-tuple-element.163), channel_id=1, source_target_pairs={{0,8},{1,9},{2,10},{3,11},{4,12},{5,13},{6,14},{7,15},{8,0},{9,1},... | collective-permute-start | bytes 1179656 | tf_op jit(solution)/shard_map/ppermute | solution.py:210
  108.3 1.3 %collective-permute-done.25.refs_0_ = bf16[384,512]{1,0:T(8,128)(2,1)S(1)} collective-permute-done((bf16[384,512]{1,0:T(8,128)(2,1)S(1)}, bf16[384,512]{1,0:T(8,128)(2,1)S(1)}, u32[]{:S(2)}, u32[]{:S(2)}) %collective-permute-start.25) | collective-permute-done | bytes 393248 | tf_op jit(solution)/shard_map/ppermute | solution.py:210
  109.7 5.2 %shard_map.80 = (bf16[384,256]{1,0:T(8,128)(2,1)S(1)}, bf16[384,512]{1,0:T(8,128)(2,1)S(1)}, bf16[3,384,3456]{2,1,0:T(8,128)(2,1)S(1)}, f32[384,1]{1,0:T(8,128)S(1)}, f32[384,1]{1,0:T(8,128)S(1)}) custom-call(s32[2]{0:T(128)S(1)} %pad_add_fusion.place_ref, ...), custom_call_target="tpu_custom_call", output_to_operand_aliasing={{2}: (1, {}), {3}: (2, {}), {4}: (3, {})} | custom-call | flops 2038431744 | tf_op jit(solution)/shard_map/pallas_call | solution.py:172
  (54 shorter events, 19.0 us)
Async XLA Ops:
  2.8 16.0 %collective-permute-start.1 = (bf16[2,384,256]{2,1,0:T(8,128)(2,1)S(1)}, bf16[2,384,256]{2,1,0:T(8,128)(2,1)S(1)}, u32[]{:S(2)}, u32[]{:S(2)}) collective-permute-start(bf16[2,384,256]{2,1,0:T(8,128)(2,1)S(1)} %copy.71.first_ref.refs_0_.refs_1_), channel_id=1, source_target_pairs={{1,0},{2,1},{3,2},{4,3},{5,4},{6,5},{7,6},{17,16},{18,17},{19,18},... | collective-permute-start | bytes 1179656 | tf_op jit(solution)/shard_map/ppermute | solution.py:210
  3.5 15.3 %collective-permute-start = (bf16[2,384,256]{2,1,0:T(8,128)(2,1)S(1)}, bf16[2,384,256]{2,1,0:T(8,128)(2,1)S(1)}, u32[]{:S(2)}, u32[]{:S(2)}) collective-permute-start(bf16[2,384,256]{2,1,0:T(8,128)(2,1)S(1)} %copy.71.first_ref.refs_0_.refs_1_), channel_id=1, source_target_pairs={{0,1},{1,2},{2,3},{3,4},{4,5},{5,6},{6,7},{16,17},{17,18},{18,19},... | collective-permute-start | bytes 1179656 | tf_op jit(solution)/shard_map/ppermute | solution.py:210
  9.9 7.7 %collective-permute-start.2 = (bf16[1,384,128]{2,1,0:T(8,128)(2,1)S(1)}, bf16[1,384,128]{2,1,0:T(8,128)(2,1)S(1)}, u32[]{:S(2)}, u32[]{:S(2)}) collective-permute-start(bf16[1,384,128]{2,1,0:T(8,128)(2,1)S(1)} %get-tuple-element.92), channel_id=1, source_target_pairs={{8,9},{9,10},{10,11},{11,12},{12,13},{13,14},{14,15},{24,25},{25,2... | collective-permute-start | bytes 294920 | tf_op jit(solution)/shard_map/ppermute | solution.py:210
  13.0 5.7 %collective-permute-start.3 = (bf16[1,384,128]{2,1,0:T(8,128)(2,1)S(1)}, bf16[1,384,128]{2,1,0:T(8,128)(2,1)S(1)}, u32[]{:S(2)}, u32[]{:S(2)}) collective-permute-start(bf16[1,384,128]{2,1,0:T(8,128)(2,1)S(1)} %get-tuple-element.93), channel_id=1, source_target_pairs={{9,8},{10,9},{11,10},{12,11},{13,12},{14,13},{15,14},{25,24},{26,2... | collective-permute-start | bytes 294920 | tf_op jit(solution)/shard_map/ppermute | solution.py:210
  16.1 4.0 %collective-permute-start.6 = (bf16[3,384,256]{2,1,0:T(8,128)(2,1)S(1)}, bf16[3,384,256]{2,1,0:T(8,128)(2,1)S(1)}, u32[]{:S(2)}, u32[]{:S(2)}) collective-permute-start(bf16[3,384,256]{2,1,0:T(8,128)(2,1)S(1)} %get-tuple-element.98.refs_4_), channel_id=1, source_target_pairs={{1,0},{2,1},{3,2},{4,3},{5,4},{6,5},{7,6}} | collective-permute-start | bytes 1769480 | tf_op jit(solution)/shard_map/ppermute | solution.py:210
  17.6 2.5 %collective-permute-start.5 = (bf16[3,384,256]{2,1,0:T(8,128)(2,1)S(1)}, bf16[3,384,256]{2,1,0:T(8,128)(2,1)S(1)}, u32[]{:S(2)}, u32[]{:S(2)}) collective-permute-start(bf16[3,384,256]{2,1,0:T(8,128)(2,1)S(1)} %get-tuple-element.98.refs_4_), channel_id=1, source_target_pairs={{0,1},{1,2},{2,3},{3,4},{4,5},{5,6},{6,7}} | collective-permute-start | bytes 1769480 | tf_op jit(solution)/shard_map/ppermute | solution.py:210
  19.4 2.0 %collective-permute-start.4 = (bf16[384,512]{1,0:T(8,128)(2,1)S(1)}, bf16[384,512]{1,0:T(8,128)(2,1)S(1)}, u32[]{:S(2)}, u32[]{:S(2)}) collective-permute-start(bf16[384,512]{1,0:T(8,128)(2,1)S(1)} %get-tuple-element.97), channel_id=1, source_target_pairs={{0,8},{1,9},{2,10},{3,11},{4,12},{5,13},{6,14},{7,15},{8,0},{9,1},... | collective-permute-start | bytes 1179656 | tf_op jit(solution)/shard_map/ppermute | solution.py:210
  22.1 2.7 %collective-permute-start.9 = (bf16[384,256]{1,0:T(8,128)(2,1)S(1)}, bf16[384,256]{1,0:T(8,128)(2,1)S(1)}, u32[]{:S(2)}, u32[]{:S(2)}) collective-permute-start(bf16[384,256]{1,0:T(8,128)(2,1)S(1)} %get-tuple-element.107), channel_id=1, source_target_pairs={{9,16},{10,17},{11,18},{12,19},{13,20},{14,21},{15,22}} | collective-permute-start | bytes 589832 | tf_op jit(solution)/shard_map/ppermute | solution.py:210
  22.8 2.0 %collective-permute-start.8 = (bf16[384,256]{1,0:T(8,128)(2,1)S(1)}, bf16[384,256]{1,0:T(8,128)(2,1)S(1)}, u32[]{:S(2)}, u32[]{:S(2)}) collective-permute-start(bf16[384,256]{1,0:T(8,128)(2,1)S(1)} %get-tuple-element.107), channel_id=1, source_target_pairs={{8,17},{9,18},{10,19},{11,20},{12,21},{13,22},{14,23}} | collective-permute-start | bytes 589832 | tf_op jit(solution)/shard_map/ppermute | solution.py:210
  24.8 25.4 %collective-permute-start.10 = (bf16[384,512]{1,0:T(8,128)(2,1)S(1)}, bf16[384,512]{1,0:T(8,128)(2,1)S(1)}, u32[]{:S(2)}, u32[]{:S(2)}) collective-permute-start(bf16[384,512]{1,0:T(8,128)(2,1)S(1)} %get-tuple-element.108), channel_id=1, source_target_pairs={{0,8},{1,9},{2,10},{3,11},{4,12},{5,13},{6,14},{7,15},{8,0},{9,1},... | collective-permute-start | bytes 1179656 | tf_op jit(solution)/shard_map/ppermute | solution.py:210
  51.0 2.7 %collective-permute-start.13 = (bf16[384,256]{1,0:T(8,128)(2,1)S(1)}, bf16[384,256]{1,0:T(8,128)(2,1)S(1)}, u32[]{:S(2)}, u32[]{:S(2)}) collective-permute-start(bf16[384,256]{1,0:T(8,128)(2,1)S(1)} %get-tuple-element.121), channel_id=1, source_target_pairs={{9,16},{10,17},{11,18},{12,19},{13,20},{14,21},{15,22}} | collective-permute-start | bytes 589832 | tf_op jit(solution)/shard_map/ppermute | solution.py:210
  51.7 2.0 %collective-permute-start.12 = (bf16[384,256]{1,0:T(8,128)(2,1)S(1)}, bf16[384,256]{1,0:T(8,128)(2,1)S(1)}, u32[]{:S(2)}, u32[]{:S(2)}) collective-permute-start(bf16[384,256]{1,0:T(8,128)(2,1)S(1)} %get-tuple-element.121), channel_id=1, source_target_pairs={{8,17},{9,18},{10,19},{11,20},{12,21},{13,22},{14,23}} | collective-permute-start | bytes 589832 | tf_op jit(solution)/shard_map/ppermute | solution.py:210
  52.4 1.4 %collective-permute-start.11 = (bf16[384,256]{1,0:T(8,128)(2,1)S(1)}, bf16[384,256]{1,0:T(8,128)(2,1)S(1)}, u32[]{:S(2)}, u32[]{:S(2)}) collective-permute-start(bf16[384,256]{1,0:T(8,128)(2,1)S(1)} %get-tuple-element.121), channel_id=1, source_target_pairs={{8,16},{9,17},{10,18},{11,19},{12,20},{13,21},{14,22},{15,23}} | collective-permute-start | bytes 589832 | tf_op jit(solution)/shard_map/ppermute | solution.py:210
  53.7 11.8 %collective-permute-start.14 = (bf16[384,512]{1,0:T(8,128)(2,1)S(1)}, bf16[384,512]{1,0:T(8,128)(2,1)S(1)}, u32[]{:S(2)}, u32[]{:S(2)}) collective-permute-start(bf16[384,512]{1,0:T(8,128)(2,1)S(1)} %get-tuple-element.122), channel_id=1, source_target_pairs={{0,8},{1,9},{2,10},{3,11},{4,12},{5,13},{6,14},{7,15},{8,0},{9,1},... | collective-permute-start | bytes 1179656 | tf_op jit(solution)/shard_map/ppermute | solution.py:210
  70.6 2.7 %collective-permute-start.17 = (bf16[384,256]{1,0:T(8,128)(2,1)S(1)}, bf16[384,256]{1,0:T(8,128)(2,1)S(1)}, u32[]{:S(2)}, u32[]{:S(2)}) collective-permute-start(bf16[384,256]{1,0:T(8,128)(2,1)S(1)} %get-tuple-element.135), channel_id=1, source_target_pairs={{9,16},{10,17},{11,18},{12,19},{13,20},{14,21},{15,22}} | collective-permute-start | bytes 589832 | tf_op jit(solution)/shard_map/ppermute | solution.py:210
  71.3 2.0 %collective-permute-start.16 = (bf16[384,256]{1,0:T(8,128)(2,1)S(1)}, bf16[384,256]{1,0:T(8,128)(2,1)S(1)}, u32[]{:S(2)}, u32[]{:S(2)}) collective-permute-start(bf16[384,256]{1,0:T(8,128)(2,1)S(1)} %get-tuple-element.135), channel_id=1, source_target_pairs={{8,17},{9,18},{10,19},{11,20},{12,21},{13,22},{14,23}} | collective-permute-start | bytes 589832 | tf_op jit(solution)/shard_map/ppermute | solution.py:210
  73.3 8.8 %collective-permute-start.18 = (bf16[384,512]{1,0:T(8,128)(2,1)S(1)}, bf16[384,512]{1,0:T(8,128)(2,1)S(1)}, u32[]{:S(2)}, u32[]{:S(2)}) collective-permute-start(bf16[384,512]{1,0:T(8,128)(2,1)S(1)} %get-tuple-element.136), channel_id=1, source_target_pairs={{0,8},{1,9},{2,10},{3,11},{4,12},{5,13},{6,14},{7,15},{8,0},{9,1},... | collective-permute-start | bytes 1179656 | tf_op jit(solution)/shard_map/ppermute | solution.py:210
  80.8 10.8 %collective-permute-start.22 = (bf16[384,256]{1,0:T(8,128)(2,1)S(1)}, bf16[384,256]{1,0:T(8,128)(2,1)S(1)}, u32[]{:S(2)}, u32[]{:S(2)}) collective-permute-start(bf16[384,256]{1,0:T(8,128)(2,1)S(1)} %get-tuple-element.135), channel_id=1, source_target_pairs={{24,0},{25,1},{26,2},{27,3},{28,4},{29,5},{30,6},{31,7}} | collective-permute-start | bytes 589832 | tf_op jit(solution)/shard_map/ppermute | solution.py:210
  87.6 4.0 %collective-permute-start.23 = (bf16[384,256]{1,0:T(8,128)(2,1)S(1)}, bf16[384,256]{1,0:T(8,128)(2,1)S(1)}, u32[]{:S(2)}, u32[]{:S(2)}) collective-permute-start(bf16[384,256]{1,0:T(8,128)(2,1)S(1)} %get-tuple-element.149), channel_id=1, source_target_pairs={{24,8},{25,9},{26,10},{27,11},{28,12},{29,13},{30,14},{31,15}} | collective-permute-start | bytes 589832 | tf_op jit(solution)/shard_map/ppermute | solution.py:210
  88.9 2.7 %collective-permute-start.21 = (bf16[384,256]{1,0:T(8,128)(2,1)S(1)}, bf16[384,256]{1,0:T(8,128)(2,1)S(1)}, u32[]{:S(2)}, u32[]{:S(2)}) collective-permute-start(bf16[384,256]{1,0:T(8,128)(2,1)S(1)} %get-tuple-element.149), channel_id=1, source_target_pairs={{9,16},{10,17},{11,18},{12,19},{13,20},{14,21},{15,22}} | collective-permute-start | bytes 589832 | tf_op jit(solution)/shard_map/ppermute | solution.py:210
  89.6 2.0 %collective-permute-start.20 = (bf16[384,256]{1,0:T(8,128)(2,1)S(1)}, bf16[384,256]{1,0:T(8,128)(2,1)S(1)}, u32[]{:S(2)}, u32[]{:S(2)}) collective-permute-start(bf16[384,256]{1,0:T(8,128)(2,1)S(1)} %get-tuple-element.149), channel_id=1, source_target_pairs={{8,17},{9,18},{10,19},{11,20},{12,21},{13,22},{14,23}} | collective-permute-start | bytes 589832 | tf_op jit(solution)/shard_map/ppermute | solution.py:210
  90.3 1.4 %collective-permute-start.19 = (bf16[384,256]{1,0:T(8,128)(2,1)S(1)}, bf16[384,256]{1,0:T(8,128)(2,1)S(1)}, u32[]{:S(2)}, u32[]{:S(2)}) collective-permute-start(bf16[384,256]{1,0:T(8,128)(2,1)S(1)} %get-tuple-element.149), channel_id=1, source_target_pairs={{8,16},{9,17},{10,18},{11,19},{12,20},{13,21},{14,22},{15,23}} | collective-permute-start | bytes 589832 | tf_op jit(solution)/shard_map/ppermute | solution.py:210
  91.7 7.7 %collective-permute-start.24 = (bf16[384,512]{1,0:T(8,128)(2,1)S(1)}, bf16[384,512]{1,0:T(8,128)(2,1)S(1)}, u32[]{:S(2)}, u32[]{:S(2)}) collective-permute-start(bf16[384,512]{1,0:T(8,128)(2,1)S(1)} %get-tuple-element.150), channel_id=1, source_target_pairs={{0,8},{1,9},{2,10},{3,11},{4,12},{5,13},{6,14},{7,15},{8,0},{9,1},... | collective-permute-start | bytes 1179656 | tf_op jit(solution)/shard_map/ppermute | solution.py:210
  105.2 4.5 %collective-permute-start.25 = (bf16[384,512]{1,0:T(8,128)(2,1)S(1)}, bf16[384,512]{1,0:T(8,128)(2,1)S(1)}, u32[]{:S(2)}, u32[]{:S(2)}) collective-permute-start(bf16[384,512]{1,0:T(8,128)(2,1)S(1)} %get-tuple-element.163), channel_id=1, source_target_pairs={{0,8},{1,9},{2,10},{3,11},{4,12},{5,13},{6,14},{7,15},{8,0},{9,1},... | collective-permute-start | bytes 1179656 | tf_op jit(solution)/shard_map/ppermute | solution.py:210
  (2 other events, 2.7 us)
